TPU v7x, 32 devices: a whole 2x2x4 slice. The times are simulated.
32 devices in a mesh: dp: 2 (over core), row: 4 (over y, x), col: 4 (over z).
Axes of the slice: x: 2, y: 2, z: 4, core: 2. Of those that a mesh axis runs over, the one named last changes fastest.
Arguments:
- activations: bfloat16 [8192, 2048], P(('dp', 'col'), 'row'), may hold values from -6 to 6
- segments: int32 [8192], P(('dp', 'row')), may hold values from 0 to 127, as said below
- positions: int32 [8192], P(('dp', 'row')), may hold values from 0 to 2046, as said below
- first_gain: float32 [2048], P('row'), may hold values from 0.5 to 1.5
- query_weight: bfloat16 [2048, 2048], P('row', 'col'), may hold values from -0.125 to 0.125
- key_weight: bfloat16 [2048, 512], P('row', 'col'), may hold values from -0.125 to 0.125
- value_weight: bfloat16 [2048, 512], P('row', 'col'), may hold values from -0.125 to 0.125
- out_weight: bfloat16 [2048, 2048], P('col', 'row'), may hold values from -1 to 1
- second_gain: float32 [2048], P('row'), may hold values from 0.5 to 1.5
- gate_weight: bfloat16 [2048, 8192], P('row', 'col'), may hold values from -0.125 to 0.125
- up_weight: bfloat16 [2048, 8192], P('row', 'col'), may hold values from -0.125 to 0.125
- down_weight: bfloat16 [8192, 2048], P('col', 'row'), may hold values from -0.125 to 0.125
- cotangent: bfloat16 [8192, 2048], P(('dp', 'col'), 'row'), may hold values from -6 to 6
Outputs:
- block_out: bfloat16 [8192, 2048], P(('dp', 'col'), 'row')
- input_grad: float32 [8192, 2048], P(('dp', 'col'), 'row')
- first_gain_grad: float32 [2048], P('row')
- query_grad: float32 [2048, 2048], P('row', 'col')
- key_grad: float32 [2048, 512], P('row', 'col')
- value_grad: float32 [2048, 512], P('row', 'col')
- out_grad: float32 [2048, 2048], P('col', 'row')
- second_gain_grad: float32 [2048], P('row')
- gate_grad: float32 [2048, 8192], P('row', 'col')
- up_grad: float32 [2048, 8192], P('row', 'col')
- down_grad: float32 [8192, 2048], P('col', 'row')
Inputs may be any that keep to these rules, and one draw needn't show every extreme that they name: `segments`: segment numbers never fall along the tokens; a document never crosses the end of a sequence of 1024 tokens. Within a document, positions rise by one from token to token; a document at the start of a sequence may begin at a position above 0.
All inputs are finite; a program needn't handle non-finite values.
Results may differ from a plain program's by a relative error of at most 0.017.
Values may be sent and summed in bfloat16 or wider, within the bound.
A program may use at most 512 MiB of HBM per device.

v0:
```python
import jax
import jax.numpy as jnp
from jax import lax
from jax.sharding import PartitionSpec as P

D = 2048
HEAD = 64


EPSILON = 1e-05
THETA = 500000.0


def half_turn(values):
    middle_index = values.shape[-1] // 2
    return jnp.concatenate([-values[..., middle_index:], values[..., :middle_index]], axis=-1)


def rotary_tables(positions):
    exponent = jnp.arange(0, HEAD, 2).astype(jnp.float32) / HEAD
    inverse = jnp.power(jnp.float32(THETA), -exponent)
    phase = positions.astype(jnp.float32)[:, None] * inverse[None, :]
    phase = jnp.concatenate([phase, phase], axis=1)
    return (jnp.cos(phase), jnp.sin(phase))


def rotate(values, cosine, sine):
    return values * cosine[:, None, :] + half_turn(values) * sine[:, None, :]


def rotate_back(gradients, cosine, sine):
    return gradients * cosine[:, None, :] - half_turn(gradients * sine[:, None, :])


def scaled_norm(values, gain):
    square_sums = lax.psum(jnp.sum(values * values, axis=1), "row")
    inverse = lax.rsqrt(square_sums / D + EPSILON)
    return (values * inverse[:, None] * gain[None, :], inverse)


def norm_back(values, inverse, gain, gradients):
    weighted = gradients * gain[None, :]
    inner_sum = lax.psum(jnp.sum(values * weighted, axis=1), "row")
    value_grad = (
        inverse[:, None] * weighted
        - values * (inverse * inverse * inverse * inner_sum / D)[:, None]
    )
    gain_grad = jnp.sum(gradients * values * inverse[:, None], axis=0)
    return (value_grad, gain_grad)


def gather_cols(values):
    return lax.all_gather(values, "col", axis=0, tiled=True)


def gather_rows(values):
    return lax.all_gather(values, "row", axis=0, tiled=True)


def cotangent_cols(values):
    return lax.all_gather(values, "col", axis=0, tiled=True)


def sum_rows(left, right):
    own_rows = left.shape[0] // lax.axis_size("row")

    def partial_product(first_row, row_total):
        return jnp.dot(left, right, preferred_element_type=jnp.float32)

    return lax.psum_scatter(
        partial_product(jnp.int32(0), own_rows * lax.axis_size("row")),
        "row",
        scatter_dimension=0,
        tiled=True,
    )


def sum_cols(left, right):
    own_rows = left.shape[0] // lax.axis_size("col")

    def partial_product(first_row, row_total):
        return jnp.dot(left, right, preferred_element_type=jnp.float32)

    return lax.psum_scatter(
        partial_product(jnp.int32(0), own_rows * lax.axis_size("col")),
        "col",
        scatter_dimension=0,
        tiled=True,
    )


def back_rows(gradients, weight):
    own_rows = gradients.shape[0] // lax.axis_size("row")

    def partial_product(first_row, row_total):
        return lax.dot_general(
            gradients, weight, (((1,), (1,)), ((), ())), preferred_element_type=jnp.float32
        )

    return lax.psum_scatter(
        partial_product(jnp.int32(0), own_rows * lax.axis_size("row")),
        "row",
        scatter_dimension=0,
        tiled=True,
    )


def outer_sum(inputs, gradients):
    return lax.dot_general(
        inputs, gradients, (((0,), (0,)), ((), ())), preferred_element_type=jnp.float32
    )


def fold_rows(gradients, kept_inputs, weight):
    shard_piece = lax.all_gather(gradients, "row", axis=0, tiled=True)
    weight_part = outer_sum(kept_inputs, shard_piece)
    rows_back = lax.dot_general(
        shard_piece, weight, (((1,), (1,)), ((), ())), preferred_element_type=jnp.float32
    )
    input_part = rows_back
    input_part, weight_part = (input_part, weight_part)
    return (lax.psum_scatter(input_part, "col", scatter_dimension=0, tiled=True), weight_part)


def visible(segments):
    places = jnp.arange(segments.shape[0])
    return (segments[:, None] == segments[None, :]) & (places[:, None] >= places[None, :])


def attn_scores(query_rot, key_rot, allowed):
    scores = jnp.einsum(
        "qhgd,shd->hgqs", query_rot, key_rot, preferred_element_type=jnp.float32
    ) * HEAD ** (-0.5)
    return jnp.where(allowed[None, None], scores, -1e30)


def attend(query_rot, key_rot, value_low, allowed):
    scores = attn_scores(query_rot, key_rot, allowed)
    row_max = jnp.max(scores, axis=-1, keepdims=True)
    exponent = jnp.exp(scores - row_max)
    denominator = jnp.sum(exponent, axis=-1, keepdims=True)
    soft_weights = exponent / denominator
    logsum = row_max + jnp.log(denominator)
    output = jnp.einsum(
        "hgqs,shd->qhgd",
        soft_weights.astype(jnp.bfloat16),
        value_low,
        preferred_element_type=jnp.float32,
    )
    return (output, logsum)


def attend_back(query_rot, key_rot, value_low, allowed, logsum, out_grads):
    scores = attn_scores(query_rot, key_rot, allowed)
    soft_weights = jnp.where(allowed[None, None], jnp.exp(scores - logsum), 0.0)
    weight_grads = jnp.einsum(
        "qhgd,shd->hgqs", out_grads, value_low, preferred_element_type=jnp.float32
    )
    value_back = jnp.einsum(
        "hgqs,qhgd->shd",
        soft_weights.astype(jnp.bfloat16),
        out_grads,
        preferred_element_type=jnp.float32,
    )
    score_grads = soft_weights * (
        weight_grads - jnp.sum(soft_weights * weight_grads, axis=-1, keepdims=True)
    )
    score_low = score_grads.astype(jnp.bfloat16)
    query_back = jnp.einsum(
        "hgqs,shd->qhgd", score_low, key_rot, preferred_element_type=jnp.float32
    ) * HEAD ** (-0.5)
    key_back = jnp.einsum(
        "hgqs,qhgd->shd", score_low, query_rot, preferred_element_type=jnp.float32
    ) * HEAD ** (-0.5)
    return (query_back, key_back, value_back)


def local(
    activations,
    segments,
    positions,
    first_gain,
    query_weight,
    key_weight,
    value_weight,
    out_weight,
    second_gain,
    gate_weight,
    up_weight,
    down_weight,
    cotangent,
):
    block_in = activations.astype(jnp.float32)
    normed_first, inverse_first = scaled_norm(block_in, first_gain)
    first_low = normed_first.astype(jnp.bfloat16)
    first_all = gather_cols(first_low)
    query_cols = query_weight.shape[1]
    key_cols = key_weight.shape[1]
    joined_qkv = jnp.concatenate([query_weight, key_weight, value_weight], axis=1)
    projected = sum_rows(first_all, joined_qkv)
    length = projected.shape[0]
    head_count = query_cols // HEAD
    kv_count = key_cols // HEAD
    group_size = head_count // kv_count
    cosine, sine = rotary_tables(positions)
    query_rot = rotate(projected[:, :query_cols].reshape(length, head_count, HEAD), cosine, sine)
    query_rot = query_rot.astype(jnp.bfloat16).reshape(length, kv_count, group_size, HEAD)
    key_rot = rotate(
        projected[:, query_cols : query_cols + key_cols].reshape(length, kv_count, HEAD),
        cosine,
        sine,
    ).astype(jnp.bfloat16)
    value_low = (
        projected[:, query_cols + key_cols :].reshape(length, kv_count, HEAD).astype(jnp.bfloat16)
    )
    allowed = visible(segments)
    attended, logsum = attend(query_rot, key_rot, value_low, allowed)
    attn_low = attended.reshape(length, query_cols).astype(jnp.bfloat16)
    attn_all = gather_rows(attn_low)
    middle = block_in + sum_cols(attn_all, out_weight)
    normed_second, inverse_second = scaled_norm(middle, second_gain)
    second_low = normed_second.astype(jnp.bfloat16)
    hidden_cols = gate_weight.shape[1]
    second_all = gather_cols(second_low)
    joined_gate_up = jnp.concatenate([gate_weight, up_weight], axis=1)
    gate_up = sum_rows(second_all, joined_gate_up)
    gate_part = gate_up[:, :hidden_cols]
    up_part = gate_up[:, hidden_cols:]
    sigma = jax.nn.sigmoid(gate_part)
    swish = gate_part * sigma
    hidden_low = (swish * up_part).astype(jnp.bfloat16)
    hidden_all = gather_rows(hidden_low)
    block_out = (middle + sum_cols(hidden_all, down_weight)).astype(jnp.bfloat16)
    swish_grad = sigma * (1.0 + gate_part * (1.0 - sigma))
    out_all = cotangent_cols(cotangent)
    down_grad = outer_sum(hidden_all, out_all)
    hidden_grad = back_rows(out_all, down_weight)
    gate_up_grad = jnp.concatenate(
        [hidden_grad * up_part * swish_grad, hidden_grad * swish], axis=1
    ).astype(jnp.bfloat16)
    second_grad, joined_gate_up_grad = fold_rows(gate_up_grad, second_all, joined_gate_up)
    middle_back, second_gain_grad = norm_back(middle, inverse_second, second_gain, second_grad)
    middle_grad = cotangent.astype(jnp.float32) + middle_back
    middle_all = cotangent_cols(middle_grad.astype(jnp.bfloat16))
    out_grad = outer_sum(attn_all, middle_all)
    attn_grad = (
        back_rows(middle_all, out_weight)
        .astype(jnp.bfloat16)
        .reshape(length, kv_count, group_size, HEAD)
    )
    query_back, key_back, value_back = attend_back(
        query_rot, key_rot, value_low, allowed, logsum, attn_grad
    )
    query_pre = rotate_back(query_back.reshape(length, head_count, HEAD), cosine, sine).reshape(
        length, query_cols
    )
    key_pre = rotate_back(key_back, cosine, sine).reshape(length, key_cols)
    qkv_grad = jnp.concatenate(
        [query_pre, key_pre, value_back.reshape(length, key_cols)], axis=1
    ).astype(jnp.bfloat16)
    first_grad, joined_qkv_grad = fold_rows(qkv_grad, first_all, joined_qkv)
    input_back, first_gain_grad = norm_back(block_in, inverse_first, first_gain, first_grad)
    input_grad = middle_grad + input_back
    first_gain_grad, second_gain_grad = lax.psum((first_gain_grad, second_gain_grad), ("dp", "col"))
    joined_qkv_grad, out_grad, joined_gate_up_grad, down_grad = (
        lax.psum(joined_qkv_grad.astype(jnp.bfloat16), "dp").astype(jnp.float32),
        lax.psum(out_grad.astype(jnp.bfloat16), "dp").astype(jnp.float32),
        lax.psum(joined_gate_up_grad.astype(jnp.bfloat16), "dp").astype(jnp.float32),
        lax.psum(down_grad.astype(jnp.bfloat16), "dp").astype(jnp.float32),
    )
    query_grad = joined_qkv_grad[:, :query_cols]
    key_grad = joined_qkv_grad[:, query_cols : query_cols + key_cols]
    value_grad = joined_qkv_grad[:, query_cols + key_cols :]
    gate_grad = joined_gate_up_grad[:, :hidden_cols]
    up_grad = joined_gate_up_grad[:, hidden_cols:]
    return (
        block_out,
        input_grad,
        first_gain_grad,
        query_grad,
        key_grad,
        value_grad,
        out_grad,
        second_gain_grad,
        gate_grad,
        up_grad,
        down_grad,
    )


def solution(mesh):
    return jax.shard_map(
        local,
        mesh=mesh,
        in_specs=(
            P(("dp", "col"), "row"),
            P(("dp", "row")),
            P(("dp", "row")),
            P("row"),
            P("row", "col"),
            P("row", "col"),
            P("row", "col"),
            P("col", "row"),
            P("row"),
            P("row", "col"),
            P("row", "col"),
            P("col", "row"),
            P(("dp", "col"), "row"),
        ),
        out_specs=(
            P(("dp", "col"), "row"),
            P(("dp", "col"), "row"),
            P("row"),
            P("row", "col"),
            P("row", "col"),
            P("row", "col"),
            P("col", "row"),
            P("row"),
            P("row", "col"),
            P("row", "col"),
            P("col", "row"),
        ),
        check_vma=False,
    )
```

profile of v0, /device:TPU:0, one launch (start us, length us, event | category | flops | bytes accessed | tf_op | source)
XLA Modules:
  0.0 3342.2 jit_solution(17196774217983548158)
XLA Ops:
  8.9 11.4 psum.70
  24.0 79.2 %all-gather.9.cloned.1.call-done = bf16[4096,512]{1,0:T(8,128)(2,1)} async-done(((bf16[1024,512]{1,0:T(8,128)(2,1)}), bf16[4096,512]{1,0:T(8,128)(2,1)}) %all-gather.9.cloned.1.call-update) | async-done | bytes 4194320 | tf_op jit(solution)/shard_map/all_gather | solution.py:53
  103.1 10.2 fusion.45
  116.5 116.3 %reduce-scatter.8.cloned.1.call-done = f32[1024,768]{1,0:T(8,128)} async-done(((f32[4096,768]{1,0:T(8,128)}), f32[1024,768]{1,0:T(8,128)}) %reduce-scatter.8.cloned.1.call-update) | async-done | bytes 3145744 | tf_op jit(solution)/shard_map/reduce_scatter | solution.py:70
  255.5 13.6 fusion.44
  269.1 13.1 fusion.3
  282.3 14.7 fusion.23
  297.1 52.8 %all-gather.11.cloned.1.call-done = bf16[4096,512]{0,1:T(8,128)(2,1)} async-done(((bf16[1024,512]{0,1:T(8,128)(2,1)}), bf16[4096,512]{0,1:T(8,128)(2,1)}) %all-gather.11.cloned.1.call-update) | async-done | bytes 4194320 | tf_op jit(solution)/shard_map/all_gather | solution.py:57
  349.9 7.9 fusion.46
  358.8 143.6 %reduce-scatter.10.cloned.1.call-done = f32[1024,512]{1,0:T(8,128)} async-done(((f32[4096,512]{1,0:T(8,128)}), f32[1024,512]{1,0:T(8,128)}) %reduce-scatter.10.cloned.1.call-update) | async-done | bytes 2097168 | tf_op jit(solution)/shard_map/reduce_scatter | solution.py:84
  505.5 9.9 psum.71
  518.3 67.0 %all-gather.17.cloned.1.call-done = bf16[4096,512]{1,0:T(8,128)(2,1)} async-done(((bf16[1024,512]{1,0:T(8,128)(2,1)}), bf16[4096,512]{1,0:T(8,128)(2,1)}) %all-gather.17.cloned.1.call-update) | async-done | bytes 4194320 | tf_op jit(solution)/shard_map/all_gather | solution.py:61
  585.3 18.3 fusion.49
  608.4 58.2 %all-gather.13.cloned.1.call-done = bf16[4096,512]{1,0:T(8,128)(2,1)} async-done(((bf16[1024,512]{1,0:T(8,128)(2,1)}), bf16[4096,512]{1,0:T(8,128)(2,1)}) %all-gather.13.cloned.1.call-update) | async-done | bytes 4194320 | tf_op jit(solution)/shard_map/all_gather | solution.py:53
  666.6 32.5 fusion.47
  701.0 255.9 %reduce-scatter.14.cloned.1.call-done = f32[1024,2048]{1,0:T(8,128)} async-done(((f32[4096,2048]{1,0:T(8,128)}), f32[1024,2048]{1,0:T(8,128)}) %reduce-scatter.14.cloned.1.call-update) | async-done | bytes 8388624 | tf_op jit(solution)/shard_map/reduce_scatter | solution.py:100
  956.9 1120.9 %all-reduce.6.cloned.1.call-done = f32[4096,4096]{1,0:T(8,128)} async-done(((f32[4096,4096]{1,0:T(8,128)}), f32[4096,4096]{1,0:T(8,128)}) %all-reduce.6.cloned.1.call-update) | async-done | bytes 67108880
  2077.8 14.1 multiply_convert_fusion.1
  2091.9 7.8 pad_maximum_fusion
  2099.8 298.7 %all-gather.19.cloned.1.call-done = bf16[4096,4096]{1,0:T(8,128)(2,1)} async-done(((bf16[1024,4096]{1,0:T(8,128)(2,1)}), bf16[4096,4096]{1,0:T(8,128)(2,1)}) %all-gather.19.cloned.1.call-update) | async-done | bytes 33554448 | tf_op jit(solution)/shard_map/all_gather | solution.py:115
  2398.5 25.0 fusion.50
  2423.6 144.6 %reduce-scatter.16.cloned.1.call-done = f32[1024,512]{1,0:T(8,128)} async-done(((f32[4096,512]{1,0:T(8,128)}), f32[1024,512]{1,0:T(8,128)}) %reduce-scatter.16.cloned.1.call-update) | async-done | bytes 2097168 | tf_op jit(solution)/shard_map/reduce_scatter | solution.py:122
  2568.2 3.4 multiply_reduce_fusion
  2571.6 9.9 psum.72
  2582.0 3.7 fusion.41
  2585.8 79.7 %all-gather.21.cloned.1.call-done = bf16[4096,512]{1,0:T(8,128)(2,1)} async-done(((bf16[1024,512]{1,0:T(8,128)(2,1)}), bf16[4096,512]{1,0:T(8,128)(2,1)}) %all-gather.21.cloned.1.call-update) | async-done | bytes 4194320 | tf_op jit(solution)/shard_map/all_gather | solution.py:61
  2665.5 7.9 fusion.51
  2674.7 83.9 %reduce-scatter.18.cloned.1.call-done = f32[1024,512]{1,0:T(8,128)} async-done(((f32[4096,512]{1,0:T(8,128)}), f32[1024,512]{1,0:T(8,128)}) %reduce-scatter.18.cloned.1.call-update) | async-done | bytes 2097168 | tf_op jit(solution)/shard_map/reduce_scatter | solution.py:100
  2763.6 25.5 fusion
  2789.1 28.4 fusion.2
  2817.5 8.8 convolution_multiply_fusion
  2829.3 12.9 broadcast_multiply_fusion
  2844.5 14.6 fusion.27
  2861.7 56.3 %all-gather.15.cloned.1.call-done = bf16[4096,2048]{1,0:T(8,128)(2,1)} async-done(((bf16[1024,2048]{1,0:T(8,128)(2,1)}), bf16[4096,2048]{1,0:T(8,128)(2,1)}) %all-gather.15.cloned.1.call-update) | async-done | bytes 16777232 | tf_op jit(solution)/shard_map/all_gather | solution.py:57
  2918.0 14.8 convolution_convert_fusion.1
  2932.8 23.2 convolution_convert_fusion
  2959.2 31.5 all-gather.23.cloned.1.call-done
  2990.6 8.4 convolution_convert_fusion.2
  3000.2 8.9 fusion.52
  3009.1 16.0 fusion.48
  3025.2 8.9 all-reduce.8.cloned.1.call-done
  3034.1 4.3 convert_element_type.115
  3041.6 4.4 fusion.42
  3046.0 136.0 %reduce-scatter.20.cloned.1.call-done = f32[1024,512]{1,0:T(8,128)} async-done(((f32[4096,512]{1,0:T(8,128)}), f32[1024,512]{1,0:T(8,128)}) %reduce-scatter.20.cloned.1.call-update) | async-done | bytes 2097168 | tf_op jit(solution)/shard_map/reduce_scatter | solution.py:122
  3184.4 9.9 psum.73
  3194.3 17.5 all-reduce.1
  3211.8 118.1 %reduce-scatter.12.cloned.1.call-done = f32[1024,512]{1,0:T(8,128)} async-done(((f32[4096,512]{1,0:T(8,128)}), f32[1024,512]{1,0:T(8,128)}) %reduce-scatter.12.cloned.1.call-update) | async-done | bytes 2097168 | tf_op jit(solution)/shard_map/reduce_scatter | solution.py:84
  3329.9 5.5 fusion.16
  (170 shorter events, 69.0 us)
Async XLA Ops:
  7.2 578.1 %copy-start = (bf16[2048,512]{1,0:T(8,128)(2,1)S(1)}, bf16[2048,512]{1,0:T(8,128)(2,1)}, u32[]{:S(2)}) copy-start(bf16[2048,512]{1,0:T(8,128)(2,1)} %param.24) | copy-start | bytes 6291460
  7.2 15.7 copy-start.22
  7.2 15.8 copy-start.25
  7.2 95.9 %all-gather.9.cloned.1.call-start = ((), (), s32[]{:S(2)}) async-start(), calls=%async_computation.7 | async-start | bytes 5242880 | tf_op jit(solution)/shard_map/all_gather | solution.py:53
  22.8 209.9 %reduce-scatter.8.cloned.1.call-start = ((), (), s32[]{:S(2)}) async-start(), calls=%async_computation.8 | async-start | bytes 15728640 | tf_op jit(solution)/shard_map/reduce_scatter | solution.py:70
  23.9 89.3 %copy-start.23 = (bf16[512,768]{1,0:T(8,128)(2,1)}, bf16[512,768]{1,0:T(8,128)(2,1)S(1)}, u32[]{:S(2)}) copy-start(bf16[512,768]{1,0:T(8,128)(2,1)S(1)} %constant_dynamic-update-slice_fusion) | copy-start | bytes 2359300
  113.3 236.5 %all-gather.11.cloned.1.call-start = ((), (), s32[]{:S(2)}) async-start(), calls=%async_computation.9 | async-start | bytes 5242880 | tf_op jit(solution)/shard_map/all_gather | solution.py:57
  115.9 136.7 %copy-start.10 = (f32[1024,64]{0,1:T(8,128)}, f32[1024,64]{0,1:T(8,128)S(1)}, u32[]{:S(2)}) copy-start(f32[1024,64]{0,1:T(8,128)S(1)} %get-tuple-element.42) | copy-start | bytes 786436
  116.5 139.0 %copy-start.1 = (pred[1024,1024]{0,1:T(8,128)(4,1)}, pred[1024,1024]{0,1:T(8,128)(4,1)S(1)}, u32[]{:S(2)}) copy-start(pred[1024,1024]{0,1:T(8,128)(4,1)S(1)} %fusion.10) | copy-start | bytes 3145732
  252.5 16.5 copy-start.17
  255.5 13.6 copy-start.6
  269.1 13.1 copy-start.26
  269.1 13.1 copy-start.19
  282.2 14.8 copy-start.28
  282.3 67.6 %copy-start.16 = (bf16[512,512]{1,0:T(8,128)(2,1)S(1)}, bf16[512,512]{1,0:T(8,128)(2,1)}, u32[]{:S(2)}) copy-start(bf16[512,512]{1,0:T(8,128)(2,1)} %param.20) | copy-start | bytes 1572868
  297.0 205.4 %reduce-scatter.10.cloned.1.call-start = ((), (), s32[]{:S(2)}) async-start(), calls=%async_computation.10 | async-start | bytes 10485760 | tf_op jit(solution)/shard_map/reduce_scatter | solution.py:84
  357.7 144.7 %copy-start.3 = (bf16[1024,512]{1,0:T(8,128)(2,1)S(1)}, bf16[1024,512]{1,0:T(8,128)(2,1)}, u32[]{:S(2)}) copy-start(bf16[1024,512]{1,0:T(8,128)(2,1)} %param.13) | copy-start | bytes 3145732
  357.7 157.7 %copy-start.38 = (f32[512]{0:T(512)S(1)}, f32[512]{0:T(512)}, u32[]{:S(2)}) copy-start(f32[512]{0:T(512)} %param.21) | copy-start | bytes 6148
  357.7 227.6 %all-gather.17.cloned.1.call-start = ((), (), s32[]{:S(2)}) async-start(), calls=%async_computation.14 | async-start | bytes 5242880 | tf_op jit(solution)/shard_map/all_gather | solution.py:61
  358.3 308.3 %all-gather.13.cloned.1.call-start = ((), (), s32[]{:S(2)}) async-start(), calls=%async_computation.11 | async-start | bytes 5242880 | tf_op jit(solution)/shard_map/all_gather | solution.py:53
  515.4 2066.0 %copy-start.30 = (f32[1024]{0:T(1024)}, f32[1024]{0:T(1024)S(1)}, u32[]{:S(2)}) copy-start(f32[1024]{0:T(1024)S(1)} %add_rsqrt_fusion) | copy-start | bytes 12292
  518.3 438.7 %reduce-scatter.14.cloned.1.call-start = ((), (), s32[]{:S(2)}) async-start(), calls=%async_computation.15 | async-start | bytes 41943040 | tf_op jit(solution)/shard_map/reduce_scatter | solution.py:100
  603.6 1474.2 %all-reduce.6.cloned.1.call-start = ((), (), s32[]{:S(2)}) async-start(), calls=%async_computation.22 | async-start | bytes 134217728
  699.1 1699.4 %all-gather.19.cloned.1.call-start = ((), (), s32[]{:S(2)}) async-start(), calls=%async_computation.16 | async-start | bytes 41943040 | tf_op jit(solution)/shard_map/all_gather | solution.py:115
  2099.7 468.4 %reduce-scatter.16.cloned.1.call-start = ((), (), s32[]{:S(2)}) async-start(), calls=%async_computation.17 | async-start | bytes 10485760 | tf_op jit(solution)/shard_map/reduce_scatter | solution.py:122
  2423.6 158.5 %copy-start.7 = (bf16[1024,512]{1,0:T(8,128)(2,1)S(1)}, bf16[1024,512]{1,0:T(8,128)(2,1)}, u32[]{:S(2)}) copy-start(bf16[1024,512]{1,0:T(8,128)(2,1)} %param.25) | copy-start | bytes 3145732
  2423.6 242.0 %all-gather.21.cloned.1.call-start = ((), (), s32[]{:S(2)}) async-start(), calls=%async_computation.18 | async-start | bytes 5242880 | tf_op jit(solution)/shard_map/all_gather | solution.py:61
  2585.8 172.8 %reduce-scatter.18.cloned.1.call-start = ((), (), s32[]{:S(2)}) async-start(), calls=%async_computation.19 | async-start | bytes 10485760 | tf_op jit(solution)/shard_map/reduce_scatter | solution.py:100
  2673.5 244.5 %all-gather.15.cloned.1.call-start = ((), (), s32[]{:S(2)}) async-start(), calls=%async_computation.12 | async-start | bytes 20971520 | tf_op jit(solution)/shard_map/all_gather | solution.py:57
  2673.6 90.0 %copy-start.2 = (pred[1024,1024]{0,1:T(8,128)(4,1)S(1)}, pred[1024,1024]{0,1:T(8,128)(4,1)}, u32[]{:S(2)}) copy-start(pred[1024,1024]{0,1:T(8,128)(4,1)} %copy-done.1) | copy-start | bytes 3145732
  2673.6 90.0 %copy-start.20 = (bf16[1024,128]{0,1:T(8,128)(2,1)S(1)}, bf16[1024,128]{0,1:T(8,128)(2,1)}, u32[]{:S(2)}) copy-start(bf16[1024,128]{0,1:T(8,128)(2,1)} %copy.47) | copy-start | bytes 786436
  2674.3 316.4 %all-gather.23.cloned.1.call-start = ((), (), s32[]{:S(2)}) async-start(), calls=%async_computation.20 | async-start | bytes 7864320 | tf_op jit(solution)/shard_map/all_gather | solution.py:115
  2789.1 28.4 copy-start.18
  2817.5 8.8 copy-start.11
  2861.7 172.4 %all-reduce.8.cloned.1.call-start = ((), (), s32[]{:S(2)}) async-start(), calls=%async_computation.23 | async-start | bytes 15204352 | tf_op jit(solution)/shard_map/psum | solution.py:266
  2918.0 14.8 copy-start.44
  2932.8 23.2 copy-start.8
  2932.8 23.2 copy-start.9
  2999.1 182.9 %reduce-scatter.20.cloned.1.call-start = ((), (), s32[]{:S(2)}) async-start(), calls=%async_computation.21 | async-start | bytes 10485760 | tf_op jit(solution)/shard_map/reduce_scatter | solution.py:122
  3009.1 320.9 %reduce-scatter.12.cloned.1.call-start = ((), (), s32[]{:S(2)}) async-start(), calls=%async_computation.13 | async-start | bytes 10485760 | tf_op jit(solution)/shard_map/reduce_scatter | solution.py:84
  3041.5 140.5 %copy-start.4 = (bf16[1024,512]{1,0:T(8,128)(2,1)S(1)}, bf16[1024,512]{1,0:T(8,128)(2,1)}, u32[]{:S(2)}) copy-start(bf16[1024,512]{1,0:T(8,128)(2,1)} %param.13) | copy-start | bytes 3145732
  3041.5 140.5 %copy-start.33 = (f32[1024]{0:T(1024)S(1)}, f32[1024]{0:T(1024)}, u32[]{:S(2)}) copy-start(f32[1024]{0:T(1024)} %copy-done.32) | copy-start | bytes 12292
  3041.5 140.5 %copy-start.40 = (f32[512]{0:T(512)S(1)}, f32[512]{0:T(512)}, u32[]{:S(2)}) copy-start(f32[512]{0:T(512)} %param.16) | copy-start | bytes 6148
  3041.5 152.8 %copy-start.42 = (f32[512]{0:T(512)S(1)}, f32[512]{0:T(512)}, u32[]{:S(2)}) copy-start(f32[512]{0:T(512)} %get-tuple-element.11) | copy-start | bytes 6148
  3041.5 170.3 %copy-start.37 = (f32[1024]{0:T(1024)S(1)}, f32[1024]{0:T(1024)}, u32[]{:S(2)}) copy-start(f32[1024]{0:T(1024)} %copy-done.36) | copy-start | bytes 12292
  3041.5 288.4 %copy-start.31 = (f32[1024]{0:T(1024)S(1)}, f32[1024]{0:T(1024)}, u32[]{:S(2)}) copy-start(f32[1024]{0:T(1024)} %copy-done.30) | copy-start | bytes 12292
  3041.5 288.4 %copy-start.35 = (f32[1024]{0:T(1024)S(1)}, f32[1024]{0:T(1024)}, u32[]{:S(2)}) copy-start(f32[1024]{0:T(1024)} %copy-done.34) | copy-start | bytes 12292
  3041.5 288.4 %copy-start.39 = (f32[512]{0:T(512)S(1)}, f32[512]{0:T(512)}, u32[]{:S(2)}) copy-start(f32[512]{0:T(512)} %param.21) | copy-start | bytes 6148
  (15 other events, 37.1 us)
Sparse Core Ops, SparseCore 0:
  22.9 80.1 all-gather.8
  113.4 119.2 reduce-scatter.7
  297.1 52.6 all-gather.10
  357.9 144.4 reduce-scatter.9
  503.8 81.4 all-gather.16
  587.3 79.2 all-gather.12
  669.7 287.1 reduce-scatter.13
  960.8 1116.9 all-reduce.5
  2099.9 298.5 all-gather.18
  2423.7 144.4 reduce-scatter.15
  2585.9 79.6 all-gather.20
  2673.6 84.9 reduce-scatter.17
  2760.6 157.3 all-gather.14
  2920.4 70.1 all-gather.22
  2999.2 34.8 all-reduce.7
  3036.3 145.6 reduce-scatter.19
  3184.2 145.7 reduce-scatter.11
where the time goes:
time: 3350 us; the launch traced here: 3340 us
  waiting for transfers between devices  2850 us (85%)
  matrix products  266 us (8%)
  other arithmetic  116 us (3%)
  blocking collectives  58.5 us (2%)
    unnamed x18, waiting for transfers between devices  1120 us
    reduce_scatter x2, waiting for transfers between devices, back_rows(): lax.psum_scatter(partial_product(jnp.int32(0), own_rows * lax.axis_size('...  340 us
    all_gather x2, waiting for transfers between devices, fold_rows(): shard_piece = lax.all_gather(gradients, 'row', axis=0, tiled=True)  330 us
    reduce_scatter x2, waiting for transfers between devices, fold_rows(): lax.psum_scatter(input_part, 'col', scatter_dimension=0, tiled=True)  281 us
    reduce_scatter x2, waiting for transfers between devices, sum_cols(): lax.psum_scatter(partial_product(jnp.int32(0), own_rows * lax.axis_size('...  262 us
    all_gather x2, waiting for transfers between devices, cotangent_cols(): return lax.all_gather(values, 'col', axis=0, tiled=True)  147 us
    all_gather x2, waiting for transfers between devices, gather_cols(): return lax.all_gather(values, 'col', axis=0, tiled=True)  137 us
    reduce_scatter x1, waiting for transfers between devices, sum_rows(): lax.psum_scatter(partial_product(jnp.int32(0), own_rows * lax.axis_size('...  116 us
  transfers between devices with their start and end apart: 17, of which 17 were waited for; matrix products, arithmetic and copies ran while one was open for 7% of the time, Pallas kernels for 0%

commit v1 on v0

v1 whole, which is shorter than its diff:
```python
import jax
import jax.numpy as jnp
from jax import lax
from jax.sharding import PartitionSpec as P

HEAD = 64
EPSILON = 1e-05
THETA = 500000.0
F32 = jnp.float32
BF16 = jnp.bfloat16


def dot(left, right, dims):
    return lax.dot_general(left, right, (dims, ((), ())), preferred_element_type=F32)


def half_turn(values):
    middle_index = values.shape[-1] // 2
    return jnp.concatenate([-values[..., middle_index:], values[..., :middle_index]], axis=-1)


def rotary_tables(positions):
    exponent = jnp.arange(0, HEAD, 2).astype(F32) / HEAD
    inverse = jnp.power(F32(THETA), -exponent)
    phase = positions[:, None] * inverse[None, :]
    phase = jnp.concatenate([phase, phase], axis=1)
    return (jnp.cos(phase), jnp.sin(phase))


def rotate(values, cosine, sine):
    return values * cosine[:, None, :] + half_turn(values) * sine[:, None, :]


def rotate_back(gradients, cosine, sine):
    return gradients * cosine[:, None, :] - half_turn(gradients * sine[:, None, :])


def visible(segments):
    places = jnp.arange(segments.shape[0])
    return (segments[:, None] == segments[None, :]) & (places[:, None] >= places[None, :])


def attn_scores(query_rot, key_rot, allowed):
    scores = jnp.einsum("qhgd,shd->hgqs", query_rot, key_rot, preferred_element_type=F32) * HEAD ** (-0.5)
    return jnp.where(allowed[None, None], scores, -1e30)


def attend(query_rot, key_rot, value_low, allowed):
    scores = attn_scores(query_rot, key_rot, allowed)
    row_max = jnp.max(scores, axis=-1, keepdims=True)
    exponent = jnp.exp(scores - row_max)
    denominator = jnp.sum(exponent, axis=-1, keepdims=True)
    soft_weights = exponent / denominator
    logsum = row_max + jnp.log(denominator)
    output = jnp.einsum("hgqs,shd->qhgd", soft_weights.astype(BF16), value_low, preferred_element_type=F32)
    return (output, logsum)


def attend_back(query_rot, key_rot, value_low, allowed, logsum, out_grads):
    scores = attn_scores(query_rot, key_rot, allowed)
    soft_weights = jnp.where(allowed[None, None], jnp.exp(scores - logsum), 0.0)
    weight_grads = jnp.einsum("qhgd,shd->hgqs", out_grads, value_low, preferred_element_type=F32)
    value_back = jnp.einsum("hgqs,qhgd->shd", soft_weights.astype(BF16), out_grads, preferred_element_type=F32)
    score_grads = soft_weights * (weight_grads - jnp.sum(soft_weights * weight_grads, axis=-1, keepdims=True))
    score_low = score_grads.astype(BF16)
    query_back = jnp.einsum("hgqs,shd->qhgd", score_low, key_rot, preferred_element_type=F32) * HEAD ** (-0.5)
    key_back = jnp.einsum("hgqs,qhgd->shd", score_low, query_rot, preferred_element_type=F32) * HEAD ** (-0.5)
    return (query_back, key_back, value_back)


def gather(values, axis_name, axis=0):
    return lax.all_gather(values, axis_name, axis=axis, tiled=True)


def scatter(values, axis_name, axis=0):
    return lax.psum_scatter(values.astype(BF16), axis_name, scatter_dimension=axis, tiled=True)


def swap(values):
    rows, cols = lax.axis_size("row"), lax.axis_size("col")
    return lax.ppermute(values, ("row", "col"), [(r * cols + c, c * cols + r) for r in range(rows) for c in range(cols)])


def gather_shared(values):
    share = values.shape[0] // lax.axis_size("dp")
    part = lax.dynamic_slice_in_dim(values, lax.axis_index("dp") * share, share, 0)
    return lax.all_gather(part, ("row", "dp"), axis=0, tiled=True)


def scatter_shared(values):
    part = scatter(values, ("row", "dp"))
    return gather(part, "dp").astype(F32)


def local(
    activations, segments, positions, first_gain, query_weight, key_weight, value_weight, out_weight,
    second_gain, gate_weight, up_weight, down_weight, cotangent,
):
    rows = lax.axis_size("row")
    row, col = lax.axis_index("row"), lax.axis_index("col")
    length, width = activations.shape
    features = rows * width
    quarter = length // rows
    query_cols, key_cols = query_weight.shape[1], key_weight.shape[1]
    heads, kv_heads = query_cols // HEAD, key_cols // HEAD
    group_size = heads // kv_heads
    hidden_cols = gate_weight.shape[1]

    small = jnp.concatenate([segments.astype(F32), positions.astype(F32), first_gain, second_gain])
    small = gather(small[None], "row")
    own = lax.dynamic_slice_in_dim(small, col, 1, 0)[0]
    segment_own, position_own = own[:length], own[length : 2 * length]
    gain1 = small[:, 2 * length : 2 * length + width].reshape(features)
    gain2 = small[:, 2 * length + width :].reshape(features)

    x_all = gather(activations, "row", 1)
    qkv_weight = jnp.concatenate([query_weight, key_weight, value_weight], axis=1)
    qkv_all = gather(swap(qkv_weight), "col")
    out_all_w = gather(swap(out_weight), "col", 1)
    gate_all = gather_shared(gate_weight)
    up_all = gather_shared(up_weight)
    down_all = gather_shared(down_weight).reshape(rows, hidden_cols, width)

    cot_tok = lax.all_to_all(cotangent, "row", 0, 1, tiled=True)
    cot_all = gather(cot_tok, "col")

    x = x_all.astype(F32)
    inv1 = lax.rsqrt(jnp.mean(x * x, axis=1, keepdims=True) + EPSILON)
    first = (x * inv1 * gain1[None]).astype(BF16)
    projected = dot(first, qkv_all, ((1,), (0,)))
    cosine, sine = rotary_tables(position_own)
    query_rot = rotate(projected[:, :query_cols].reshape(length, heads, HEAD), cosine, sine)
    query_rot = query_rot.astype(BF16).reshape(length, kv_heads, group_size, HEAD)
    key_rot = rotate(projected[:, query_cols : query_cols + key_cols].reshape(length, kv_heads, HEAD), cosine, sine).astype(BF16)
    value_low = projected[:, query_cols + key_cols :].reshape(length, kv_heads, HEAD).astype(BF16)
    allowed = visible(segment_own)
    attended, logsum = attend(query_rot, key_rot, value_low, allowed)
    attn = attended.reshape(length, query_cols).astype(BF16)
    mixed = scatter(dot(attn, out_all_w, ((1,), (0,))), "row")
    x_tok = lax.dynamic_slice_in_dim(x_all, row * quarter, quarter, 0).astype(F32)
    middle = x_tok + mixed.astype(F32)
    inv2 = lax.rsqrt(jnp.mean(middle * middle, axis=1, keepdims=True) + EPSILON)
    second = (middle * inv2 * gain2[None]).astype(BF16)

    second_all = gather(second, "col")
    gate = dot(second_all, gate_all, ((1,), (0,)))
    up = dot(second_all, up_all, ((1,), (0,)))
    sigma = jax.nn.sigmoid(gate)
    swish = gate * sigma
    hidden = (swish * up).astype(BF16)
    tokens = hidden.shape[0]
    down_part = lax.dot_general(hidden, down_all, (((1,), (1,)), ((), ())), preferred_element_type=F32).reshape(tokens, features)
    out_tok = (middle + scatter(down_part, "col").astype(F32)).astype(BF16)
    block_out = lax.all_to_all(out_tok, "row", 1, 0, tiled=True)

    cot_split = cot_all.reshape(tokens, rows, width)
    dhidden = lax.dot_general(cot_split, down_all, (((1, 2), (0, 2)), ((), ())), preferred_element_type=F32)
    swish_grad = sigma * (1.0 + gate * (1.0 - sigma))
    dgate = (dhidden * up * swish_grad).astype(BF16)
    dup = (dhidden * swish).astype(BF16)
    dsecond = scatter(dot(dgate, gate_all, ((1,), (1,))) + dot(dup, up_all, ((1,), (1,))), "col").astype(F32)

    weighted = dsecond * gain2[None]
    inner = jnp.sum(middle * weighted, axis=1, keepdims=True) / features
    dmiddle = cot_tok.astype(F32) + inv2 * weighted - middle * (inv2 * inv2 * inv2 * inner)
    gain2_grad = jnp.sum(dsecond * middle * inv2, axis=0)
    dmid_all = gather(dmiddle.astype(BF16), "row")

    attn_grad = dot(dmid_all, out_all_w, ((1,), (1,))).astype(BF16).reshape(length, kv_heads, group_size, HEAD)
    query_back, key_back, value_back = attend_back(query_rot, key_rot, value_low, allowed, logsum, attn_grad)
    query_pre = rotate_back(query_back.reshape(length, heads, HEAD), cosine, sine).reshape(length, query_cols)
    key_pre = rotate_back(key_back, cosine, sine).reshape(length, key_cols)
    dqkv = jnp.concatenate([query_pre, key_pre, value_back.reshape(length, key_cols)], axis=1).astype(BF16)
    dfirst_part = dot(dqkv, qkv_all, ((1,), (1,)))
    inner1 = lax.psum(jnp.sum(x * gain1[None] * dfirst_part, axis=1), "row") / features
    dfirst = scatter(dfirst_part, "row", 1).astype(F32)
    own_x = activations.astype(F32)
    dmid_own = lax.dynamic_slice_in_dim(dmid_all, row * width, width, 1).astype(F32)
    input_grad = dmid_own + inv1 * first_gain[None] * dfirst - own_x * (inv1 * inv1 * inv1 * inner1[:, None])
    gain1_grad = lax.psum(jnp.sum(dfirst * own_x * inv1, axis=0), ("dp", "col"))
    gain2_grad = lax.psum(gain2_grad, ("dp", "row", "col"))
    gain2_grad = lax.dynamic_slice_in_dim(gain2_grad, row * width, width, 0)

    down_grad = lax.dot_general(hidden, cot_split, (((0,), (0,)), ((), ())), preferred_element_type=F32)
    down_grad = scatter_shared(down_grad.transpose(1, 0, 2).reshape(rows * hidden_cols, width))
    gate_grad = scatter_shared(dot(second_all, dgate, ((0,), (0,))))
    up_grad = scatter_shared(dot(second_all, dup, ((0,), (0,))))
    out_grad = swap(lax.psum(scatter(dot(attn, dmid_all, ((0,), (0,))), "col", 1), "dp")).astype(F32)
    qkv_grad = swap(lax.psum(scatter(dot(first, dqkv, ((0,), (0,))), "col"), "dp")).astype(F32)
    return (
        block_out,
        input_grad,
        gain1_grad,
        qkv_grad[:, :query_cols],
        qkv_grad[:, query_cols : query_cols + key_cols],
        qkv_grad[:, query_cols + key_cols :],
        out_grad,
        gain2_grad,
        gate_grad,
        up_grad,
        down_grad,
    )


def solution(mesh):
    tokens, block, swapped = P(("dp", "col"), "row"), P("row", "col"), P("col", "row")
    return jax.shard_map(
        local,
        mesh=mesh,
        in_specs=(
            tokens, P(("dp", "row")), P(("dp", "row")), P("row"), block, block, block, swapped,
            P("row"), block, block, swapped, tokens,
        ),
        out_specs=(tokens, tokens, P("row"), block, block, block, swapped, P("row"), block, block, swapped),
        check_vma=False,
    )
```

time: 3350 us -> 1450 us (0.43)
  waiting for transfers between devices: 2850 us -> 793 us
  blocking collectives: 58.5 us -> 235 us
    unnamed x18 -> x22, waiting for transfers between devices: 1120 us -> 1.03 us
    reduce_scatter x7 -> x9, waiting for transfers between devices: 998 us -> 446 us  [scatter(): lax.psum_scatter(values.astype(BF16), axis_name, scatter_dimension=axis,...]
    all_gather x8 -> x12, waiting for transfers between devices: 723 us -> 346 us  [the longest x9 250 us: gather(): return lax.all_gather(values, axis_name, axis=axis, tiled=True)]
    all_gather x0 -> x1, blocking collectives: none -> 91 us  [gather(): return lax.all_gather(values, axis_name, axis=axis, tiled=True)]
    psum x5 -> x3, blocking collectives: 58.5 us -> 127 us  [the longest x1 101 us: local(): gain2_grad = lax.psum(gain2_grad, ('dp', 'row', 'col'))]
    dot_general x16 -> x19, matrix products: 228 us -> 224 us  [the longest x12 124 us: dot(): lax.dot_general(left, right, (dims, ((), ())), preferred_element_type=F32)]
  transfers between devices with their start and end apart: 17 -> 27, of which waited for: 17 -> 14; matrix products, arithmetic and copies ran while one was open for 7% -> 21% of each run, Pallas kernels for 0% -> 0%
where the time goes in v1:
time: 1450 us; the launch traced here: 1440 us
  waiting for transfers between devices  793 us (55%)
  matrix products  259 us (18%)
  blocking collectives  235 us (16%)
  other arithmetic  86.1 us (6%)
  local copies, waits for them, and re-layouts  29.4 us (2%)
  starting transfers between devices  23.7 us (2%)
  between operations  16.6 us (1%)
    reduce_scatter x9, waiting for transfers between devices, scatter(): lax.psum_scatter(values.astype(BF16), axis_name, scatter_dimension=axis,...  446 us
    all_gather x9, waiting for transfers between devices, gather(): return lax.all_gather(values, axis_name, axis=axis, tiled=True)  250 us
    dot_general x12, matrix products, dot(): lax.dot_general(left, right, (dims, ((), ())), preferred_element_type=F32)  124 us
    psum x1, blocking collectives, local(): gain2_grad = lax.psum(gain2_grad, ('dp', 'row', 'col'))  101 us
    all_gather x3, waiting for transfers between devices, gather_shared(): return lax.all_gather(part, ('row', 'dp'), axis=0, tiled=True)  96.2 us
    all_gather x1, blocking collectives, gather(): return lax.all_gather(values, axis_name, axis=axis, tiled=True)  91 us
  transfers between devices with their start and end apart: 27, of which 14 were waited for; matrix products, arithmetic and copies ran while one was open for 21% of the time, Pallas kernels for 0%

profile of v1, /device:TPU:0, one launch (start us, length us, event | category | flops | bytes accessed | tf_op | source)
XLA Modules:
  0.0 1442.5 jit_solution(4554512305655128667)
XLA Ops:
  11.7 5.4 collective-permute-start.1
  19.2 91.0 %all-gather = f32[12288]{0:T(1024)S(1)} all-gather(f32[3072]{0:T(1024)S(1)} %pad_maximum_fusion.6), channel_id=2, replica_groups=mesh['dp'=2,'row'=4,'col'=4] {'row'}, dimensions={0}, use_global_device_ids=true | all-gather | bytes 61440 | tf_op jit(solution)/shard_map/all_gather | solution.py:72
  112.9 6.4 all-gather.14.cloned.1.call-done
  122.9 64.2 %all-gather.16.cloned.1.call-done = bf16[2048,768]{1,0:T(8,128)(2,1)} async-done(((bf16[512,768]{1,0:T(8,128)(2,1)}), bf16[2048,768]{1,0:T(8,128)(2,1)}) %all-gather.16.cloned.1.call-update) | async-done | bytes 3145744 | tf_op jit(solution)/shard_map/all_gather | solution.py:72
  187.2 7.2 fusion.46
  196.2 13.8 fusion.64
  210.0 13.2 fusion.3
  223.2 13.7 fusion.41
  236.9 6.3 convolution_convert_fusion.4
  244.7 74.9 %reduce-scatter.10.cloned.1.call-done = bf16[256,2048]{1,0:T(8,128)(2,1)} async-done(((bf16[1024,2048]{1,0:T(8,128)(2,1)}), bf16[256,2048]{1,0:T(8,128)(2,1)}) %reduce-scatter.10.cloned.1.call-update) | async-done | bytes 1048592 | tf_op jit(solution)/shard_map/reduce_scatter | solution.py:76
  327.1 16.8 %all_to_all.38 = bf16[4,256,512]{2,1,0:T(8,128)(2,1)S(1)} all-to-all(bf16[4,256,512]{2,1,0:T(8,128)(2,1)S(1)} %bitcast.164), channel_id=1, replica_groups=mesh['dp'=2,'row'=4,'col'=4] {'row'}, dimensions={0} | all-to-all | bytes 2097152 | tf_op jit(solution)/shard_map/all_to_all | solution.py:124
  347.5 57.8 %all-gather.20.cloned.1.call-done = bf16[1024,2048]{1,0:T(8,128)(2,1)} async-done(((bf16[256,2048]{1,0:T(8,128)(2,1)}), bf16[1024,2048]{1,0:T(8,128)(2,1)}) %all-gather.20.cloned.1.call-update) | async-done | bytes 4194320 | tf_op jit(solution)/shard_map/all_gather | solution.py:72
  405.3 14.6 %fusion.66 = f32[1024,2048]{1,0:T(8,128)} fusion(bf16[1024,2048]{1,0:T(8,128)(2,1)} %all-gather.20.cloned.1.call-done, bf16[2048,2048]{1,0:T(8,128)(2,1)} %all-gather.24.cloned.1.call-done), kind=kOutput, calls=%fused_computation.125 | convolution fusion | flops 8589934592 | bytes 20971520 | tf_op jit(solution)/shard_map/dot_general | solution.py:14
  419.9 40.7 %all-gather.22.cloned.1.call-done = bf16[2048,2048]{1,0:T(8,128)(2,1)} async-done(((bf16[256,2048]{1,0:T(8,128)(2,1)}), bf16[2048,2048]{1,0:T(8,128)(2,1)}) %all-gather.22.cloned.1.call-update) | async-done | bytes 8388624 | tf_op jit(solution)/shard_map/all_gather | solution.py:87
  460.6 14.5 %fusion.65 = f32[1024,2048]{1,0:T(8,128)} fusion(bf16[1024,2048]{1,0:T(8,128)(2,1)} %all-gather.20.cloned.1.call-done, bf16[2048,2048]{1,0:T(8,128)(2,1)} %all-gather.22.cloned.1.call-done), kind=kOutput, calls=%fused_computation.124 | convolution fusion | flops 8589934592 | bytes 20971520 | tf_op jit(solution)/shard_map/dot_general | solution.py:14
  475.1 67.8 %all-gather.28.cloned.1.call-done = bf16[1024,2048]{1,0:T(8,128)(2,1)} async-done(((bf16[256,2048]{1,0:T(8,128)(2,1)}), bf16[1024,2048]{1,0:T(8,128)(2,1)}) %all-gather.28.cloned.1.call-update) | async-done | bytes 4194320 | tf_op jit(solution)/shard_map/all_gather | solution.py:72
  542.9 55.4 %all-gather.26.cloned.1.call-done = bf16[8192,512]{1,0:T(8,128)(2,1)} async-done(((bf16[1024,512]{1,0:T(8,128)(2,1)}), bf16[8192,512]{1,0:T(8,128)(2,1)}) %all-gather.26.cloned.1.call-update) | async-done | bytes 8388624 | tf_op jit(solution)/shard_map/all_gather | solution.py:87
  598.3 22.0 %fusion.16 = (bf16[1024,2048]{1,0:T(8,128)(2,1)}, bf16[1024,2048]{1,0:T(8,128)(2,1)}, bf16[1024,2048]{1,0:T(8,128)(2,1)}) fusion(f32[1024,2048]{1,0:T(8,128)} %fusion.65, f32[1024,2048]{1,0:T(8,128)} %fusion.66, bf16[4,2048,512]{2,1,0:T(8,128)(2,1)} %bitcast.147, bf16[128,4,8,512]{3,2,1,0:T(8,128)(2,1)} %bitcast.177), kind=kOutput, calls=%fused_computation.26 | convolution fusion | flops 8621391872 | bytes 41943040 | tf_op jit(solution)/shard_map/dot_general | solution.py:157
  620.4 13.2 fusion.67
  633.6 12.9 add_convert_fusion
  646.5 11.7 copy.46
  658.2 14.0 convolution_convert_fusion.3
  672.5 50.9 %reduce-scatter.14.cloned.1.call-done = bf16[256,2048]{1,0:T(8,128)(2,1)} async-done(((bf16[1024,2048]{1,0:T(8,128)(2,1)}), bf16[256,2048]{1,0:T(8,128)(2,1)}) %reduce-scatter.14.cloned.1.call-update) | async-done | bytes 1048592 | tf_op jit(solution)/shard_map/reduce_scatter | solution.py:76
  726.2 76.6 %reduce-scatter.12.cloned.1.call-done = bf16[256,2048]{1,0:T(8,128)(2,1)} async-done(((bf16[1024,2048]{1,0:T(8,128)(2,1)}), bf16[256,2048]{1,0:T(8,128)(2,1)}) %reduce-scatter.12.cloned.1.call-update) | async-done | bytes 1048592 | tf_op jit(solution)/shard_map/reduce_scatter | solution.py:76
  802.8 4.6 fusion.29
  807.5 53.3 %all-gather.30.cloned.1.call-done = bf16[1024,2048]{1,0:T(8,128)(2,1)} async-done(((bf16[256,2048]{1,0:T(8,128)(2,1)}), bf16[1024,2048]{1,0:T(8,128)(2,1)}) %all-gather.30.cloned.1.call-update) | async-done | bytes 4194320 | tf_op jit(solution)/shard_map/all_gather | solution.py:72
  860.8 6.2 convolution_convert_fusion.6
  867.1 5.3 convolution_convert_fusion.7
  872.4 23.8 %fusion = (f32[2,4,1024]{2,1,0:T(4,128)S(1)}, f32[2,1024,1024,4]{2,1,3,0:T(8,128)}) fusion(f32[2,4,1024,1024]{2,3,1,0:T(8,128)} %get-tuple-element.43, f32[2,4,1024]{2,1,0:T(4,128)S(1)} %bitcast.157, pred[1024,1024]{0,1:T(8,128)(4,1)S(1)} %copy-done.3, bf16[1024,2,64,1]{0,2,3,1:T(8,128)(2,1)S(1)} %bitcast.163, bf16[1024,2,4,64]{0,3,2,1:T(8,128)(2,1)S(1)} %bitcast.160), kind=kOutput, calls=%fused_computation.2 | convolution fusion | flops 1107288064 | bytes 69533696 | tf_op jit(solution)/shard_map/qhgd,shd->hgqs/dot_general | solution.py:62
  896.3 28.5 %fusion.2 = bf16[2,4,1024,1024]{2,3,1,0:T(8,128)(2,1)} fusion(f32[2,1024,1024,4]{2,1,3,0:T(8,128)} %get-tuple-element.45, f32[2,4,1024,1024]{2,3,1,0:T(8,128)} %get-tuple-element.43, f32[2,4,1024]{2,1,0:T(4,128)S(1)} %get-tuple-element.44, f32[2,4,1024]{2,1,0:T(4,128)S(1)} %bitcast.158, pred[1024,1024]{0,1:T(8,128)(4,1)S(1)} %copy-done.3), kind=kLoop, calls=%fused_computation.4 | loop fusion | flops 41943040 | bytes 85000192 | tf_op jit(solution)/shard_map/convert_element_type | solution.py:65
  924.7 8.8 convolution_multiply_fusion
  936.5 11.0 broadcast_multiply_fusion
  948.6 14.2 fusion.48
  962.8 7.6 convolution_convert_fusion.5
  970.5 14.0 convolution_convert_fusion
  984.6 14.3 convolution_convert_fusion.1
  998.9 14.1 convolution_convert_fusion.2
  1013.1 18.1 %reduce-scatter.18.cloned.1.call-done = bf16[512,768]{1,0:T(8,128)(2,1)} async-done(((bf16[2048,768]{1,0:T(8,128)(2,1)}), bf16[512,768]{1,0:T(8,128)(2,1)}) %reduce-scatter.18.cloned.1.call-update) | async-done | bytes 786448 | tf_op jit(solution)/shard_map/reduce_scatter | solution.py:76
  1031.2 74.6 %reduce-scatter.24.cloned.1.call-done = bf16[256,2048]{1,0:T(8,128)(2,1)} async-done(((bf16[2048,2048]{1,0:T(8,128)(2,1)}), bf16[256,2048]{1,0:T(8,128)(2,1)}) %reduce-scatter.24.cloned.1.call-update) | async-done | bytes 1048592 | tf_op jit(solution)/shard_map/reduce_scatter | solution.py:76
  1105.9 76.1 %reduce-scatter.22.cloned.1.call-done = bf16[256,2048]{1,0:T(8,128)(2,1)} async-done(((bf16[2048,2048]{1,0:T(8,128)(2,1)}), bf16[256,2048]{1,0:T(8,128)(2,1)}) %reduce-scatter.22.cloned.1.call-update) | async-done | bytes 1048592 | tf_op jit(solution)/shard_map/reduce_scatter | solution.py:76
  1182.1 74.9 %reduce-scatter.26.cloned.1.call-done = bf16[1024,512]{1,0:T(8,128)(2,1)} async-done(((bf16[8192,512]{1,0:T(8,128)(2,1)}), bf16[1024,512]{1,0:T(8,128)(2,1)}) %reduce-scatter.26.cloned.1.call-update) | async-done | bytes 1048592 | tf_op jit(solution)/shard_map/reduce_scatter | solution.py:76
  1257.1 7.8 fusion.13
  1270.7 5.4 collective-permute-start.3
  1276.1 7.5 collective-permute-start.2
  1283.6 100.8 %psum.39 = f32[2048]{0:T(1024)S(1)} all-reduce(f32[2048]{0:T(1024)S(1)} %copy-done.24), channel_id=1, replica_groups=mesh['dp'=2,'row'=4,'col'=4] {'dp','row','col'}, use_global_device_ids=true, to_apply=%region_19.20 | all-reduce | flops 2048 | bytes 16384 | tf_op jit(solution)/shard_map/psum | solution.py:181
  1393.4 4.2 convert_element_type.186
  1397.6 11.0 psum.35
  1414.9 15.1 %psum.36 = f32[512]{0:T(512)} all-reduce(f32[512]{0:T(512)S(1)} %get-tuple-element.22), channel_id=1, replica_groups=mesh['dp'=2,'row'=4,'col'=4] {'dp','col'}, use_global_device_ids=true, to_apply=%region_13.14 | all-reduce | flops 512 | bytes 4096 | tf_op jit(solution)/shard_map/psum | solution.py:180
  (171 shorter events, 60.0 us)
Async XLA Ops:
  8.0 235.4 %copy-start = (bf16[512,2048]{1,0:T(8,128)(2,1)S(1)}, bf16[512,2048]{1,0:T(8,128)(2,1)}, u32[]{:S(2)}) copy-start(bf16[512,2048]{1,0:T(8,128)(2,1)} %param.23) | copy-start | bytes 6291460
  8.0 111.2 %all-gather.14.cloned.1.call-start = ((), (), s32[]{:S(2)}) async-start(), calls=%async_computation.11 | async-start | bytes 5242880 | tf_op jit(solution)/shard_map/all_gather | solution.py:72
  8.8 178.4 %all-gather.16.cloned.1.call-start = ((), (), s32[]{:S(2)}) async-start(), calls=%async_computation.12 | async-start | bytes 3932160 | tf_op jit(solution)/shard_map/all_gather | solution.py:72
  10.1 0.7 collective-permute-start
  11.7 225.2 %all-gather.18.cloned.1.call-start = ((), (), s32[]{:S(2)}) async-start(), calls=%async_computation.13 | async-start | bytes 2621440 | tf_op jit(solution)/shard_map/all_gather | solution.py:72
  11.7 101.0 %collective-permute-start.1 = (bf16[512,512]{1,0:T(8,128)(2,1)}, bf16[512,512]{1,0:T(8,128)(2,1)}, u32[]{:S(2)}, u32[]{:S(2)}) collective-permute-start(bf16[512,512]{1,0:T(8,128)(2,1)} %param.20), channel_id=1, source_target_pairs={{0,0},{1,4},{2,8},{3,12},{4,1},{5,5},{6,9},{7,13},{8,2},{9,6},{10,... | collective-permute-start | bytes 1572872 | tf_op jit(solution)/shard_map/ppermute | solution.py:81
  110.5 83.9 %copy-start.28 = (f32[1,4,4,128]{3,1,2,0:T(4,128)}, f32[1,4,4,128]{3,1,2,0:T(4,128)S(1)}, u32[]{:S(2)}) copy-start(f32[1,4,4,128]{3,1,2,0:T(4,128)S(1)} %copy.71) | copy-start | bytes 24580
  112.2 83.5 %copy-start.9 = (f32[1024,64]{0,1:T(8,128)}, f32[1024,64]{0,1:T(8,128)S(1)}, u32[]{:S(2)}) copy-start(f32[1024,64]{0,1:T(8,128)S(1)} %get-tuple-element.36) | copy-start | bytes 786436
  112.8 83.4 %copy-start.2 = (pred[1024,1024]{0,1:T(8,128)(4,1)}, pred[1024,1024]{0,1:T(8,128)(4,1)S(1)}, u32[]{:S(2)}) copy-start(pred[1024,1024]{0,1:T(8,128)(4,1)S(1)} %fusion.22) | copy-start | bytes 3145732
  112.8 206.8 %reduce-scatter.10.cloned.1.call-start = ((), (), s32[]{:S(2)}) async-start(), calls=%async_computation.14 | async-start | bytes 5242880 | tf_op jit(solution)/shard_map/reduce_scatter | solution.py:76
  122.9 71.4 %copy-start.25 = (f32[1024]{0:T(1024)}, f32[1024]{0:T(1024)S(1)}, u32[]{:S(2)}) copy-start(f32[1024]{0:T(1024)S(1)} %add_rsqrt_fusion) | copy-start | bytes 12292
  194.4 28.8 %copy-start.17 = (bf16[1024,128]{0,1:T(8,128)(2,1)}, bf16[1024,128]{0,1:T(8,128)(2,1)S(1)}, u32[]{:S(2)}) copy-start(bf16[1024,128]{0,1:T(8,128)(2,1)S(1)} %slice.98) | copy-start | bytes 786436
  195.6 14.4 copy-start.15
  196.2 13.8 copy-start.5
  243.3 104.2 %all-gather.24.cloned.1.call-start = ((), (), s32[]{:S(2)}) async-start(), calls=%async_computation.17 | async-start | bytes 9437184 | tf_op jit(solution)/shard_map/all_gather | solution.py:87
  244.5 160.8 %all-gather.20.cloned.1.call-start = ((), (), s32[]{:S(2)}) async-start(), calls=%async_computation.15 | async-start | bytes 5242880 | tf_op jit(solution)/shard_map/all_gather | solution.py:72
  324.6 136.0 %all-gather.22.cloned.1.call-start = ((), (), s32[]{:S(2)}) async-start(), calls=%async_computation.16 | async-start | bytes 9437184 | tf_op jit(solution)/shard_map/all_gather | solution.py:87
  327.0 215.9 %all-gather.28.cloned.1.call-start = ((), (), s32[]{:S(2)}) async-start(), calls=%async_computation.20 | async-start | bytes 5242880 | tf_op jit(solution)/shard_map/all_gather | solution.py:72
  345.1 253.3 %all-gather.26.cloned.1.call-start = ((), (), s32[]{:S(2)}) async-start(), calls=%async_computation.18 | async-start | bytes 9437184 | tf_op jit(solution)/shard_map/all_gather | solution.py:87
  347.4 376.0 %reduce-scatter.14.cloned.1.call-start = ((), (), s32[]{:S(2)}) async-start(), calls=%async_computation.21 | async-start | bytes 5242880 | tf_op jit(solution)/shard_map/reduce_scatter | solution.py:76
  620.4 13.2 copy-start.31
  646.5 156.4 %reduce-scatter.12.cloned.1.call-start = ((), (), s32[]{:S(2)}) async-start(), calls=%async_computation.19 | async-start | bytes 5242880 | tf_op jit(solution)/shard_map/reduce_scatter | solution.py:76
  672.2 51.2 %copy-start.4 = (bf16[256,2048]{1,0:T(8,128)(2,1)S(1)}, bf16[256,2048]{1,0:T(8,128)(2,1)}, u32[]{:S(2)}) copy-start(bf16[256,2048]{1,0:T(8,128)(2,1)} %reduce-scatter.10.cloned.1.call-done) | copy-start | bytes 3145732
  672.2 130.6 %copy-start.7 = (bf16[4,32,8,512]{3,2,0,1:T(8,128)(2,1)S(1)}, bf16[4,32,8,512]{3,2,0,1:T(8,128)(2,1)}, u32[]{:S(2)}) copy-start(bf16[4,32,8,512]{3,2,0,1:T(8,128)(2,1)} %copy.70) | copy-start | bytes 3145732
  672.2 188.6 %all-gather.30.cloned.1.call-start = ((), (), s32[]{:S(2)}) async-start(), calls=%async_computation.22 | async-start | bytes 5242880 | tf_op jit(solution)/shard_map/all_gather | solution.py:72
  807.4 205.7 %reduce-scatter.20.cloned.1.call-start = ((), (), s32[]{:S(2)}) async-start(), calls=%async_computation.25 | async-start | bytes 2621440 | tf_op jit(solution)/shard_map/reduce_scatter | solution.py:76
  867.0 164.1 %reduce-scatter.18.cloned.1.call-start = ((), (), s32[]{:S(2)}) async-start(), calls=%async_computation.24 | async-start | bytes 3932160 | tf_op jit(solution)/shard_map/reduce_scatter | solution.py:76
  872.4 23.9 %copy-start.14 = (bf16[1024,512]{0,1:T(8,128)(2,1)}, bf16[1024,512]{0,1:T(8,128)(2,1)S(1)}, u32[]{:S(2)}) copy-start(bf16[1024,512]{0,1:T(8,128)(2,1)S(1)} %convolution_convert_fusion.7) | copy-start | bytes 3145732
  896.3 28.5 %copy-start.16 = (bf16[1024,2,64,1]{0,2,3,1:T(8,128)(2,1)S(1)}, bf16[1024,2,64,1]{0,2,3,1:T(8,128)(2,1)}, u32[]{:S(2)}) copy-start(bf16[1024,2,64,1]{0,2,3,1:T(8,128)(2,1)} %copy-done.15) | copy-start | bytes 786436
  924.7 8.8 copy-start.10
  948.5 14.2 copy-start.20
  948.5 14.2 copy-start.26
  948.5 14.2 copy-start.29
  970.4 135.4 %reduce-scatter.24.cloned.1.call-start = ((), (), s32[]{:S(2)}) async-start(), calls=%async_computation.28 | async-start | bytes 9437184 | tf_op jit(solution)/shard_map/reduce_scatter | solution.py:76
  984.5 197.4 %reduce-scatter.22.cloned.1.call-start = ((), (), s32[]{:S(2)}) async-start(), calls=%async_computation.26 | async-start | bytes 9437184 | tf_op jit(solution)/shard_map/reduce_scatter | solution.py:76
  998.9 258.1 %reduce-scatter.26.cloned.1.call-start = ((), (), s32[]{:S(2)}) async-start(), calls=%async_computation.30 | async-start | bytes 9437184 | tf_op jit(solution)/shard_map/reduce_scatter | solution.py:76
  1013.0 257.7 %all-reduce.3.cloned.1.call-start = ((), (), s32[]{:S(2)}) async-start(), calls=%async_computation.32 | async-start | bytes 2621440 | tf_op jit(solution)/shard_map/psum | solution.py:189
  1031.2 353.8 %all-gather.34.cloned.1.call-start = ((), (), s32[]{:S(2)}) async-start(), calls=%async_computation.29 | async-start | bytes 3145728 | tf_op jit(solution)/shard_map/all_gather | solution.py:72
  1105.8 283.4 %all-gather.32.cloned.1.call-start = ((), (), s32[]{:S(2)}) async-start(), calls=%async_computation.27 | async-start | bytes 3145728 | tf_op jit(solution)/shard_map/all_gather | solution.py:72
  1182.0 211.4 %all-gather.36.cloned.1.call-start = ((), (), s32[]{:S(2)}) async-start(), calls=%async_computation.31 | async-start | bytes 3145728 | tf_op jit(solution)/shard_map/all_gather | solution.py:72
  1257.0 153.9 %reduce-scatter.16.cloned.1.call-start = ((), (), s32[]{:S(2)}) async-start(), calls=%async_computation.23 | async-start | bytes 5242880 | tf_op jit(solution)/shard_map/reduce_scatter | solution.py:76
  1264.8 18.8 %copy-start.24 = (f32[2048]{0:T(1024)S(1)}, f32[2048]{0:T(1024)}, u32[]{:S(2)}) copy-start(f32[2048]{0:T(1024)} %get-tuple-element.11) | copy-start | bytes 24580
  1267.2 117.9 %all-to-all-start = ((bf16[256,4,512]{2,0,1:T(8,128)(2,1)}), bf16[256,4,512]{2,0,1:T(8,128)(2,1)S(1)}, u32[]{:S(2)}, u32[]{:S(2)}) async-start(bf16[256,4,512]{2,0,1:T(8,128)(2,1)} %bitcast.138), calls=%async_computation.2 | async-start | bytes 2097152 | tf_op jit(solution)/shard_map/all_to_all | solution.py:154
  1270.7 137.8 %collective-permute-start.3 = (bf16[512,512]{1,0:T(8,128)(2,1)}, bf16[512,512]{1,0:T(8,128)(2,1)}, u32[]{:S(2)}, u32[]{:S(2)}) collective-permute-start(bf16[512,512]{1,0:T(8,128)(2,1)} %get-tuple-element.14), channel_id=1, source_target_pairs={{0,0},{1,4},{2,8},{3,12},{4,1},{5,5},{6,9},{7,13},{8,2},{9,6},{10,... | collective-permute-start | bytes 1572872 | tf_op jit(solution)/shard_map/ppermute | solution.py:81
  1276.1 153.9 %collective-permute-start.2 = (bf16[512,768]{1,0:T(8,128)(2,1)}, bf16[512,768]{1,0:T(8,128)(2,1)}, u32[]{:S(2)}, u32[]{:S(2)}) collective-permute-start(bf16[512,768]{1,0:T(8,128)(2,1)} %get-tuple-element.13), channel_id=1, source_target_pairs={{0,0},{1,4},{2,8},{3,12},{4,1},{5,5},{6,9},{7,13},{8,2},{9,6},{10,... | collective-permute-start | bytes 2359304 | tf_op jit(solution)/shard_map/ppermute | solution.py:81
  1393.4 15.2 %copy-start.23 = (f32[1024]{0:T(1024)S(1)}, f32[1024]{0:T(1024)}, u32[]{:S(2)}) copy-start(f32[1024]{0:T(1024)} %copy-done.22) | copy-start | bytes 12292
  1393.4 17.5 %copy-start.27 = (f32[512]{0:T(512)S(1)}, f32[512]{0:T(512)}, u32[]{:S(2)}) copy-start(f32[512]{0:T(512)} %param.16) | copy-start | bytes 6148
  1408.6 26.3 %copy-start.1 = (bf16[512,2048]{1,0:T(8,128)(2,1)S(1)}, bf16[512,2048]{1,0:T(8,128)(2,1)}, u32[]{:S(2)}) copy-start(bf16[512,2048]{1,0:T(8,128)(2,1)} %param.23) | copy-start | bytes 6291460
  (11 other events, 31.9 us)
Sparse Core Ops, SparseCore 0:
  10.7 108.5 all-gather.13
  121.4 65.7 all-gather.15
  188.7 44.5 all-gather.17
  243.4 76.1 reduce-scatter.9
  646.6 76.7 reduce-scatter.13
  725.5 77.2 reduce-scatter.11
  807.6 53.2 all-gather.29
  867.1 43.8 reduce-scatter.19
  970.5 60.5 reduce-scatter.17
  1034.5 71.2 reduce-scatter.23
  1109.7 72.2 reduce-scatter.21
  1185.3 71.6 reduce-scatter.25
  1265.0 121.1 reduce-scatter.15
Sparse Core Ops, SparseCore 1:
  246.4 62.6 all-gather.23
  324.7 80.6 all-gather.19
  407.8 52.7 all-gather.21
  462.3 80.6 all-gather.27
  545.6 52.7 all-gather.25
  1031.3 19.7 all-reduce.2
  1105.9 10.7 all-gather.33
  1182.1 11.9 all-gather.31
  1257.1 10.4 all-gather.35

commit v2 on v1

v2 whole, which is shorter than its diff:
```python
import functools

import jax
import jax.numpy as jnp
from jax import lax
from jax.experimental import pallas as pl
from jax.experimental.pallas import tpu as pltpu
from jax.sharding import PartitionSpec as P

HEAD = 64
EPSILON = 1e-05
THETA = 500000.0
F32 = jnp.float32
BF16 = jnp.bfloat16


MESH = pl.DeviceIdType.MESH
VMEM_LIMIT = 60 * 1024 * 1024


def greet(row_size=0, col_size=0, dp_size=0):
    barrier = pltpu.get_barrier_semaphore()
    if row_size:
        row = lax.axis_index("row")
        for mask in range(1, row_size):
            pl.semaphore_signal(barrier, inc=1, device_id={"row": row ^ mask}, device_id_type=MESH)
    if col_size:
        col = lax.axis_index("col")

        @pl.when(col > 0)
        def _():
            pl.semaphore_signal(barrier, inc=1, device_id={"col": col - 1}, device_id_type=MESH)

        @pl.when(col < col_size - 1)
        def _():
            pl.semaphore_signal(barrier, inc=1, device_id={"col": col + 1}, device_id_type=MESH)

    if dp_size:
        pl.semaphore_signal(barrier, inc=1, device_id={"dp": 1 - lax.axis_index("dp")}, device_id_type=MESH)
    count = max(row_size - 1, 0) + (1 if dp_size else 0)
    if col_size:
        count = count + jnp.where(col > 0, 1, 0) + jnp.where(col < col_size - 1, 1, 0)
    pl.semaphore_wait(barrier, count)


def remote(src, dst, sends, recvs, place, device):
    return pltpu.make_async_remote_copy(
        src_ref=src, dst_ref=dst, send_sem=sends.at[place], recv_sem=recvs.at[place],
        device_id=device, device_id_type=MESH,
    )


class RowGather:
    def __init__(self, size, ref, sends, recvs):
        self.size, self.ref, self.sends, self.recvs = size, ref, sends, recvs
        self.bits = size.bit_length() - 1
        self.row = lax.axis_index("row")
        self.half = ref.shape[1] // 2

    @staticmethod
    def semaphores(size):
        return pltpu.SemaphoreType.DMA((2 * (size - 1),))

    def copies(self, step):
        out = []
        for part in range(2):
            order = list(range(self.bits)) if part == 0 else list(range(self.bits))[::-1]
            bit = 1 << order[step]
            for item in range(1 << step):
                mask = 0
                for j in range(step):
                    if item >> j & 1:
                        mask |= 1 << order[j]
                piece = self.ref.at[self.row ^ mask, pl.ds(part * self.half, self.half)]
                place = part * (self.size - 1) + (1 << step) - 1 + item
                out.append(remote(piece, piece, self.sends, self.recvs, place, {"row": self.row ^ bit}))
        return out

    def start(self):
        self.all = [self.copies(step) for step in range(self.bits)]
        for step in range(self.bits):
            count = 1 << step
            for part in range(2):
                self.all[step][part * count].start()

    def run(self):
        for step in range(self.bits):
            for copy in self.all[step]:
                copy.wait_recv()
            if step + 1 < self.bits:
                count = 1 << (step + 1)
                for part in range(2):
                    for item in range(1, count):
                        if item >> step & 1:
                            self.all[step + 1][part * count + item].start()
                for later in range(step + 2, self.bits):
                    count = 1 << later
                    for part in range(2):
                        for item in range(1, count):
                            if item >> (step + 1) == 0 and item >> step & 1:
                                self.all[later][part * count + item].start()
        for step in range(self.bits):
            for copy in self.all[step]:
                copy.wait_send()


def row_scatter_semaphores(size):
    return pltpu.SemaphoreType.DMA((2 * (size - 1),))


def row_scatter(size, part_ref, recv_ref, sends, recvs, finish):
    bits = size.bit_length() - 1
    row = lax.axis_index("row")
    half = part_ref.shape[1] // 2
    plans = []
    for part in range(2):
        order = list(range(bits)) if part == 0 else list(range(bits))[::-1]
        steps = []
        for step in range(bits):
            bit = 1 << order[step]
            rest = order[step + 1 :]
            copies = []
            count = 1 << len(rest)
            for item in range(count - 1, -1, -1):
                mask = bit
                for j, other in enumerate(rest):
                    if item >> j & 1:
                        mask |= 1 << other
                place = (size - 2 * count) + item
                copies.append((
                    item, mask ^ bit, place,
                    remote(
                        part_ref.at[row ^ mask, pl.ds(part * half, half)],
                        recv_ref.at[place, pl.ds(part * half, half)],
                        sends, recvs, part * (size - 1) + place, {"row": row ^ bit},
                    ),
                ))
            steps.append(copies)
        plans.append(steps)
    for part in range(2):
        for _, _, _, copy in plans[part][0]:
            copy.start()
    for step in range(bits):
        for part in range(2):
            rows = pl.ds(part * half, half)
            for item, mask, place, copy in plans[part][step]:
                copy.wait_recv()
                total = part_ref[row ^ mask, rows].astype(F32) + recv_ref[place, rows].astype(F32)
                if item:
                    part_ref[row ^ mask, rows] = total.astype(BF16)
                    if step + 1 < bits:
                        for item2, mask2, _, copy2 in plans[part][step + 1]:
                            sent = mask2 ^ (1 << (list(range(bits)) if part == 0 else list(range(bits))[::-1])[step + 1])
                            if sent == mask:
                                copy2.start()
                elif step + 1 < bits:
                    part_ref[row, rows] = total.astype(BF16)
                else:
                    finish(rows, total)
    for part in range(2):
        for step in range(bits):
            for _, _, _, copy in plans[part][step]:
                copy.wait_send()


def col_gather(size, ref, sends, recvs, seen=None):
    col = lax.axis_index("col")

    def right(step):
        piece = ref.at[lax.rem(col - step + size, size)]
        return remote(piece, piece, sends, recvs, step, {"col": lax.rem(col + 1, size)})

    def left(step):
        piece = ref.at[lax.rem(col + step, size)]
        return remote(piece, piece, sends, recvs, size - 1 + step, {"col": lax.rem(col + size - 1, size)})

    for step in range(size):
        for copy, has, goes in ((right, col >= step, col < size - 1), (left, col + step < size, col > 0)):
            if step:

                @pl.when(has)
                def _():
                    copy(step - 1).wait_recv()

            if step < size - 1:

                @pl.when(has & goes)
                def _():
                    copy(step).start()

            if seen is not None and (step or copy is right):

                @pl.when(has)
                def _():
                    seen(lax.rem(col - step + size, size) if copy is right else lax.rem(col + step, size))

    for step in range(size - 1):
        for copy, has, goes in ((right, col >= step, col < size - 1), (left, col + step < size, col > 0)):

            @pl.when(has & goes)
            def _():
                copy(step).wait_send()


def col_scatter(size, part_ref, recv_ref, sends, recvs, prepare):
    col = lax.axis_index("col")

    def right(target, source):
        return pltpu.make_async_remote_copy(
            src_ref=source.at[target], dst_ref=recv_ref.at[0, target], send_sem=sends.at[0], recv_sem=recvs.at[target],
            device_id={"col": lax.rem(col + 1, size)}, device_id_type=MESH,
        )

    def left(target, source):
        return pltpu.make_async_remote_copy(
            src_ref=source.at[target], dst_ref=recv_ref.at[1, target], send_sem=sends.at[1], recv_sem=recvs.at[size + target],
            device_id={"col": lax.rem(col + size - 1, size)}, device_id_type=MESH,
        )

    for time in range(2 * size - 1):
        for copy, side, first, step in ((right, 0, col == 0, time - col), (left, 1, col == size - 1, time - (size - 1 - col))):
            target = size - 1 - step if side == 0 else step
            valid = (step >= 0) & ((target >= col) if side == 0 else (target <= col))
            place = lax.rem(target + 4 * size, size)

            @pl.when(valid & ((target != col) | (side == 0)))
            def _():
                prepare(place)

            @pl.when(valid & jnp.logical_not(first))
            def _():
                copy(place, part_ref).wait_recv()

            @pl.when(valid & jnp.logical_not(first) & (target != col))
            def _():
                recv_ref[side, place] = (
                    recv_ref[side, place].astype(F32) + part_ref[place].astype(F32)
                ).astype(BF16)

            @pl.when(valid & (step > 0))
            def _():
                copy(place, part_ref).wait_send()

            @pl.when(valid & (target != col) & first)
            def _():
                copy(place, part_ref).start()

            @pl.when(valid & (target != col) & jnp.logical_not(first))
            def _():
                copy(place, recv_ref.at[side]).start()


VM = pl.BlockSpec(memory_space=pltpu.VMEM)


def params(ident):
    return pltpu.CompilerParams(collective_id=ident, has_side_effects=True, vmem_limit_bytes=VMEM_LIMIT)


def first_kernel(
    size, act_ref, cot_ref, small_ref, qkv_ref, out_ref,
    x_ref, first_ref, inv_ref, tok_ref, smalls_ref, qkvs_ref, outs_ref,
    got_ref, zq_ref, zo_ref, s1, r1, s2, r2, s3, r3, szq, rzq, szo, rzo, srow, rrow, score, rcore,
):
    row, col, core = lax.axis_index("row"), lax.axis_index("col"), lax.axis_index("dp")
    length, width = act_ref.shape
    quarter = length // size
    small_rows = small_ref.shape[0]
    gain_row = 2 * length // 128
    x_ref[row] = act_ref[...]
    smalls_ref[row] = small_ref[...]
    blocks = ((qkv_ref, zq_ref, qkvs_ref, szq, rzq), (out_ref, zo_ref, outs_ref, szo, rzo))
    for block, line, _, _, _ in blocks:
        share = block.shape[0] // 2
        line[col] = block[pl.ds(pl.multiple_of(core * share, 16), share)]
    greet(row_size=size, col_size=size, dp_size=2)
    gather = RowGather(size, x_ref, s1, r1)
    smalls = [
        remote(small_ref, smalls_ref.at[row], s3, r3, mask - 1, {"row": row ^ mask}) for mask in range(1, size)
    ]
    for move in smalls:
        move.start()
    gather.start()
    moves = [
        remote(cot_ref.at[pl.ds((row ^ mask) * quarter, quarter)], got_ref.at[row], s2, r2, mask - 1, {"row": row ^ mask})
        for mask in range(1, size)
    ]
    got_ref[row] = cot_ref[pl.ds(pl.multiple_of(row * quarter, 16), quarter)]

    def half(ref, place):
        share = ref.shape[1] // 2
        return ref.at[place, pl.ds(pl.multiple_of(core * share, 16), share)]

    def hand(which, mask):
        _, line, full, _, _ = blocks[which]
        return remote(line.at[row ^ mask], half(full, row), srow, rrow, which * (size - 1) + mask - 1, {"row": row ^ mask})

    def across(which, mask):
        full = blocks[which][2]
        piece = half(full, row ^ mask)
        return remote(piece, piece, score, rcore, which * size + mask, {"dp": 1 - core})

    def seen(which):
        def act(place):
            _, line, full, _, _ = blocks[which]

            @pl.when(place == row)
            def _():
                share = full.shape[1] // 2
                full[row, pl.ds(pl.multiple_of(core * share, 16), share)] = line[row]
                across(which, 0).start()

            for mask in range(1, size):

                @pl.when(place == row ^ mask)
                def _():
                    hand(which, mask).start()

        return act

    gather.run()
    for move in smalls:
        move.wait()

    for which, (_, line, _, sends, recvs) in enumerate(blocks):
        col_gather(size, line, sends, recvs, seen(which))
        if which == 0:
            for move in moves:
                move.start()

    @pl.loop(0, length // 128)
    def _(i):
        rows = pl.ds(pl.multiple_of(i * 128, 128), 128)
        total = jnp.zeros((128, 1), F32)
        for j in range(size):
            value = x_ref[j, rows].astype(F32)
            total += jnp.sum(value * value, axis=1, keepdims=True)
        inverse = lax.rsqrt(total / (size * width) + EPSILON)
        inv_ref[rows] = inverse
        for j in range(size):
            for k in range(width // 128):
                gain = smalls_ref[j, gain_row + k : gain_row + k + 1]
                value = x_ref[j, rows, k * 128 : (k + 1) * 128].astype(F32)
                first_ref[rows, j * width + k * 128 : j * width + (k + 1) * 128] = (value * inverse * gain).astype(BF16)

    for which in range(2):
        for mask in range(1, size):
            hand(which, mask).wait_recv()
            across(which, mask).start()
    for move in moves:
        move.wait()
    for j in range(size):
        tok_ref[:, j * width : (j + 1) * width] = got_ref[j]
    for which in range(2):
        for mask in range(1, size):
            hand(which, mask).wait_send()
        for mask in range(size):
            across(which, mask).wait()


def first_call(activations, cotangent, small, qkv_weight, out_weight):
    size = lax.axis_size("row")
    length, width = activations.shape
    quarter = length // size
    qkv_cols, heads_cols = qkv_weight.shape[1], out_weight.shape[0]
    dma = pltpu.SemaphoreType.DMA
    return pl.pallas_call(
        functools.partial(first_kernel, size),
        out_shape=(
            jax.ShapeDtypeStruct((size, length, width), BF16),
            jax.ShapeDtypeStruct((length, size * width), BF16),
            jax.ShapeDtypeStruct((length, 1), F32),
            jax.ShapeDtypeStruct((quarter, size * width), BF16),
            jax.ShapeDtypeStruct((size,) + small.shape, F32),
            jax.ShapeDtypeStruct((size,) + qkv_weight.shape, BF16),
            jax.ShapeDtypeStruct((size,) + out_weight.shape, BF16),
        ),
        in_specs=[VM] * 5,
        out_specs=(VM,) * 7,
        scratch_shapes=[
            pltpu.VMEM((size, quarter, width), BF16),
            pltpu.VMEM((size, width // 2, qkv_cols), BF16),
            pltpu.VMEM((size, heads_cols // 2, width), BF16),
        ]
        + [dma((2 * (size - 1),))] * 2
        + [dma((size - 1,))] * 4
        + [dma((2 * (size - 1),))] * 4
        + [dma((2 * (size - 1),))] * 2
        + [dma((2 * size,))] * 2,
        compiler_params=params(1),
    )(activations, cotangent, small, qkv_weight, out_weight)


def turn(values, low):
    return jnp.where(low, -pltpu.roll(values, 128 - HEAD // 2, 1), pltpu.roll(values, HEAD // 2, 1))


def low_columns(rows):
    return lax.broadcasted_iota(jnp.int32, (rows, 128), 1) % HEAD < HEAD // 2


def masked_scores(query, key, seg_col, seg_row, first_row):
    scores = lax.dot_general(query, key, (((1,), (1,)), ((), ())), preferred_element_type=F32)
    rows = lax.broadcasted_iota(jnp.int32, scores.shape, 0) + first_row
    columns = lax.broadcasted_iota(jnp.int32, scores.shape, 1)
    allowed = (seg_col == seg_row) & (rows >= columns)
    return jnp.where(allowed, scores, -1e30)


def attend_kernel(first_ref, weight_ref, cos_ref, sin_ref, segc_ref, segr_ref, q_ref, k_ref, v_ref, o_ref, oh_ref):
    heads, length, _ = q_ref.shape
    kvs = k_ref.shape[0]
    group = heads // kvs
    query_cols = heads * HEAD
    key_cols = (weight_ref.shape[1] - query_cols) // 2
    block = 256

    @pl.loop(0, length // block)
    def _(i):
        rows = pl.ds(pl.multiple_of(i * block, block), block)
        low = low_columns(block)
        cosine, sine = cos_ref[rows], sin_ref[rows]
        whole = jnp.dot(first_ref[rows], weight_ref[...], preferred_element_type=F32)
        for ref, count, start, factor in ((q_ref, heads, 0, HEAD ** (-0.5)), (k_ref, kvs, query_cols, 1.0)):
            for j in range((count + 1) // 2):
                part = whole[:, start + 128 * j : start + 128 * (j + 1)]
                part = ((part * cosine + turn(part, low) * sine) * factor).astype(BF16)
                for side in range(min(2, count - 2 * j)):
                    ref[2 * j + side, rows] = part[:, side * HEAD : (side + 1) * HEAD]
        for j in range(kvs):
            at = query_cols + key_cols + j * HEAD
            v_ref[j, rows] = whole[:, at : at + HEAD].astype(BF16)

    @pl.loop(0, heads)
    def _(head):
        kv = lax.div(head, group)
        for i in range(length // block):
            rows, extent = slice(i * block, (i + 1) * block), (i + 1) * block
            scores = masked_scores(q_ref[head, rows], k_ref[kv, :extent], segc_ref[rows], segr_ref[:, :extent], i * block)
            top = jnp.max(scores, axis=1, keepdims=True)
            weights = jnp.exp(scores - top)
            total = jnp.sum(weights, axis=1, keepdims=True)
            mixed = jnp.dot(weights.astype(BF16), v_ref[kv, :extent], preferred_element_type=F32)
            oh_ref[head, rows] = (mixed / total).astype(BF16)

    for head in range(heads):
        o_ref[:, head * HEAD : (head + 1) * HEAD] = oh_ref[head]


def attend_call(first, weight, cosine, sine, segc, segr, heads, kvs):
    length = first.shape[0]
    return pl.pallas_call(
        attend_kernel,
        out_shape=(
            jax.ShapeDtypeStruct((heads, length, HEAD), BF16),
            jax.ShapeDtypeStruct((kvs, length, HEAD), BF16),
            jax.ShapeDtypeStruct((kvs, length, HEAD), BF16),
            jax.ShapeDtypeStruct((length, heads * HEAD), BF16),
        ),
        in_specs=[VM] * 6,
        out_specs=(VM,) * 4,
        scratch_shapes=[pltpu.VMEM((heads, length, HEAD), BF16)],
        compiler_params=pltpu.CompilerParams(vmem_limit_bytes=VMEM_LIMIT),
    )(first, weight, cosine, sine, segc, segr)


def attend_back_kernel(
    dmid_ref, weight_ref, q_ref, k_ref, v_ref, cos_ref, sin_ref, segc_ref, segr_ref,
    dqkv_ref, inner_ref, do_ref, dq_ref, dk_ref, dv_ref,
):
    heads, length, _ = q_ref.shape
    kvs = k_ref.shape[0]
    group = heads // kvs
    query_cols = heads * HEAD
    key_cols = (dqkv_ref.shape[1] - query_cols) // 2
    block = 256
    parts, _, width = weight_ref.shape
    dk_ref[...] = jnp.zeros_like(dk_ref)
    dv_ref[...] = jnp.zeros_like(dv_ref)
    inner_ref[...] = jnp.zeros_like(inner_ref)

    @pl.loop(0, length // block)
    def _(i):
        rows = pl.ds(pl.multiple_of(i * block, block), block)
        total = jnp.zeros((block, query_cols), F32)
        for j in range(parts):
            total += lax.dot_general(
                dmid_ref[rows, j * width : (j + 1) * width], weight_ref[j], (((1,), (1,)), ((), ())), preferred_element_type=F32
            )
        for head in range(heads):
            do_ref[head, rows] = total[:, head * HEAD : (head + 1) * HEAD].astype(BF16)

    @pl.loop(0, heads)
    def _(head):
        kv = lax.div(head, group)
        for i in range(length // block):
            rows, extent = slice(i * block, (i + 1) * block), (i + 1) * block
            query, keys, grads = q_ref[head, rows], k_ref[kv, :extent], do_ref[head, rows]
            scores = masked_scores(query, keys, segc_ref[rows], segr_ref[:, :extent], i * block)
            top = jnp.max(scores, axis=1, keepdims=True)
            weights = jnp.exp(scores - top)
            weights = weights * (1.0 / jnp.sum(weights, axis=1, keepdims=True))
            back = lax.dot_general(grads, v_ref[kv, :extent], (((1,), (1,)), ((), ())), preferred_element_type=F32)
            dv_ref[kv, :extent] += lax.dot_general(
                weights.astype(BF16), grads, (((0,), (0,)), ((), ())), preferred_element_type=F32
            )
            ds = (weights * (back - jnp.sum(weights * back, axis=1, keepdims=True))).astype(BF16)
            dq = jnp.dot(ds, keys, preferred_element_type=F32)
            inner_ref[rows] += jnp.sum(dq * query.astype(F32), axis=1, keepdims=True)
            dq_ref[head, rows] = dq
            dk_ref[kv, :extent] += lax.dot_general(ds, query, (((0,), (0,)), ((), ())), preferred_element_type=F32)

    @pl.loop(0, length // block)
    def _(i):
        rows = pl.ds(pl.multiple_of(i * block, block), block)
        low = low_columns(block)
        cosine, sine = cos_ref[rows], sin_ref[rows]
        for ref, count, start, factor in ((dq_ref, heads, 0, HEAD ** (-0.5)), (dk_ref, kvs, query_cols, 1.0), (dv_ref, kvs, query_cols + key_cols, None)):
            for j in range((count + 1) // 2):
                sides = [ref[2 * j + side, rows] if 2 * j + side < count else jnp.zeros((block, HEAD), F32) for side in range(2)]
                part = jnp.concatenate(sides, axis=1)
                if factor is not None:
                    part = (part * cosine - turn(part * sine, low)) * factor
                dqkv_ref[rows, start + 128 * j : start + 128 * (j + 1)] = part.astype(BF16)
        more = jnp.zeros((block, 1), F32)
        for kv in range(kvs):
            more += jnp.sum(dk_ref[kv, rows] * k_ref[kv, rows].astype(F32) + dv_ref[kv, rows] * v_ref[kv, rows].astype(F32), axis=1, keepdims=True)
        inner_ref[rows] += more


def attend_back_call(dmid, weight, q, k, v, cosine, sine, segc, segr, columns):
    heads, length, _ = q.shape
    kvs = k.shape[0]
    return pl.pallas_call(
        attend_back_kernel,
        out_shape=(jax.ShapeDtypeStruct((length, columns), BF16), jax.ShapeDtypeStruct((length, 1), F32)),
        in_specs=[VM] * 9,
        out_specs=(VM,) * 2,
        scratch_shapes=[
            pltpu.VMEM((heads, length, HEAD), BF16),
            pltpu.VMEM((heads, length, HEAD), F32),
            pltpu.VMEM((kvs, length, HEAD), F32),
            pltpu.VMEM((kvs, length, HEAD), F32),
        ],
        compiler_params=pltpu.CompilerParams(vmem_limit_bytes=VMEM_LIMIT),
    )(dmid, weight, q, k, v, cosine, sine, segc, segr)


def middle_kernel(rows_n, cols_n, attn_ref, weight_ref, x_ref, gain_ref, mid_ref, second_ref, part_ref, recv_ref, s1, r1, s2, r2):
    row, col = lax.axis_index("row"), lax.axis_index("col")
    quarter, features = mid_ref.shape
    width = features // rows_n
    greet(row_size=rows_n, col_size=cols_n)

    @pl.loop(0, rows_n)
    def _(i):
        own = attn_ref[pl.ds(pl.multiple_of(i * quarter, 16), quarter)]
        for j in range(rows_n):
            part_ref[i, :, j * width : (j + 1) * width] = jnp.dot(own, weight_ref[j], preferred_element_type=F32).astype(BF16)

    def finish(rows, total):
        own = pl.ds(row * quarter + rows.start, rows.size)
        squares = jnp.zeros((rows.size, 1), F32)
        for j in range(rows_n):
            columns = slice(j * width, (j + 1) * width)
            value = total[:, columns] + x_ref[j, own].astype(F32)
            mid_ref[rows, columns] = value
            squares += jnp.sum(value * value, axis=1, keepdims=True)
        inverse = lax.rsqrt(squares / features + EPSILON)
        second_ref[col, rows] = (mid_ref[rows] * inverse * gain_ref[...]).astype(BF16)

    row_scatter(rows_n, part_ref, recv_ref, s1, r1, finish)
    col_gather(cols_n, second_ref, s2, r2)


def middle_call(attn, weight, x, gain):
    rows_n, cols_n = lax.axis_size("row"), lax.axis_size("col")
    length, features = attn.shape[0], weight.shape[0] * weight.shape[2]
    quarter = length // rows_n
    return pl.pallas_call(
        functools.partial(middle_kernel, rows_n, cols_n),
        out_shape=(
            jax.ShapeDtypeStruct((quarter, features), F32),
            jax.ShapeDtypeStruct((cols_n, quarter, features), BF16),
        ),
        in_specs=[VM] * 4,
        out_specs=(VM,) * 2,
        scratch_shapes=[
            pltpu.VMEM((rows_n, quarter, features), BF16),
            pltpu.VMEM((rows_n - 1, quarter, features), BF16),
        ]
        + [pltpu.SemaphoreType.DMA((2 * (rows_n - 1),))] * 2
        + [pltpu.SemaphoreType.DMA((2 * (cols_n - 1),))] * 2,
        compiler_params=params(2),
    )(attn, weight, x, gain)


def back_kernel(rows_n, cols_n, dgate_ref, dup_ref, gate_ref, up_ref, mid_ref, tok_ref, gain_ref, dmid_ref, grad_ref, part_ref, recv_ref, s1, r1, s2, r2):
    row, col = lax.axis_index("row"), lax.axis_index("col")
    quarter, features = mid_ref.shape
    greet(row_size=rows_n, col_size=cols_n)

    def prepare(target):
        tile = 512

        @pl.loop(0, features // tile)
        def _(i):
            columns = pl.ds(i * tile, tile)
            value = lax.dot_general(dgate_ref[target], gate_ref[columns], (((1,), (1,)), ((), ())), preferred_element_type=F32)
            value += lax.dot_general(dup_ref[target], up_ref[columns], (((1,), (1,)), ((), ())), preferred_element_type=F32)
            part_ref[target, :, columns] = value.astype(BF16)

    col_scatter(cols_n, part_ref, recv_ref, s1, r1, prepare)

    grad_ref[...] = jnp.zeros_like(grad_ref)

    @pl.loop(0, quarter // 64)
    def _(i):
        rows = pl.ds(i * 64, 64)
        got = part_ref[col, rows].astype(F32)
        got += jnp.where(col > 0, recv_ref[0, col, rows].astype(F32), 0.0)
        got += jnp.where(col < cols_n - 1, recv_ref[1, col, rows].astype(F32), 0.0)
        middle = mid_ref[rows]
        inverse = lax.rsqrt(jnp.sum(middle * middle, axis=1, keepdims=True) / features + EPSILON)
        weighted = got * gain_ref[...]
        inner = jnp.sum(middle * weighted, axis=1, keepdims=True) / features
        grad_ref[...] += jnp.sum(got * middle * inverse, axis=0, keepdims=True)
        value = tok_ref[rows].astype(F32) + inverse * weighted - middle * (inverse * inverse * inverse * inner)
        dmid_ref[row, rows] = value.astype(BF16)

    gather = RowGather(rows_n, dmid_ref, s2, r2)
    gather.start()
    gather.run()


def back_call(dgate, dup, gate, up, middle, tok, gain):
    rows_n, cols_n = lax.axis_size("row"), lax.axis_size("col")
    quarter, features = middle.shape
    hidden = gate.shape[1]
    return pl.pallas_call(
        functools.partial(back_kernel, rows_n, cols_n),
        out_shape=(
            jax.ShapeDtypeStruct((rows_n, quarter, features), BF16),
            jax.ShapeDtypeStruct((1, features), F32),
        ),
        in_specs=[VM] * 7,
        out_specs=(VM,) * 2,
        scratch_shapes=[
            pltpu.VMEM((cols_n, quarter, features), BF16),
            pltpu.VMEM((2, cols_n, quarter, features), BF16),
        ]
        + [pltpu.SemaphoreType.DMA((2,)), pltpu.SemaphoreType.DMA((2 * cols_n,))]
        + [pltpu.SemaphoreType.DMA((2 * (rows_n - 1),))] * 2,
        compiler_params=params(3),
    )(dgate.reshape(cols_n, quarter, hidden), dup.reshape(cols_n, quarter, hidden), gate, up, middle, tok, gain)


def last_kernel(size, dqkv_ref, weight_ref, out_ref, part_ref, recv_ref, s1, r1):
    greet(row_size=size)

    @pl.loop(0, size)
    def _(i):
        part_ref[i] = lax.dot_general(dqkv_ref[...], weight_ref[i], (((1,), (1,)), ((), ())), preferred_element_type=F32).astype(BF16)

    def finish(rows, total):
        out_ref[rows] = total

    row_scatter(size, part_ref, recv_ref, s1, r1, finish)


def last_call(dqkv, weight):
    size = lax.axis_size("row")
    length = dqkv.shape[0]
    width = weight.shape[0] // size
    return pl.pallas_call(
        functools.partial(last_kernel, size),
        out_shape=jax.ShapeDtypeStruct((length, width), F32),
        in_specs=[VM] * 2,
        out_specs=VM,
        scratch_shapes=[pltpu.VMEM((size, length, width), BF16), pltpu.VMEM((size - 1, length, width), BF16)]
        + [pltpu.SemaphoreType.DMA((2 * (size - 1),))] * 2,
        compiler_params=params(4),
    )(dqkv, weight.reshape(size, width, weight.shape[1]))


def dot(left, right, dims):
    return lax.dot_general(left, right, (dims, ((), ())), preferred_element_type=F32)


def rotary_tables(positions):
    exponent = jnp.arange(0, HEAD, 2).astype(F32) / HEAD
    inverse = jnp.power(F32(THETA), -exponent)
    phase = positions[:, None] * inverse[None, :]
    phase = jnp.concatenate([phase] * (2 * 128 // HEAD), axis=1)
    return (jnp.cos(phase), jnp.sin(phase))


def gather(values, axis_name, axis=0):
    return lax.all_gather(values, axis_name, axis=axis, tiled=True)


def scatter(values, axis_name, axis=0):
    return lax.psum_scatter(values.astype(BF16), axis_name, scatter_dimension=axis, tiled=True)


def swap(values):
    rows, cols = lax.axis_size("row"), lax.axis_size("col")
    return lax.ppermute(values, ("row", "col"), [(r * cols + c, c * cols + r) for r in range(rows) for c in range(cols)])


def gather_shared(values):
    share = values.shape[0] // lax.axis_size("dp")
    part = lax.dynamic_slice_in_dim(values, lax.axis_index("dp") * share, share, 0)
    return lax.all_gather(part, ("row", "dp"), axis=0, tiled=True)


def scatter_shared(values):
    part = scatter(values, ("row", "dp"))
    return gather(part, "dp").astype(F32)


def local(
    activations, segments, positions, first_gain, query_weight, key_weight, value_weight, out_weight,
    second_gain, gate_weight, up_weight, down_weight, cotangent,
):
    rows = lax.axis_size("row")
    row, col = lax.axis_index("row"), lax.axis_index("col")
    length, width = activations.shape
    features = rows * width
    query_cols, key_cols = query_weight.shape[1], key_weight.shape[1]
    heads, kvs = query_cols // HEAD, key_cols // HEAD
    hidden_cols = gate_weight.shape[1]
    spare = jnp.zeros((width, -key_cols % 128), BF16)
    key_span = key_cols + spare.shape[1]
    qkv_cols = query_cols + 2 * key_span

    small = jnp.concatenate([segments.astype(F32), positions.astype(F32), first_gain, second_gain]).reshape(-1, 128)
    qkv_weight = jnp.concatenate([query_weight, key_weight, spare, value_weight, spare], axis=1)
    x_blocks, first, inv1, cot_tok, smalls, qkv_all, out_all_w = first_call(activations, cotangent, small, qkv_weight, out_weight)
    qkv_all = qkv_all.reshape(features, qkv_cols)
    smalls = smalls.reshape(rows, -1)
    own = lax.dynamic_slice_in_dim(smalls, col, 1, 0)[0]
    segment_own, position_own = own[:length], own[length : 2 * length]
    gain2 = smalls[:, 2 * length + width :].reshape(1, features)

    gate_all = gather_shared(gate_weight)
    up_all = gather_shared(up_weight)
    cot_all = gather(cot_tok, "col")
    down_all = gather_shared(down_weight).reshape(rows, hidden_cols, width)

    cosine, sine = rotary_tables(position_own)
    segc, segr = segment_own[:, None], segment_own[None]
    q, k, v, attn = attend_call(first, qkv_all, cosine, sine, segc, segr, heads, kvs)
    middle, second_all = middle_call(attn, out_all_w, x_blocks, gain2)
    second_all = second_all.reshape(-1, features)
    gate = dot(second_all, gate_all, ((1,), (0,)))
    up = dot(second_all, up_all, ((1,), (0,)))
    sigma = jax.nn.sigmoid(gate)
    swish = gate * sigma
    hidden = (swish * up).astype(BF16)
    tokens = hidden.shape[0]
    down_part = lax.dot_general(hidden, down_all, (((1,), (1,)), ((), ())), preferred_element_type=F32).reshape(tokens, features)
    out_tok = (middle + scatter(down_part, "col").astype(F32)).astype(BF16)
    block_out = lax.all_to_all(out_tok, "row", 1, 0, tiled=True)

    cot_split = cot_all.reshape(tokens, rows, width)
    dhidden = lax.dot_general(cot_split, down_all, (((1, 2), (0, 2)), ((), ())), preferred_element_type=F32)
    swish_grad = sigma * (1.0 + gate * (1.0 - sigma))
    dgate = (dhidden * up * swish_grad).astype(BF16)
    dup = (dhidden * swish).astype(BF16)
    dmid_all, gain2_grad = back_call(dgate, dup, gate_all, up_all, middle, cot_tok, gain2)
    dmid_all, gain2_grad = dmid_all.reshape(length, features), gain2_grad[0]

    dqkv, inner1 = attend_back_call(dmid_all, out_all_w, q, k, v, cosine, sine, segc, segr, qkv_cols)
    inner1 = lax.psum(inner1, "row") / (inv1 * features)
    dfirst = last_call(dqkv, qkv_all)
    own_x = activations.astype(F32)
    dmid_own = lax.dynamic_slice_in_dim(dmid_all, row * width, width, 1).astype(F32)
    input_grad = dmid_own + inv1 * first_gain[None] * dfirst - own_x * (inv1 * inv1 * inv1 * inner1)
    gain1_grad = lax.psum(jnp.sum(dfirst * own_x * inv1, axis=0), ("dp", "col"))
    gain2_grad = lax.psum(gain2_grad, ("dp", "row", "col"))
    gain2_grad = lax.dynamic_slice_in_dim(gain2_grad, row * width, width, 0)

    down_grad = lax.dot_general(hidden, cot_split, (((0,), (0,)), ((), ())), preferred_element_type=F32)
    down_grad = scatter_shared(down_grad.transpose(1, 0, 2).reshape(rows * hidden_cols, width))
    gate_grad = scatter_shared(dot(second_all, dgate, ((0,), (0,))))
    up_grad = scatter_shared(dot(second_all, dup, ((0,), (0,))))
    out_grad = swap(lax.psum(scatter(dot(attn, dmid_all, ((0,), (0,))), "col", 1), "dp")).astype(F32)
    qkv_grad = swap(lax.psum(scatter(dot(first, dqkv, ((0,), (0,))), "col"), "dp")).astype(F32)
    return (
        block_out,
        input_grad,
        gain1_grad,
        qkv_grad[:, :query_cols],
        qkv_grad[:, query_cols : query_cols + key_cols],
        qkv_grad[:, query_cols + key_span : query_cols + key_span + key_cols],
        out_grad,
        gain2_grad,
        gate_grad,
        up_grad,
        down_grad,
    )


def solution(mesh):
    tokens, block, swapped = P(("dp", "col"), "row"), P("row", "col"), P("col", "row")
    return jax.shard_map(
        local,
        mesh=mesh,
        in_specs=(
            tokens, P(("dp", "row")), P(("dp", "row")), P("row"), block, block, block, swapped,
            P("row"), block, block, swapped, tokens,
        ),
        out_specs=(tokens, tokens, P("row"), block, block, block, swapped, P("row"), block, block, swapped),
        check_vma=False,
    )
```

time: 1450 us -> 1090 us (0.75)
  waiting for transfers between devices: 793 us -> 215 us
  Pallas kernels: 0 us -> 525 us
  matrix products: 259 us -> 120 us
  blocking collectives: 235 us -> 138 us
  other arithmetic: 86.1 us -> 27.1 us
    pallas_call x0 -> x6, Pallas kernels: none -> 525 us  [the longest x1 154 us: middle_call(): pl.pallas_call(functools.partial(middle_kernel, rows_n, cols_n), out_shap...]
    all_gather x9 -> x4, waiting for transfers between devices: 250 us -> 0.01 us  [gather(): return lax.all_gather(values, axis_name, axis=axis, tiled=True)]
    reduce_scatter x9 -> x6, waiting for transfers between devices: 446 us -> 214 us  [scatter(): lax.psum_scatter(values.astype(BF16), axis_name, scatter_dimension=axis,...]
    all_gather x3, waiting for transfers between devices: 96.2 us -> 0.02 us  [gather_shared(): return lax.all_gather(part, ('row', 'dp'), axis=0, tiled=True)]
    all_gather x1 -> x0, blocking collectives: 91 us -> none  [gather(): return lax.all_gather(values, axis_name, axis=axis, tiled=True)]
    dot_general x6 -> x0, matrix products: 85.2 us -> none  [the longest x1 23.8 us: attend_back(): jnp.einsum('qhgd,shd->hgqs', out_grads, value_low, preferred_element_type...]
    psum x1, blocking collectives: 101 us -> 44.5 us  [local(): gain2_grad = lax.psum(gain2_grad, ('dp', 'row', 'col'))]
    dot_general x12 -> x6, matrix products: 124 us -> 71.1 us  [dot(): lax.dot_general(left, right, (dims, ((), ())), preferred_element_type=F32)]
  transfers between devices with their start and end apart: 27 -> 17, of which waited for: 14 -> 4; matrix products, arithmetic and copies ran while one was open for 21% -> 13% of each run, Pallas kernels for 0% -> 37%
where the time goes in v2:
time: 1090 us; the launch traced here: 1080 us
  Pallas kernels  525 us (48%)
  waiting for transfers between devices  215 us (20%)
  blocking collectives  138 us (13%)
  matrix products  120 us (11%)
  other arithmetic  27.1 us (2%)
  local copies, waits for them, and re-layouts  26 us (2%)
  starting transfers between devices  18 us (2%)
  between operations  14.7 us (1%)
    reduce_scatter x6, waiting for transfers between devices, scatter(): lax.psum_scatter(values.astype(BF16), axis_name, scatter_dimension=axis,...  214 us
    pallas_call x1, Pallas kernels, middle_call(): pl.pallas_call(functools.partial(middle_kernel, rows_n, cols_n), out_shap...  154 us
    pallas_call x1, Pallas kernels, first_call(): pl.pallas_call(functools.partial(first_kernel, size), out_shape=(jax.Shap...  136 us
    pallas_call x1, Pallas kernels, back_call(): pl.pallas_call(functools.partial(back_kernel, rows_n, cols_n), out_shape=...  121 us
    dot_general x6, matrix products, dot(): lax.dot_general(left, right, (dims, ((), ())), preferred_element_type=F32)  71.1 us
    psum x1, blocking collectives, local(): gain1_grad = lax.psum(jnp.sum(dfirst * own_x * inv1, axis=0), ('dp', 'col'))  66.9 us
    pallas_call x1, Pallas kernels, last_call(): pl.pallas_call(functools.partial(last_kernel, size), out_shape=jax.ShapeD...  45.6 us
    psum x1, blocking collectives, local(): gain2_grad = lax.psum(gain2_grad, ('dp', 'row', 'col'))  44.5 us
  transfers between devices with their start and end apart: 17, of which 4 were waited for; matrix products, arithmetic and copies ran while one was open for 13% of the time, Pallas kernels for 37%

profile of v2, /device:TPU:0, one launch (start us, length us, event | category | flops | bytes accessed | tf_op | source)
XLA Modules:
  0.0 1083.2 jit_solution(17182985547710274260)
XLA Ops:
  7.3 1.5 copy-done
  8.8 1.1 constant_dynamic-slice_fusion.2
  9.9 2.4 constant_dynamic-slice_fusion.1
  12.5 0.6 maximum_bitcast_fusion.small_ref
  13.1 0.9 pad_maximum_fusion.qkv_ref
  14.1 136.0 %shard_map.212 = (bf16[4,1024,512]{2,1,0:T(8,128)(2,1)}, bf16[1024,2048]{1,0:T(8,128)(2,1)}, f32[1024,1]{1,0:T(8,128)}, bf16[256,2048]{1,0:T(8,128)(2,1)}, f32[4...) custom-call(bf16[1024,512]{1,0:T(8,128)(2,1)} %act_ref.1, bf16[1024,512]{1,0:T(8,128)(2,1)} %cot_ref.1, ...), custom_call_target="tpu_custom_call" | custom-call | tf_op jit(solution)/shard_map/pallas_call | solution.py:367
  150.2 1.0 constant_dynamic-slice_fusion
  151.4 1.0 copy.35.segc_ref
  152.4 0.6 copy.47
  153.3 3.0 fusion.15
  156.3 27.1 %shard_map.213 = (bf16[8,1024,64]{2,1,0:T(8,128)(2,1)}, bf16[2,1024,64]{2,1,0:T(8,128)(2,1)}, bf16[2,1024,64]{2,1,0:T(8,128)(2,1)}, bf16[1024,512]{1,0:T(8,128)(2,1)}) custom-call(bf16[1024,2048]{1,0:T(8,128)(2,1)} %get-tuple-element.28.first_ref, bf16[2048,768]{1,0:T(8,128)(2,1)} %bitcast.67, f32[1024,128]{1,0:T(8,128)} %get-tuple-element.57.cos_ref, ...), custom_call_target="tpu_custom_call" | custom-call | tf_op jit(solution)/shard_map/pallas_call | solution.py:452
  183.3 154.5 %shard_map.214 = (f32[256,2048]{1,0:T(8,128)}, bf16[4,256,2048]{2,1,0:T(8,128)(2,1)}) custom-call(bf16[1024,512]{1,0:T(8,128)(2,1)} %get-tuple-element.31.attn_ref, bf16[4,512,512]{2,1,0:T(8,128)(2,1)} %get-tuple-element.32.weight_ref, bf16[4,1024,512]{2,1,0:T(8,128)(2,1)} %get-tuple-element.33.x_ref, f32[1,2048]{1,0:T(1,128)} %bitcast.82), custom_call_target="tpu_custom_call" | custom-call | tf_op jit(solution)/shard_map/pallas_call | solution.py:580
  337.9 14.6 %fusion.19 = f32[1024,2048]{1,0:T(8,128)} fusion(bf16[1024,2048]{1,0:T(8,128)(2,1)} %bitcast.90, bf16[2048,2048]{1,0:T(8,128)(2,1)} %all-gather.8.cloned.1.call-done.gate_ref), kind=kOutput, calls=%fused_computation.45 | convolution fusion | flops 8589934592 | bytes 20971520 | tf_op jit(solution)/shard_map/dot_general | solution.py:687
  352.4 14.7 %fusion.20 = f32[1024,2048]{1,0:T(8,128)} fusion(bf16[1024,2048]{1,0:T(8,128)(2,1)} %bitcast.91, bf16[2048,2048]{1,0:T(8,128)(2,1)} %all-gather.10.cloned.1.call-done.up_ref), kind=kOutput, calls=%fused_computation.46 | convolution fusion | flops 8589934592 | bytes 20971520 | tf_op jit(solution)/shard_map/dot_general | solution.py:687
  367.1 20.7 %fusion.2 = (bf16[1024,2048]{1,0:T(8,128)(2,1)}, bf16[1024,2048]{1,0:T(8,128)(2,1)}, bf16[1024,2048]{1,0:T(8,128)(2,1)}) fusion(f32[1024,2048]{1,0:T(8,128)} %fusion.19, f32[1024,2048]{1,0:T(8,128)} %fusion.20, bf16[4,2048,512]{2,1,0:T(8,128)(2,1)} %bitcast.68, bf16[128,4,8,512]{3,2,1,0:T(8,128)(2,1)} %bitcast.88), kind=kOutput, calls=%fused_computation.4 | convolution fusion | flops 8621391872 | bytes 41943040 | tf_op jit(solution)/shard_map/dot_general | solution.py:767
  387.8 120.7 %shard_map.215 = (bf16[4,256,2048]{2,1,0:T(8,128)(2,1)}, f32[1,2048]{1,0:T(1,128)}) custom-call(bf16[4,256,2048]{2,1,0:T(8,128)(2,1)} %bitcast.79, bf16[4,256,2048]{2,1,0:T(8,128)(2,1)} %bitcast.78, bf16[2048,2048]{1,0:T(8,128)(2,1)} %all-gather.8.cloned.1.call-done.gate_ref, bf16[2048,2048]{1,0:T(8,128)(2,1)} %all-gather.10.cloned.1.call-done.up_ref, ...), custom_call_target="tpu_custom_call" | custom-call | tf_op jit(solution)/shard_map/pallas_call | solution.py:640
  508.5 5.9 convolution_convert_fusion.5
  514.7 41.2 %shard_map.216 = (bf16[1024,768]{1,0:T(8,128)(2,1)}, f32[1024,1]{1,0:T(8,128)}) custom-call(bf16[1024,2048]{1,0:T(8,128)(2,1)} %bitcast.73, bf16[4,512,512]{2,1,0:T(8,128)(2,1)} %get-tuple-element.32.weight_ref, bf16[8,1024,64]{2,1,0:T(8,128)(2,1)} %get-tuple-element.39.q_ref, bf16[2,1024,64]{2,1,0:T(8,128)(2,1)} %get-tuple-element.40.k_ref, ...), custom_call_target="tpu_custom_call" | custom-call | tf_op jit(solution)/shard_map/pallas_call | solution.py:534
  555.9 7.8 convolution_convert_fusion.4
  564.0 14.0 %convolution_convert_fusion.1 = bf16[2048,2048]{1,0:T(8,128)(2,1)} fusion(bf16[1024,2048]{1,0:T(8,128)(2,1)} %bitcast.92, bf16[1024,2048]{1,0:T(8,128)(2,1)} %get-tuple-element.50), kind=kOutput, calls=%fused_computation.9 | convolution fusion | flops 8594128896 | bytes 16777216 | tf_op jit(solution)/shard_map/dot_general | solution.py:687
  578.1 14.1 %convolution_convert_fusion = bf16[2048,2048]{1,0:T(8,128)(2,1)} fusion(bf16[1024,2048]{1,0:T(8,128)(2,1)} %bitcast.93, bf16[1024,2048]{1,0:T(8,128)(2,1)} %get-tuple-element.49), kind=kOutput, calls=%fused_computation.8 | convolution fusion | flops 8594128896 | bytes 16777216 | tf_op jit(solution)/shard_map/dot_general | solution.py:687
  592.2 0.3 reduce-scatter.17.cloned.1.call-start
  592.5 14.2 %convolution_convert_fusion.2 = bf16[2048,4,512]{2,0,1:T(8,128)(2,1)} fusion(bf16[1024,2048]{1,0:T(8,128)(2,1)} %get-tuple-element.51, bf16[128,4,8,512]{3,2,1,0:T(8,128)(2,1)} %bitcast.89), kind=kOutput, calls=%fused_computation.10 | convolution fusion | flops 8594128896 | bytes 16777216 | tf_op jit(solution)/shard_map/dot_general | solution.py:784
  606.8 11.5 %copy.36 = bf16[4,512,2048]{2,1,0:T(8,128)(2,1)} copy(bf16[4,512,2048]{1,2,0:T(8,128)(2,1)} %bitcast.69) | data formatting | bytes 16777216 | tf_op jit(solution)/shard_map/dot_general | solution.py:762
  618.3 3.3 reduce-scatter.9.cloned.1.call-done
  621.7 13.9 %convolution_convert_fusion.3 = bf16[1024,2048]{1,0:T(8,128)(2,1)} fusion(bf16[1024,2048]{1,0:T(8,128)(2,1)} %get-tuple-element.51, bf16[2048,2048]{1,0:T(8,128)(2,1)} %bitcast.71), kind=kOutput, calls=%fused_computation.15 | convolution fusion | flops 8592031744 | bytes 16777216 | tf_op jit(solution)/shard_map/dot_general | solution.py:762
  635.6 61.2 %reduce-scatter.13.cloned.1.call-done = bf16[256,2048]{1,0:T(8,128)(2,1)} async-done(((bf16[2048,2048]{1,0:T(8,128)(2,1)}), bf16[256,2048]{1,0:T(8,128)(2,1)}) %reduce-scatter.13.cloned.1.call-update) | async-done | bytes 1048592 | tf_op jit(solution)/shard_map/reduce_scatter | solution.py:703
  696.9 74.7 %reduce-scatter.15.cloned.1.call-done = bf16[256,2048]{1,0:T(8,128)(2,1)} async-done(((bf16[2048,2048]{1,0:T(8,128)(2,1)}), bf16[256,2048]{1,0:T(8,128)(2,1)}) %reduce-scatter.15.cloned.1.call-update) | async-done | bytes 1048592 | tf_op jit(solution)/shard_map/reduce_scatter | solution.py:703
  771.7 75.1 %reduce-scatter.17.cloned.1.call-done = bf16[1024,512]{1,0:T(8,128)(2,1)} async-done(((bf16[8192,512]{1,0:T(8,128)(2,1)}), bf16[1024,512]{1,0:T(8,128)(2,1)}) %reduce-scatter.17.cloned.1.call-update) | async-done | bytes 1048592 | tf_op jit(solution)/shard_map/reduce_scatter | solution.py:703
  846.8 45.6 %shard_map.217 = f32[1024,512]{1,0:T(8,128)} custom-call(bf16[1024,768]{1,0:T(8,128)(2,1)} %get-tuple-element.42.dqkv_ref, bf16[4,512,768]{2,1,0:T(8,128)(2,1)} %get-tuple-element.29.weight_ref), custom_call_target="tpu_custom_call" | custom-call | tf_op jit(solution)/shard_map/pallas_call | solution.py:675
  892.4 44.5 %psum.39 = f32[2048]{0:T(1024)S(1)} all-reduce(f32[2048]{0:T(1024)S(1)} %bitcast.87), channel_id=1, replica_groups=mesh['dp'=2,'row'=4,'col'=4] {'dp','row','col'}, use_global_device_ids=true, to_apply=%region_8.0 | all-reduce | flops 2048 | bytes 16384 | tf_op jit(solution)/shard_map/psum | solution.py:781
  936.9 0.7 dynamic_slice.23
  937.5 26.5 %psum.35 = f32[1024,1]{1,0:T(8,128)} all-reduce(f32[1024,1]{1,0:T(8,128)S(1)} %copy-done.6), channel_id=1, replica_groups=mesh['dp'=2,'row'=4,'col'=4] {'row'}, use_global_device_ids=true, to_apply=%region_1.0 | all-reduce | flops 1024 | bytes 8192 | tf_op jit(solution)/shard_map/psum | solution.py:775
  964.1 7.4 collective-permute-start
  971.5 5.6 collective-permute-start.1
  977.1 2.1 add_convert_fusion
  979.3 1.1 copy.60
  980.3 3.8 all-to-all-start
  984.1 1.6 fusion.17
  985.8 3.9 fusion.12
  989.7 66.9 %psum.36 = f32[512]{0:T(512)} all-reduce(f32[512]{0:T(512)S(1)} %get-tuple-element.52), channel_id=1, replica_groups=mesh['dp'=2,'row'=4,'col'=4] {'dp','col'}, use_global_device_ids=true, to_apply=%region_3.0 | all-reduce | flops 512 | bytes 4096 | tf_op jit(solution)/shard_map/psum | solution.py:780
  1056.5 2.1 convert_element_type.87
  1058.7 2.1 slice.27
  1060.8 1.8 fusion.18
  1062.6 4.1 convert_element_type.89
  1066.8 4.3 convert_element_type.91
  1071.0 4.2 convert_element_type.95
  1075.2 1.0 copy.65
  (80 shorter events, 1.6 us)
Async XLA Ops:
  7.2 1.6 copy-start
  7.2 5.3 copy-start.14
  7.2 5.3 copy-start.15
  7.2 5.3 copy-start.16
  7.2 5.3 copy-start.11
  7.2 5.9 copy-start.7
  7.2 5.9 copy-start.8
  7.3 5.9 copy-start.4
  7.3 330.6 %all-gather.8.cloned.1.call-start = ((), (), s32[]{:S(2)}) async-start(), calls=%async_computation.7 | async-start | bytes 9437184 | tf_op jit(solution)/shard_map/all_gather | solution.py:714
  9.9 140.3 %copy-start.5 = (bf16[2048,512]{1,0:T(8,128)(2,1)S(1)}, bf16[2048,512]{1,0:T(8,128)(2,1)}, u32[]{:S(2)}) copy-start(bf16[2048,512]{1,0:T(8,128)(2,1)} %param.24) | copy-start | bytes 6291460
  9.9 342.5 %all-gather.10.cloned.1.call-start = ((), (), s32[]{:S(2)}) async-start(), calls=%async_computation.8 | async-start | bytes 9437184 | tf_op jit(solution)/shard_map/all_gather | solution.py:714
  12.4 354.7 %all-gather.14.cloned.1.call-start = ((), (), s32[]{:S(2)}) async-start(), calls=%async_computation.11 | async-start | bytes 5242880 | tf_op jit(solution)/shard_map/all_gather | solution.py:699
  150.1 1.2 copy-start.10
  150.1 217.0 %all-gather.12.cloned.1.call-start = ((), (), s32[]{:S(2)}) async-start(), calls=%async_computation.9 | async-start | bytes 9437184 | tf_op jit(solution)/shard_map/all_gather | solution.py:714
  151.2 467.1 %reduce-scatter.11.cloned.1.call-start = ((), (), s32[]{:S(2)}) async-start(), calls=%async_computation.13 | async-start | bytes 2621440 | tf_op jit(solution)/shard_map/reduce_scatter | solution.py:703
  151.4 4.8 copy-start.9
  387.8 120.7 %copy-start.3 = (bf16[1024,512]{1,0:T(8,128)(2,1)S(1)}, bf16[1024,512]{1,0:T(8,128)(2,1)}, u32[]{:S(2)}) copy-start(bf16[1024,512]{1,0:T(8,128)(2,1)} %get-tuple-element.31.attn_ref) | copy-start | bytes 3145732
  514.5 107.1 %reduce-scatter.9.cloned.1.call-start = ((), (), s32[]{:S(2)}) async-start(), calls=%async_computation.12 | async-start | bytes 3932160 | tf_op jit(solution)/shard_map/reduce_scatter | solution.py:703
  563.8 133.0 %reduce-scatter.13.cloned.1.call-start = ((), (), s32[]{:S(2)}) async-start(), calls=%async_computation.14 | async-start | bytes 9437184 | tf_op jit(solution)/shard_map/reduce_scatter | solution.py:703
  578.0 193.5 %reduce-scatter.15.cloned.1.call-start = ((), (), s32[]{:S(2)}) async-start(), calls=%async_computation.16 | async-start | bytes 9437184 | tf_op jit(solution)/shard_map/reduce_scatter | solution.py:703
  592.2 254.6 %reduce-scatter.17.cloned.1.call-start = ((), (), s32[]{:S(2)}) async-start(), calls=%async_computation.18 | async-start | bytes 9437184 | tf_op jit(solution)/shard_map/reduce_scatter | solution.py:703
  606.7 357.4 %all-reduce.3.cloned.1.call-start = ((), (), s32[]{:S(2)}) async-start(), calls=%async_computation.20 | async-start | bytes 2621440 | tf_op jit(solution)/shard_map/psum | solution.py:789
  621.6 355.5 %reduce-scatter.7.cloned.1.call-start = ((), (), s32[]{:S(2)}) async-start(), calls=%async_computation.10 | async-start | bytes 5242880 | tf_op jit(solution)/shard_map/reduce_scatter | solution.py:703
  635.6 427.1 %all-gather.16.cloned.1.call-start = ((), (), s32[]{:S(2)}) async-start(), calls=%async_computation.15 | async-start | bytes 3145728 | tf_op jit(solution)/shard_map/all_gather | solution.py:699
  696.8 369.9 %all-gather.18.cloned.1.call-start = ((), (), s32[]{:S(2)}) async-start(), calls=%async_computation.17 | async-start | bytes 3145728 | tf_op jit(solution)/shard_map/all_gather | solution.py:699
  771.6 120.8 %copy-start.13 = (f32[1,2048]{1,0:T(1,128)S(1)}, f32[1,2048]{1,0:T(1,128)}, u32[]{:S(2)}) copy-start(f32[1,2048]{1,0:T(1,128)} %get-tuple-element.44) | copy-start | bytes 24580
  771.6 165.9 %copy-start.6 = (f32[1024,1]{1,0:T(8,128)S(1)}, f32[1024,1]{1,0:T(8,128)}, u32[]{:S(2)}) copy-start(f32[1024,1]{1,0:T(8,128)} %get-tuple-element.43) | copy-start | bytes 12292
  771.6 299.4 %all-gather.20.cloned.1.call-start = ((), (), s32[]{:S(2)}) async-start(), calls=%async_computation.19 | async-start | bytes 3145728 | tf_op jit(solution)/shard_map/all_gather | solution.py:699
  964.1 94.6 %collective-permute-start = (bf16[512,768]{1,0:T(8,128)(2,1)}, bf16[512,768]{1,0:T(8,128)(2,1)}, u32[]{:S(2)}, u32[]{:S(2)}) collective-permute-start(bf16[512,768]{1,0:T(8,128)(2,1)} %get-tuple-element.47), channel_id=1, source_target_pairs={{0,0},{1,4},{2,8},{3,12},{4,1},{5,5},{6,9},{7,13},{8,2},{9,6},{10,... | collective-permute-start | bytes 2359304 | tf_op jit(solution)/shard_map/ppermute | solution.py:708
  971.5 14.3 %copy-start.2 = (f32[1024,512]{1,0:T(8,128)S(1)}, f32[1024,512]{1,0:T(8,128)}, u32[]{:S(2)}) copy-start(f32[1024,512]{1,0:T(8,128)} %shard_map.217) | copy-start | bytes 6291460
  971.5 14.3 %copy-start.12 = (f32[512]{0:T(512)S(1)}, f32[512]{0:T(512)}, u32[]{:S(2)}) copy-start(f32[512]{0:T(512)} %param.16) | copy-start | bytes 6148
  971.5 85.0 %collective-permute-start.1 = (bf16[512,512]{1,0:T(8,128)(2,1)}, bf16[512,512]{1,0:T(8,128)(2,1)}, u32[]{:S(2)}, u32[]{:S(2)}) collective-permute-start(bf16[512,512]{1,0:T(8,128)(2,1)} %get-tuple-element.48), channel_id=1, source_target_pairs={{0,0},{1,4},{2,8},{3,12},{4,1},{5,5},{6,9},{7,13},{8,2},{9,6},{10,... | collective-permute-start | bytes 1572872 | tf_op jit(solution)/shard_map/ppermute | solution.py:708
  980.3 82.3 %all-to-all-start = ((bf16[256,4,512]{2,0,1:T(8,128)(2,1)}), bf16[256,4,512]{2,0,1:T(8,128)(2,1)S(1)}, u32[]{:S(2)}, u32[]{:S(2)}) async-start(bf16[256,4,512]{2,0,1:T(8,128)(2,1)} %bitcast.76), calls=%async_computation.1 | async-start | bytes 2097152 | tf_op jit(solution)/shard_map/all_to_all | solution.py:764
  1066.8 9.5 copy-start.1
Sparse Core Ops, SparseCore 0:
  10.6 97.0 all-gather.7
  110.1 73.5 all-gather.9
  185.3 98.4 all-gather.13
  286.1 57.4 all-gather.11
  514.6 41.2 reduce-scatter.10
  563.9 57.6 reduce-scatter.8
  625.5 71.3 reduce-scatter.12
  700.3 71.2 reduce-scatter.14
  775.4 71.2 reduce-scatter.16
  849.0 20.0 all-reduce.2
  872.1 78.9 reduce-scatter.6
  952.5 10.9 all-gather.15
  965.1 11.7 all-gather.17
  978.3 11.7 all-gather.19

commit v3 on v2

v3 whole, which is shorter than its diff:
```python
import functools

import jax
import jax.numpy as jnp
from jax import lax
from jax.experimental import pallas as pl
from jax.experimental.pallas import tpu as pltpu
from jax.sharding import PartitionSpec as P

HEAD = 64
EPSILON = 1e-05
THETA = 500000.0
F32 = jnp.float32
BF16 = jnp.bfloat16


MESH = pl.DeviceIdType.MESH
VMEM_LIMIT = 60 * 1024 * 1024


def greet(row_size=0, col_size=0, dp_size=0):
    barrier = pltpu.get_barrier_semaphore()
    if row_size:
        row = lax.axis_index("row")
        for mask in range(1, row_size):
            pl.semaphore_signal(barrier, inc=1, device_id={"row": row ^ mask}, device_id_type=MESH)
    if col_size:
        col = lax.axis_index("col")

        @pl.when(col > 0)
        def _():
            pl.semaphore_signal(barrier, inc=1, device_id={"col": col - 1}, device_id_type=MESH)

        @pl.when(col < col_size - 1)
        def _():
            pl.semaphore_signal(barrier, inc=1, device_id={"col": col + 1}, device_id_type=MESH)

    if dp_size:
        pl.semaphore_signal(barrier, inc=1, device_id={"dp": 1 - lax.axis_index("dp")}, device_id_type=MESH)
    count = max(row_size - 1, 0) + (1 if dp_size else 0)
    if col_size:
        count = count + jnp.where(col > 0, 1, 0) + jnp.where(col < col_size - 1, 1, 0)
    pl.semaphore_wait(barrier, count)


def remote(src, dst, sends, recvs, place, device):
    return pltpu.make_async_remote_copy(
        src_ref=src, dst_ref=dst, send_sem=sends.at[place], recv_sem=recvs.at[place],
        device_id=device, device_id_type=MESH,
    )


class RowGather:
    def __init__(self, size, ref, sends, recvs, begin=0, count=None, first=0):
        self.size, self.ref, self.sends, self.recvs = size, ref, sends, recvs
        self.bits = size.bit_length() - 1
        self.row = lax.axis_index("row")
        self.begin, self.first = begin, first
        self.half = (count or ref.shape[1]) // 2
        self.all = [self.copies(step) for step in range(self.bits)]

    def rows(self, part):
        return pl.ds(pl.multiple_of(self.begin + part * self.half, 16), self.half)

    def order(self, part):
        return list(range(self.bits)) if part == 0 else list(range(self.bits))[::-1]

    def copies(self, step):
        out = []
        for part in range(2):
            order = self.order(part)
            for item in range(1 << step):
                mask = 0
                for j in range(step):
                    if item >> j & 1:
                        mask |= 1 << order[j]
                piece = self.ref.at[self.row ^ mask, self.rows(part)]
                place = self.first + part * (self.size - 1) + (1 << step) - 1 + item
                out.append(remote(piece, piece, self.sends, self.recvs, place, {"row": self.row ^ (1 << order[step])}))
        return out

    def start(self):
        for step in range(self.bits):
            for part in range(2):
                self.all[step][part << step].start()

    def event(self, step, seen=None):
        for part in range(2):
            order = self.order(part)
            for item in range(1 << step):
                self.all[step][(part << step) + item].wait_recv()
                got = item | 1 << step
                for later in range(step + 1, self.bits):
                    self.all[later][(part << later) + got].start()
                if seen is not None:
                    mask = 0
                    for j in range(step + 1):
                        if got >> j & 1:
                            mask |= 1 << order[j]
                    seen(mask, part)

    def finish(self):
        for step in range(self.bits):
            for copy in self.all[step]:
                copy.wait_send()

    def run(self):
        for step in range(self.bits):
            self.event(step)
        self.finish()


class SharedGather:
    def __init__(self, size, shard, full, copied, sends, recvs, score, rcore, first):
        self.core, self.row = lax.axis_index("dp"), lax.axis_index("row")
        self.size, self.full, self.score, self.rcore, self.first = size, full, score, rcore, first * 2 * (size - 1)
        share = full.shape[1] // 2
        self.own = pltpu.make_async_copy(shard, full.at[self.row], copied.at[first])
        self.gather = RowGather(size, full, sends, recvs, self.core * share, share, self.first)

    def across(self, mask, part):
        piece = self.full.at[self.row ^ mask, self.gather.rows(part)]
        return remote(piece, piece, self.score, self.rcore, self.first + part * (self.size - 1) + mask - 1, {"dp": 1 - self.core})

    def load(self):
        self.own.start()

    def start(self):
        self.own.wait()
        self.gather.start()

    def event(self, step):
        self.gather.event(step, lambda mask, part: self.across(mask, part).start())

    def finish(self):
        self.gather.finish()
        for mask in range(1, self.size):
            for part in range(2):
                self.across(mask, part).wait()

    @staticmethod
    def scratch(size, count):
        dma = pltpu.SemaphoreType.DMA
        return [dma((count,))] + [dma((count * 2 * (size - 1),))] * 4


class RowScatter:
    def __init__(self, size, part_ref, recv_ref, sends, recvs):
        self.size, self.part, self.recv = size, part_ref, recv_ref
        self.bits = size.bit_length() - 1
        self.row = lax.axis_index("row")
        half = part_ref.shape[1] // 2
        self.rows = [pl.ds(part * half, half) for part in range(2)]
        self.plans = []
        for part in range(2):
            order = self.order(part)
            steps = []
            for step in range(self.bits):
                bit, rest = 1 << order[step], order[step + 1 :]
                count = 1 << len(rest)
                copies = []
                for item in range(count - 1, -1, -1):
                    mask = sum(1 << other for j, other in enumerate(rest) if item >> j & 1)
                    place = size - 2 * count + item
                    copies.append((
                        item, mask, place,
                        remote(
                            part_ref.at[self.row ^ mask ^ bit, self.rows[part]], recv_ref.at[place, self.rows[part]],
                            sends, recvs, part * (size - 1) + place, {"row": self.row ^ bit},
                        ),
                    ))
                steps.append(copies)
            self.plans.append(steps)

    def order(self, part):
        return list(range(self.bits)) if part == 0 else list(range(self.bits))[::-1]

    def start(self):
        for part in range(2):
            for _, _, _, copy in self.plans[part][0]:
                copy.start()

    def event(self, step, finish):
        last = step + 1 == self.bits
        for part in range(2):
            rows = self.rows[part]
            for item, mask, place, copy in self.plans[part][step]:
                copy.wait_recv()
                total = self.part[self.row ^ mask, rows].astype(F32) + self.recv[place, rows].astype(F32)
                if last:
                    finish(rows, total)
                    continue
                self.part[self.row ^ mask, rows] = total.astype(BF16)
                for _, mask2, _, copy2 in self.plans[part][step + 1]:
                    if mask2 ^ 1 << self.order(part)[step + 1] == mask:
                        copy2.start()

    def close(self):
        for part in range(2):
            for step in self.plans[part]:
                for _, _, _, copy in step:
                    copy.wait_send()

    def run(self, finish):
        self.start()
        for step in range(self.bits):
            self.event(step, finish)
        self.close()


class ColGather:
    def __init__(self, size, ref, sends, recvs, begin=0, end=None):
        self.size, self.ref, self.sends, self.recvs = size, ref, sends, recvs
        self.begin, self.end = begin, size - 1 if end is None else end
        self.col = lax.axis_index("col")

    def sides(self, step):
        size, col = self.size, self.col
        return (
            (0, lax.rem(col - step + size, size), col >= step, col < size - 1),
            (1, lax.rem(col + step, size), col + step < size, col > 0),
        )

    def copy(self, side, step):
        size, col = self.size, self.col
        piece = self.ref.at[self.sides(step)[side][1]]
        target = lax.rem(col + (1 if side == 0 else size - 1), size)
        return remote(piece, piece, self.sends, self.recvs, side * (size - 1) + step, {"col": target})

    def event(self, step, seen=None):
        for side, place, has, goes in self.sides(step):
            if step > self.begin:

                @pl.when(has)
                def _():
                    self.copy(side, step - 1).wait_recv()

            if step < self.end:

                @pl.when(has & goes)
                def _():
                    self.copy(side, step).start()

            if seen is not None and (step or side == 0):

                @pl.when(has)
                def _():
                    seen(place)

    def finish(self):
        for step in range(self.begin, self.end):
            for side, place, has, goes in self.sides(step):

                @pl.when(has & goes)
                def _():
                    self.copy(side, step).wait_send()

    def run(self):
        for step in range(self.begin, self.end + 1):
            self.event(step)
        self.finish()


class ColScatter:
    def __init__(self, size, part, recv, sends, recvs):
        self.size, self.part, self.recv, self.sends, self.recvs = size, part, recv, sends, recvs
        self.col = lax.axis_index("col")
        self.times = 2 * size - 1

    def copy(self, side, target, source):
        step = 1 if side == 0 else self.size - 1
        return pltpu.make_async_remote_copy(
            src_ref=source.at[target], dst_ref=self.recv.at[side, target], send_sem=self.sends.at[side],
            recv_sem=self.recvs.at[side * self.size + target],
            device_id={"col": lax.rem(self.col + step, self.size)}, device_id_type=MESH,
        )

    def event(self, time, prepare=None):
        size, col = self.size, self.col
        for side, first, step in ((0, col == 0, time - col), (1, col == size - 1, time - (size - 1 - col))):
            target = size - 1 - step if side == 0 else step
            valid = (step >= 0) & ((target >= col) if side == 0 else (target <= col))
            place = lax.rem(target + 4 * size, size)

            if prepare is not None:

                @pl.when(valid & ((target != col) | (side == 0)))
                def _():
                    prepare(place)

            @pl.when(valid & jnp.logical_not(first))
            def _():
                self.copy(side, place, self.part).wait_recv()

            @pl.when(valid & jnp.logical_not(first) & (target != col))
            def _():
                self.recv[side, place] = (self.recv[side, place].astype(F32) + self.part[place].astype(F32)).astype(BF16)

            @pl.when(valid & (step > 0))
            def _():
                self.copy(side, place, self.part).wait_send()

            @pl.when(valid & (target != col) & first)
            def _():
                self.copy(side, place, self.part).start()

            @pl.when(valid & (target != col) & jnp.logical_not(first))
            def _():
                self.copy(side, place, self.recv.at[side]).start()

    def total(self, rows):
        got = self.part[self.col, rows].astype(F32)
        got += jnp.where(self.col > 0, self.recv[0, self.col, rows].astype(F32), 0.0)
        got += jnp.where(self.col < self.size - 1, self.recv[1, self.col, rows].astype(F32), 0.0)
        return got


VM = pl.BlockSpec(memory_space=pltpu.VMEM)


def params(ident):
    return pltpu.CompilerParams(collective_id=ident, has_side_effects=True, vmem_limit_bytes=VMEM_LIMIT)


def keep_near(size, line, near, step):
    col = lax.axis_index("col")
    for side, place, has in ((0, col - step, col >= step), (1, col + step, col + step < size)):

        @pl.when(has)
        def _():
            near[side] = line[lax.rem(place + size, size)]


def take_near(size, line, near, step):
    col = lax.axis_index("col")
    for side, place, has in ((0, col - step, col >= step), (1, col + step, col + step < size)):

        @pl.when(has)
        def _():
            line[lax.rem(place + size, size)] = near[side]


def first_kernel(
    size, act_ref, cot_ref, small_ref, qkv_ref, out_ref,
    x_ref, first_ref, inv_ref, tok_ref, smalls_ref, qkvs_ref, outs_ref,
    near_ref,
    got_ref, zq_ref, zo_ref, zc_ref, s1, r1, s2, r2, s3, r3, szq, rzq, szo, rzo, srow, rrow, score, rcore, szc, rzc,
):
    row, col, core = lax.axis_index("row"), lax.axis_index("col"), lax.axis_index("dp")
    length, width = act_ref.shape
    quarter = length // size
    small_rows = small_ref.shape[0]
    gain_row = 2 * length // 128
    x_ref[row] = act_ref[...]
    smalls_ref[row] = small_ref[...]
    blocks = ((qkv_ref, zq_ref, qkvs_ref, szq, rzq), (out_ref, zo_ref, outs_ref, szo, rzo))
    for block, line, _, _, _ in blocks:
        share = block.shape[0] // 2
        line[col] = block[pl.ds(pl.multiple_of(core * share, 16), share)]
    greet(row_size=size, col_size=size, dp_size=2)
    gather = RowGather(size, x_ref, s1, r1)
    smalls = [
        remote(small_ref, smalls_ref.at[row], s3, r3, mask - 1, {"row": row ^ mask}) for mask in range(1, size)
    ]
    lines = [ColGather(size, line, sends, recvs) for _, line, _, sends, recvs in blocks]
    lines[0].event(0)
    for move in smalls:
        move.start()
    gather.start()
    moves = [
        remote(cot_ref.at[pl.ds((row ^ mask) * quarter, quarter)], got_ref.at[row], s2, r2, mask - 1, {"row": row ^ mask})
        for mask in range(1, size)
    ]
    got_ref[row] = cot_ref[pl.ds(pl.multiple_of(row * quarter, 16), quarter)]

    def half(ref, place):
        share = ref.shape[1] // 2
        return ref.at[place, pl.ds(pl.multiple_of(core * share, 16), share)]

    def hand(which, mask):
        _, line, full, _, _ = blocks[which]
        return remote(line.at[row ^ mask], half(full, row), srow, rrow, which * (size - 1) + mask - 1, {"row": row ^ mask})

    def across(which, mask):
        full = blocks[which][2]
        piece = half(full, row ^ mask)
        return remote(piece, piece, score, rcore, which * size + mask, {"dp": 1 - core})

    def seen(which):
        def act(place):
            _, line, full, _, _ = blocks[which]

            @pl.when(place == row)
            def _():
                share = full.shape[1] // 2
                full[row, pl.ds(pl.multiple_of(core * share, 16), share)] = line[row]
                across(which, 0).start()

            for mask in range(1, size):

                @pl.when(place == row ^ mask)
                def _():
                    hand(which, mask).start()

        return act

    act = seen(0)
    act(col)
    for step in range(1, size - 1):
        lines[0].event(step, act)
    gather.event(0)
    lines[0].event(size - 1, act)
    lines[1].event(0)
    for move in moves:
        move.start()
    for step in range(1, gather.bits):
        gather.event(step)
    for move in smalls:
        move.wait()

    @pl.loop(0, length // 128)
    def _(i):
        rows = pl.ds(pl.multiple_of(i * 128, 128), 128)
        total = jnp.zeros((128, 1), F32)
        for j in range(size):
            value = x_ref[j, rows].astype(F32)
            total += jnp.sum(value * value, axis=1, keepdims=True)
        inverse = lax.rsqrt(total / (size * width) + EPSILON)
        inv_ref[rows] = inverse
        for j in range(size):
            for k in range(width // 128):
                gain = smalls_ref[j, gain_row + k : gain_row + k + 1]
                value = x_ref[j, rows, k * 128 : (k + 1) * 128].astype(F32)
                first_ref[rows, j * width + k * 128 : j * width + (k + 1) * 128] = (value * inverse * gain).astype(BF16)

    for mask in range(1, size):
        hand(0, mask).wait_recv()
        across(0, mask).start()
    act = seen(1)
    act(col)
    lines[1].event(1, act)
    for move in moves:
        move.wait()
    for j in range(size):
        zc_ref[col, :, j * width : (j + 1) * width] = got_ref[j]
    tok_ref[...] = zc_ref[col]
    near = ColGather(size, zc_ref, szc, rzc, 0, 1)
    near.event(0)
    for step in range(2, size):
        lines[1].event(step, act)
    for mask in range(1, size):
        hand(1, mask).wait_recv()
        across(1, mask).start()
    near.event(1)
    keep_near(size, zc_ref, near_ref, 1)
    near.finish()
    gather.finish()
    for line in lines:
        line.finish()
    for which in range(2):
        for mask in range(1, size):
            hand(which, mask).wait_send()
        for mask in range(size):
            across(which, mask).wait()


def first_call(activations, cotangent, small, qkv_weight, out_weight):
    size = lax.axis_size("row")
    length, width = activations.shape
    quarter = length // size
    qkv_cols, heads_cols = qkv_weight.shape[1], out_weight.shape[0]
    dma = pltpu.SemaphoreType.DMA
    return pl.pallas_call(
        functools.partial(first_kernel, size),
        out_shape=(
            jax.ShapeDtypeStruct((size, length, width), BF16),
            jax.ShapeDtypeStruct((length, size * width), BF16),
            jax.ShapeDtypeStruct((length, 1), F32),
            jax.ShapeDtypeStruct((quarter, size * width), BF16),
            jax.ShapeDtypeStruct((size,) + small.shape, F32),
            jax.ShapeDtypeStruct((size,) + qkv_weight.shape, BF16),
            jax.ShapeDtypeStruct((size,) + out_weight.shape, BF16),
            jax.ShapeDtypeStruct((2, quarter, size * width), BF16),
        ),
        in_specs=[VM] * 5,
        out_specs=(VM,) * 8,
        scratch_shapes=[
            pltpu.VMEM((size, quarter, width), BF16),
            pltpu.VMEM((size, width // 2, qkv_cols), BF16),
            pltpu.VMEM((size, heads_cols // 2, width), BF16),
            pltpu.VMEM((size, quarter, size * width), BF16),
        ]
        + [dma((2 * (size - 1),))] * 2
        + [dma((size - 1,))] * 4
        + [dma((2 * (size - 1),))] * 4
        + [dma((2 * (size - 1),))] * 2
        + [dma((2 * size,))] * 2
        + [dma((2 * (size - 1),))] * 2,
        compiler_params=params(1),
    )(activations, cotangent, small, qkv_weight, out_weight)


def turn(values, low):
    return jnp.where(low, -pltpu.roll(values, 128 - HEAD // 2, 1), pltpu.roll(values, HEAD // 2, 1))


def low_columns(rows):
    return lax.broadcasted_iota(jnp.int32, (rows, 128), 1) % HEAD < HEAD // 2


def masked_scores(query, key, seg_col, seg_row, first_row):
    scores = lax.dot_general(query, key, (((1,), (1,)), ((), ())), preferred_element_type=F32)
    rows = lax.broadcasted_iota(jnp.int32, scores.shape, 0) + first_row
    columns = lax.broadcasted_iota(jnp.int32, scores.shape, 1)
    allowed = (seg_col == seg_row) & (rows >= columns)
    return jnp.where(allowed, scores, -1e30)


def attend_kernel(
    size, first_ref, weight_ref, cos_ref, sin_ref, segc_ref, segr_ref, near_ref, gate_ref,
    q_ref, k_ref, v_ref, o_ref, next_ref, gates_ref, oh_ref, zc_ref, szc, rzc, *shared,
):
    bulk = SharedGather(size, gate_ref, gates_ref, *shared, 0)
    bulk.load()
    take_near(size, zc_ref, near_ref, 1)
    greet(row_size=size, col_size=size, dp_size=2)
    bulk.start()
    line = ColGather(size, zc_ref, szc, rzc, 1, 2)
    line.event(1)
    heads, length, _ = q_ref.shape
    kvs = k_ref.shape[0]
    group = heads // kvs
    query_cols = heads * HEAD
    key_cols = (weight_ref.shape[1] - query_cols) // 2
    block = 256

    @pl.loop(0, length // block)
    def _(i):
        rows = pl.ds(pl.multiple_of(i * block, block), block)
        low = low_columns(block)
        cosine, sine = cos_ref[rows], sin_ref[rows]
        whole = jnp.dot(first_ref[rows], weight_ref[...], preferred_element_type=F32)
        for ref, count, start, factor in ((q_ref, heads, 0, HEAD ** (-0.5)), (k_ref, kvs, query_cols, 1.0)):
            for j in range((count + 1) // 2):
                part = whole[:, start + 128 * j : start + 128 * (j + 1)]
                part = ((part * cosine + turn(part, low) * sine) * factor).astype(BF16)
                for side in range(min(2, count - 2 * j)):
                    ref[2 * j + side, rows] = part[:, side * HEAD : (side + 1) * HEAD]
        for j in range(kvs):
            at = query_cols + key_cols + j * HEAD
            v_ref[j, rows] = whole[:, at : at + HEAD].astype(BF16)

    @pl.loop(0, heads)
    def _(head):
        kv = lax.div(head, group)
        for i in range(length // block):
            rows, extent = slice(i * block, (i + 1) * block), (i + 1) * block
            scores = masked_scores(q_ref[head, rows], k_ref[kv, :extent], segc_ref[rows], segr_ref[:, :extent], i * block)
            top = jnp.max(scores, axis=1, keepdims=True)
            weights = jnp.exp(scores - top)
            total = jnp.sum(weights, axis=1, keepdims=True)
            mixed = jnp.dot(weights.astype(BF16), v_ref[kv, :extent], preferred_element_type=F32)
            oh_ref[head, rows] = (mixed / total).astype(BF16)

    for head in range(heads):
        o_ref[:, head * HEAD : (head + 1) * HEAD] = oh_ref[head]
    for step in range(bulk.gather.bits):
        bulk.event(step)
    line.event(2)
    keep_near(size, zc_ref, next_ref, 2)
    line.finish()
    bulk.finish()


def attend_call(first, weight, cosine, sine, segc, segr, near, gate, heads, kvs):
    size = lax.axis_size("row")
    length = first.shape[0]
    dma = pltpu.SemaphoreType.DMA
    return pl.pallas_call(
        functools.partial(attend_kernel, size),
        out_shape=(
            jax.ShapeDtypeStruct((heads, length, HEAD), BF16),
            jax.ShapeDtypeStruct((kvs, length, HEAD), BF16),
            jax.ShapeDtypeStruct((kvs, length, HEAD), BF16),
            jax.ShapeDtypeStruct((length, heads * HEAD), BF16),
            jax.ShapeDtypeStruct(near.shape, BF16),
            jax.ShapeDtypeStruct((size,) + gate.shape, BF16),
        ),
        in_specs=[VM] * 8,
        out_specs=(VM,) * 5 + (pl.BlockSpec(memory_space=pl.ANY),),
        scratch_shapes=[
            pltpu.VMEM((heads, length, HEAD), BF16),
            pltpu.VMEM((size,) + near.shape[1:], BF16),
            dma((2 * (size - 1),)), dma((2 * (size - 1),)),
        ]
        + SharedGather.scratch(size, 1),
        compiler_params=params(6),
        cost_estimate=cost(45),
    )(first, weight, cosine, sine, segc, segr, near, gate)


class swap_halves:
    def __init__(self, part, other, sends, recvs):
        core = lax.axis_index("dp")
        share = part.shape[1] // 2
        self.move = remote(
            part.at[:, pl.ds(pl.multiple_of((1 - core) * share, 16), share)], other, sends, recvs, 0, {"dp": 1 - core}
        )

    def start(self):
        self.move.start()

    def wait(self):
        self.move.wait()


def add_halves(part, other, share):
    rows = pl.ds(pl.multiple_of(lax.axis_index("dp") * share.shape[1], 16), share.shape[1])
    for j in range(part.shape[0]):
        share[j] = (part[j, rows].astype(F32) + other[j].astype(F32)).astype(BF16)


def row_moves(size, source, target, sends, recvs, first, begin):
    row = lax.axis_index("row")
    if begin:
        target[row] = source[row]
    for mask in range(1, size):
        move = remote(source.at[row ^ mask], target.at[row], sends, recvs, first + mask - 1, {"row": row ^ mask})
        if begin:
            move.start()
        else:
            move.wait()


def cost(micros):
    return pl.CostEstimate(flops=int(micros * 1e9), bytes_accessed=1 << 20, transcendentals=0)


def attend_back_kernel(
    dmid_ref, weight_ref, q_ref, k_ref, v_ref, cos_ref, sin_ref, segc_ref, segr_ref,
    attn_ref, down_ref, mid_ref,
    dqkv_ref, inner_ref, blk_ref, line_ref, do_ref, dq_ref, dk_ref, dv_ref,
    recv_ref, part_ref, other_ref, share_ref, s1, r1, score, rcore, srow, rrow,
):
    row, core = lax.axis_index("row"), lax.axis_index("dp")
    cols_n = down_ref.shape[0]
    heads, length, _ = q_ref.shape
    kvs = k_ref.shape[0]
    group = heads // kvs
    query_cols = heads * HEAD
    key_cols = (dqkv_ref.shape[1] - query_cols) // 2
    block = 256
    parts, _, width = weight_ref.shape
    greet(row_size=parts, col_size=cols_n, dp_size=2)
    line = ColScatter(cols_n, down_ref, recv_ref, s1, r1)
    line.event(0)
    for j in range(parts):
        part_ref[j] = lax.dot_general(
            attn_ref[...], dmid_ref[:, j * width : (j + 1) * width], (((0,), (0,)), ((), ())), preferred_element_type=F32
        ).astype(BF16)
    cross = swap_halves(part_ref, other_ref, score, rcore)
    cross.start()
    dk_ref[...] = jnp.zeros_like(dk_ref)
    dv_ref[...] = jnp.zeros_like(dv_ref)
    inner_ref[...] = jnp.zeros_like(inner_ref)

    @pl.loop(0, length // block)
    def _(i):
        rows = pl.ds(pl.multiple_of(i * block, block), block)
        total = jnp.zeros((block, query_cols), F32)
        for j in range(parts):
            total += lax.dot_general(
                dmid_ref[rows, j * width : (j + 1) * width], weight_ref[j], (((1,), (1,)), ((), ())), preferred_element_type=F32
            )
        for head in range(heads):
            do_ref[head, rows] = total[:, head * HEAD : (head + 1) * HEAD].astype(BF16)

    @pl.loop(0, heads)
    def _(head):
        @pl.when(head == min(1, heads - 1))
        def _():
            cross.wait()
            add_halves(part_ref, other_ref, share_ref)
            row_moves(parts, share_ref, line_ref, srow, rrow, 0, True)

        @pl.when(head == heads // 2)
        def _():
            line.event(1)

        kv = lax.div(head, group)
        for i in range(length // block):
            rows, extent = slice(i * block, (i + 1) * block), (i + 1) * block
            query, keys, grads = q_ref[head, rows], k_ref[kv, :extent], do_ref[head, rows]
            scores = masked_scores(query, keys, segc_ref[rows], segr_ref[:, :extent], i * block)
            top = jnp.max(scores, axis=1, keepdims=True)
            weights = jnp.exp(scores - top)
            weights = weights * (1.0 / jnp.sum(weights, axis=1, keepdims=True))
            back = lax.dot_general(grads, v_ref[kv, :extent], (((1,), (1,)), ((), ())), preferred_element_type=F32)
            dv_ref[kv, :extent] += lax.dot_general(
                weights.astype(BF16), grads, (((0,), (0,)), ((), ())), preferred_element_type=F32
            )
            ds = (weights * (back - jnp.sum(weights * back, axis=1, keepdims=True))).astype(BF16)
            dq = jnp.dot(ds, keys, preferred_element_type=F32)
            inner_ref[rows] += jnp.sum(dq * query.astype(F32), axis=1, keepdims=True)
            dq_ref[head, rows] = dq
            dk_ref[kv, :extent] += lax.dot_general(ds, query, (((0,), (0,)), ((), ())), preferred_element_type=F32)

    @pl.loop(0, length // block)
    def _(i):
        rows = pl.ds(pl.multiple_of(i * block, block), block)
        low = low_columns(block)
        cosine, sine = cos_ref[rows], sin_ref[rows]
        for ref, count, start, factor in ((dq_ref, heads, 0, HEAD ** (-0.5)), (dk_ref, kvs, query_cols, 1.0), (dv_ref, kvs, query_cols + key_cols, None)):
            for j in range((count + 1) // 2):
                sides = [ref[2 * j + side, rows] if 2 * j + side < count else jnp.zeros((block, HEAD), F32) for side in range(2)]
                part = jnp.concatenate(sides, axis=1)
                if factor is not None:
                    part = (part * cosine - turn(part * sine, low)) * factor
                dqkv_ref[rows, start + 128 * j : start + 128 * (j + 1)] = part.astype(BF16)
        more = jnp.zeros((block, 1), F32)
        for kv in range(kvs):
            more += jnp.sum(dk_ref[kv, rows] * k_ref[kv, rows].astype(F32) + dv_ref[kv, rows] * v_ref[kv, rows].astype(F32), axis=1, keepdims=True)
        inner_ref[rows] += more

    for time in range(2, line.times):
        line.event(time)
    for j in range(parts):
        columns = slice(j * width, (j + 1) * width)
        blk_ref[j] = (mid_ref[:, columns] + line.total(slice(None))[:, columns]).astype(BF16)
    row_moves(parts, share_ref, line_ref, srow, rrow, 0, False)


def attend_back_call(dmid, weight, q, k, v, cosine, sine, segc, segr, columns, attn, down, middle):
    rows_n, cols_n = lax.axis_size("row"), lax.axis_size("col")
    _, heads_cols, width = weight.shape
    quarter = middle.shape[0]
    dma = pltpu.SemaphoreType.DMA
    heads, length, _ = q.shape
    kvs = k.shape[0]
    return pl.pallas_call(
        attend_back_kernel,
        out_shape=(
            jax.ShapeDtypeStruct((length, columns), BF16),
            jax.ShapeDtypeStruct((length, 1), F32),
            jax.ShapeDtypeStruct((rows_n, quarter, width), BF16),
            jax.ShapeDtypeStruct((rows_n, heads_cols // 2, width), BF16),
        ),
        in_specs=[VM] * 12,
        out_specs=(VM,) * 4,
        scratch_shapes=[
            pltpu.VMEM((heads, length, HEAD), BF16),
            pltpu.VMEM((heads, length, HEAD), F32),
            pltpu.VMEM((kvs, length, HEAD), F32),
            pltpu.VMEM((kvs, length, HEAD), F32),
            pltpu.VMEM((2,) + down.shape, BF16),
            pltpu.VMEM(weight.shape, BF16),
            pltpu.VMEM((rows_n, heads_cols // 2, width), BF16),
            pltpu.VMEM((rows_n, heads_cols // 2, width), BF16),
            dma((2,)), dma((2 * cols_n,)), dma((1,)), dma((1,)), dma((rows_n - 1,)), dma((rows_n - 1,)),
        ],
        compiler_params=params(5),
        cost_estimate=cost(80),
    )(dmid, weight, q, k, v, cosine, sine, segc, segr, attn, down, middle)


def middle_kernel(
    rows_n, cols_n, attn_ref, weight_ref, x_ref, gain_ref, tok_ref, near_ref, next_ref, up_ref, down_ref,
    mid_ref, second_ref, cot_ref, ups_ref, downs_ref, part_ref, recv_ref, s1, r1, s2, r2, szc, rzc, *shared,
):
    row, col = lax.axis_index("row"), lax.axis_index("col")
    quarter, features = mid_ref.shape
    width = features // rows_n
    bulks = [SharedGather(rows_n, up_ref, ups_ref, *shared, 0), SharedGather(rows_n, down_ref, downs_ref, *shared, 1)]
    for bulk in bulks:
        bulk.load()
    cot_ref[col] = tok_ref[...]
    take_near(cols_n, cot_ref, near_ref, 1)
    take_near(cols_n, cot_ref, next_ref, 2)
    greet(row_size=rows_n, col_size=cols_n, dp_size=2)
    rest = ColGather(cols_n, cot_ref, szc, rzc, 2)
    rest.event(2)

    @pl.loop(0, rows_n)
    def _(i):
        own = attn_ref[pl.ds(pl.multiple_of(i * quarter, 16), quarter)]
        for j in range(rows_n):
            part_ref[i, :, j * width : (j + 1) * width] = jnp.dot(own, weight_ref[j], preferred_element_type=F32).astype(BF16)

    def finish(rows, total):
        own = pl.ds(row * quarter + rows.start, rows.size)
        squares = jnp.zeros((rows.size, 1), F32)
        for j in range(rows_n):
            columns = slice(j * width, (j + 1) * width)
            value = total[:, columns] + x_ref[j, own].astype(F32)
            mid_ref[rows, columns] = value
            squares += jnp.sum(value * value, axis=1, keepdims=True)
        inverse = lax.rsqrt(squares / features + EPSILON)
        second_ref[col, rows] = (mid_ref[rows] * inverse * gain_ref[...]).astype(BF16)

    RowScatter(rows_n, part_ref, recv_ref, s1, r1).run(finish)
    line = ColGather(cols_n, second_ref, s2, r2)
    line.event(0)
    for bulk in bulks:
        bulk.start()
    for step in range(3, cols_n):
        rest.event(step)
    rest.finish()
    line.event(1)
    bits = bulks[0].gather.bits
    for bulk in bulks:
        bulk.event(0)
    for step in range(2, cols_n):
        line.event(step)
    for step in range(1, bits):
        for bulk in bulks:
            bulk.event(step)
    for bulk in bulks:
        bulk.finish()
    line.finish()


def middle_call(attn, weight, x, gain, tok, near, following, up, down):
    rows_n, cols_n = lax.axis_size("row"), lax.axis_size("col")
    length, features = attn.shape[0], weight.shape[0] * weight.shape[2]
    quarter = length // rows_n
    dma = pltpu.SemaphoreType.DMA
    anywhere = pl.BlockSpec(memory_space=pl.ANY)
    return pl.pallas_call(
        functools.partial(middle_kernel, rows_n, cols_n),
        out_shape=(
            jax.ShapeDtypeStruct((quarter, features), F32),
            jax.ShapeDtypeStruct((cols_n, quarter, features), BF16),
            jax.ShapeDtypeStruct((cols_n, quarter, features), BF16),
            jax.ShapeDtypeStruct((rows_n,) + up.shape, BF16),
            jax.ShapeDtypeStruct((rows_n,) + down.shape, BF16),
        ),
        in_specs=[VM] * 9,
        out_specs=(VM, VM, VM, anywhere, anywhere),
        scratch_shapes=[
            pltpu.VMEM((rows_n, quarter, features), BF16),
            pltpu.VMEM((rows_n - 1, quarter, features), BF16),
        ]
        + [dma((2 * (rows_n - 1),))] * 2
        + [dma((2 * (cols_n - 1),))] * 4
        + SharedGather.scratch(rows_n, 2),
        compiler_params=params(2),
        cost_estimate=cost(130),
    )(attn, weight, x, gain, tok, near, following, up, down)


def back_kernel(rows_n, cols_n, dgate_ref, dup_ref, gate_ref, up_ref, mid_ref, tok_ref, gain_ref, dmid_ref, grad_ref, part_ref, recv_ref, s1, r1, s2, r2):
    row, col = lax.axis_index("row"), lax.axis_index("col")
    quarter, features = mid_ref.shape
    greet(row_size=rows_n, col_size=cols_n)

    def prepare(target):
        tile = 512

        @pl.loop(0, features // tile)
        def _(i):
            columns = pl.ds(i * tile, tile)
            value = lax.dot_general(dgate_ref[target], gate_ref[columns], (((1,), (1,)), ((), ())), preferred_element_type=F32)
            value += lax.dot_general(dup_ref[target], up_ref[columns], (((1,), (1,)), ((), ())), preferred_element_type=F32)
            part_ref[target, :, columns] = value.astype(BF16)

    line = ColScatter(cols_n, part_ref, recv_ref, s1, r1)
    for time in range(line.times):
        line.event(time, prepare)

    grad_ref[...] = jnp.zeros_like(grad_ref)

    @pl.loop(0, quarter // 64)
    def _(i):
        rows = pl.ds(i * 64, 64)
        got = line.total(rows)
        middle = mid_ref[rows]
        inverse = lax.rsqrt(jnp.sum(middle * middle, axis=1, keepdims=True) / features + EPSILON)
        weighted = got * gain_ref[...]
        inner = jnp.sum(middle * weighted, axis=1, keepdims=True) / features
        grad_ref[...] += jnp.sum(got * middle * inverse, axis=0, keepdims=True)
        value = tok_ref[rows].astype(F32) + inverse * weighted - middle * (inverse * inverse * inverse * inner)
        dmid_ref[row, rows] = value.astype(BF16)

    gather = RowGather(rows_n, dmid_ref, s2, r2)
    gather.start()
    gather.run()


def back_call(dgate, dup, gate, up, middle, tok, gain):
    rows_n, cols_n = lax.axis_size("row"), lax.axis_size("col")
    quarter, features = middle.shape
    hidden = gate.shape[1]
    return pl.pallas_call(
        functools.partial(back_kernel, rows_n, cols_n),
        out_shape=(
            jax.ShapeDtypeStruct((rows_n, quarter, features), BF16),
            jax.ShapeDtypeStruct((1, features), F32),
        ),
        in_specs=[VM] * 7,
        out_specs=(VM,) * 2,
        scratch_shapes=[
            pltpu.VMEM((cols_n, quarter, features), BF16),
            pltpu.VMEM((2, cols_n, quarter, features), BF16),
        ]
        + [pltpu.SemaphoreType.DMA((2,)), pltpu.SemaphoreType.DMA((2 * cols_n,))]
        + [pltpu.SemaphoreType.DMA((2 * (rows_n - 1),))] * 2,
        compiler_params=params(3),
    )(dgate.reshape(cols_n, quarter, hidden), dup.reshape(cols_n, quarter, hidden), gate, up, middle, tok, gain)


def last_kernel(
    size, dqkv_ref, weight_ref, first_ref, outline_ref, blk_ref, inner_ref, act_ref, inv_ref, grad2_ref,
    out_ref, block_ref, inners_ref, gains_ref, gqkv_ref, gout_ref,
    part_ref, recv_ref, qpart_ref, qother_ref, qshare_ref, qline_ref, qrecv_ref, orecv_ref, rgain_ref, pair_ref, pairs_ref,
    s1, r1, sblk, rblk, sinn, rinn, score, rcore, srow, rrow, so, ro, sq, rq, sg, rg, sp, rp, sf, rf,
):
    row, col, core = lax.axis_index("row"), lax.axis_index("col"), lax.axis_index("dp")
    length, width = act_ref.shape
    quarter = length // size
    barrier = pltpu.get_barrier_semaphore()
    peers = [{"row": row ^ mask} for mask in range(1, size)]
    others = [{"col": lax.rem(col + k, size)} for k in range(1, size)]
    others += [{"col": lax.rem(col + k, size), "dp": 1 - core} for k in range(size)]
    for peer in peers + others:
        pl.semaphore_signal(barrier, inc=1, device_id=peer, device_id_type=MESH)
    pl.semaphore_wait(barrier, len(peers) + len(others))

    scatter = RowScatter(size, part_ref, recv_ref, s1, r1)
    inners_ref[row] = inner_ref[...]
    rgain_ref[row] = grad2_ref[row]
    small = []
    for mask in range(1, size):
        small.append(remote(inner_ref, inners_ref.at[row], sinn, rinn, mask - 1, {"row": row ^ mask}))
        small.append(remote(grad2_ref.at[row ^ mask], rgain_ref.at[row], sg, rg, mask - 1, {"row": row ^ mask}))
    for move in small:
        move.start()
    oline = ColScatter(size, outline_ref, orecv_ref, so, ro)
    oline.event(0)

    @pl.loop(0, size)
    def _(j):
        columns = pl.ds(pl.multiple_of(j * width, 128), width)
        qpart_ref[j] = lax.dot_general(
            first_ref[:, columns], dqkv_ref[...], (((0,), (0,)), ((), ())), preferred_element_type=F32
        ).astype(BF16)

    cross = swap_halves(qpart_ref, qother_ref, score, rcore)
    cross.start()
    oline.event(1)

    @pl.loop(0, size)
    def _(j):
        part_ref[j] = lax.dot_general(dqkv_ref[...], weight_ref[j], (((1,), (1,)), ((), ())), preferred_element_type=F32).astype(BF16)

    cross.wait()
    add_halves(qpart_ref, qother_ref, qshare_ref)
    row_moves(size, qshare_ref, qline_ref, srow, rrow, 0, True)
    scatter.start()
    for time in range(2, oline.times):
        oline.event(time)
    share_o = outline_ref.shape[1]
    share_q = qline_ref.shape[1]

    def across(ref, share, which):
        piece = ref.at[pl.ds(pl.multiple_of(core * share, 8), share)]
        return remote(piece, piece, sf, rf, which, {"dp": 1 - core})

    gout_ref[pl.ds(pl.multiple_of(core * share_o, 8), share_o)] = oline.total(slice(None))
    across(gout_ref, share_o, 0).start()

    block_ref[pl.ds(pl.multiple_of(row * quarter, 16), quarter)] = blk_ref[row]
    for mask in range(1, size):
        remote(
            blk_ref.at[row ^ mask], block_ref.at[pl.ds(pl.multiple_of(row * quarter, 16), quarter)], sblk, rblk, mask - 1, {"row": row ^ mask}
        ).start()
    row_moves(size, qshare_ref, qline_ref, srow, rrow, 0, False)
    qline = ColScatter(size, qline_ref, qrecv_ref, sq, rq)
    qline.event(0)
    pair_ref[0] = jnp.zeros_like(pair_ref[0])

    def finish(rows, total):
        out_ref[rows] = total
        pair_ref[0] += jnp.sum(total * act_ref[rows].astype(F32) * inv_ref[rows], axis=0, keepdims=True)

    for step in range(scatter.bits - 1):
        scatter.event(step, finish)
    qline.event(1)
    qline.event(2)
    scatter.event(scatter.bits - 1, finish)
    scatter.close()
    for move in small:
        move.wait()
    pair_ref[1] = jnp.sum(rgain_ref[...], axis=0)
    own = core * size + col
    pairs_ref[own] = pair_ref[...]
    for k, peer in enumerate(others):
        remote(pair_ref, pairs_ref.at[own], sp, rp, k, peer).start()
    for time in range(3, qline.times):
        qline.event(time)
    gqkv_ref[pl.ds(pl.multiple_of(core * share_q, 8), share_q)] = qline.total(slice(None))
    across(gqkv_ref, share_q, 1).start()
    for k, peer in enumerate(others):
        remote(pair_ref, pairs_ref.at[own], sp, rp, k, peer).wait()
    gains_ref[...] = jnp.sum(pairs_ref[...], axis=0)
    for mask in range(1, size):
        remote(
            blk_ref.at[row ^ mask], block_ref.at[pl.ds(pl.multiple_of(row * quarter, 16), quarter)], sblk, rblk, mask - 1, {"row": row ^ mask}
        ).wait()
    across(gout_ref, share_o, 0).wait()
    across(gqkv_ref, share_q, 1).wait()


def last_call(dqkv, weight, first, outline, blk, inner, activations, inv1, grad2):
    size = lax.axis_size("row")
    length, width = activations.shape
    columns = weight.shape[1]
    heads_cols = 2 * outline.shape[1]
    dma = pltpu.SemaphoreType.DMA
    count = 2 * size - 1
    return pl.pallas_call(
        functools.partial(last_kernel, size),
        out_shape=(
            jax.ShapeDtypeStruct((length, width), F32),
            jax.ShapeDtypeStruct((length, width), BF16),
            jax.ShapeDtypeStruct((size,) + inner.shape, F32),
            jax.ShapeDtypeStruct((2, 1, width), F32),
            jax.ShapeDtypeStruct((width, columns), F32),
            jax.ShapeDtypeStruct((heads_cols, width), F32),
        ),
        in_specs=[VM] * 9,
        out_specs=(VM,) * 6,
        scratch_shapes=[
            pltpu.VMEM((size, length, width), BF16),
            pltpu.VMEM((size - 1, length, width), BF16),
            pltpu.VMEM((size, width, columns), BF16),
            pltpu.VMEM((size, width // 2, columns), BF16),
            pltpu.VMEM((size, width // 2, columns), BF16),
            pltpu.VMEM((size, width // 2, columns), BF16),
            pltpu.VMEM((2, size, width // 2, columns), BF16),
            pltpu.VMEM((2, size, heads_cols // 2, width), BF16),
            pltpu.VMEM((size, 1, width), F32),
            pltpu.VMEM((2, 1, width), F32),
            pltpu.VMEM((2 * size, 2, 1, width), F32),
        ]
        + [dma((2 * (size - 1),))] * 2
        + [dma((size - 1,))] * 2
        + [dma((size - 1,))] * 2
        + [dma((1,))] * 2
        + [dma((size - 1,))] * 2
        + [dma((2,)), dma((2 * size,))] * 2
        + [dma((size - 1,))] * 2
        + [dma((count,))] * 2
        + [dma((2,))] * 2,
        compiler_params=params(4),
        cost_estimate=cost(80),
    )(dqkv, weight.reshape(size, width, columns), first, outline, blk, inner, activations, inv1, grad2.reshape(size, 1, width))


def weight_grads_kernel(second_ref, cot_ref, dgate_ref, dup_ref, hidden_ref, out_ref):
    which, part = pl.program_id(0), pl.program_id(1)
    span = out_ref.shape[2]
    columns = pl.ds(pl.multiple_of(part * span, 128), span)
    for index, left, right in ((0, second_ref, dgate_ref), (1, second_ref, dup_ref), (2, cot_ref, hidden_ref)):

        @pl.when(which == index)
        def _():
            out_ref[0, 0] = lax.dot_general(
                left[:, columns], right[...], (((0,), (0,)), ((), ())), preferred_element_type=F32
            ).astype(BF16)


def weight_grads_call(second, cot, dgate, dup, hidden):
    parts = 2 * lax.axis_size("row")
    span, columns = second.shape[1] // parts, hidden.shape[1]
    return pl.pallas_call(
        weight_grads_kernel,
        grid=(3, parts),
        out_shape=jax.ShapeDtypeStruct((parts, 3, span, columns), BF16),
        in_specs=[VM] * 5,
        out_specs=pl.BlockSpec((1, 1, span, columns), lambda g, p: (p, g, 0, 0)),
        compiler_params=pltpu.CompilerParams(vmem_limit_bytes=VMEM_LIMIT),
        cost_estimate=cost(30),
    )(second, cot, dgate, dup, hidden)


def dot(left, right, dims):
    return lax.dot_general(left, right, (dims, ((), ())), preferred_element_type=F32)


def rotary_tables(positions):
    exponent = jnp.arange(0, HEAD, 2).astype(F32) / HEAD
    inverse = jnp.power(F32(THETA), -exponent)
    phase = positions[:, None] * inverse[None, :]
    phase = jnp.concatenate([phase] * (2 * 128 // HEAD), axis=1)
    return (jnp.cos(phase), jnp.sin(phase))


def gather(values, axis_name, axis=0):
    return lax.all_gather(values, axis_name, axis=axis, tiled=True)


def local(
    activations, segments, positions, first_gain, query_weight, key_weight, value_weight, out_weight,
    second_gain, gate_weight, up_weight, down_weight, cotangent,
):
    rows = lax.axis_size("row")
    row, col = lax.axis_index("row"), lax.axis_index("col")
    length, width = activations.shape
    features = rows * width
    query_cols, key_cols = query_weight.shape[1], key_weight.shape[1]
    heads, kvs = query_cols // HEAD, key_cols // HEAD
    hidden_cols = gate_weight.shape[1]
    spare = jnp.zeros((width, -key_cols % 128), BF16)
    key_span = key_cols + spare.shape[1]
    qkv_cols = query_cols + 2 * key_span

    small = jnp.concatenate([segments.astype(F32), positions.astype(F32), first_gain, second_gain]).reshape(-1, 128)
    qkv_weight = jnp.concatenate([query_weight, key_weight, spare, value_weight, spare], axis=1)
    x_blocks, first, inv1, cot_tok, smalls, qkv_all, out_all_w, near = first_call(activations, cotangent, small, qkv_weight, out_weight)
    qkv_all = qkv_all.reshape(features, qkv_cols)
    smalls = smalls.reshape(rows, -1)
    own = lax.dynamic_slice_in_dim(smalls, col, 1, 0)[0]
    segment_own, position_own = own[:length], own[length : 2 * length]
    gain2 = smalls[:, 2 * length + width :].reshape(1, features)

    cosine, sine = rotary_tables(position_own)
    segc, segr = segment_own[:, None], segment_own[None]
    q, k, v, attn, following, gate_all = attend_call(first, qkv_all, cosine, sine, segc, segr, near, gate_weight, heads, kvs)
    middle, second_all, cot_all, up_all, down_all = middle_call(
        attn, out_all_w, x_blocks, gain2, cot_tok, near, following, up_weight, down_weight
    )
    gate_all, up_all = gate_all.reshape(features, hidden_cols), up_all.reshape(features, hidden_cols)
    second_all, cot_all = second_all.reshape(-1, features), cot_all.reshape(-1, features)
    gate = dot(second_all, gate_all, ((1,), (0,)))
    up = dot(second_all, up_all, ((1,), (0,)))
    sigma = jax.nn.sigmoid(gate)
    swish = gate * sigma
    hidden = (swish * up).astype(BF16)
    tokens = hidden.shape[0]
    down_part = lax.dot_general(hidden, down_all, (((1,), (1,)), ((), ())), preferred_element_type=F32).reshape(tokens, features)
    down_part = down_part.astype(BF16).reshape(-1, middle.shape[0], features)

    cot_split = cot_all.reshape(tokens, rows, width)
    dhidden = lax.dot_general(cot_split, down_all, (((1, 2), (0, 2)), ((), ())), preferred_element_type=F32)
    swish_grad = sigma * (1.0 + gate * (1.0 - sigma))
    dgate = (dhidden * up * swish_grad).astype(BF16)
    dup = (dhidden * swish).astype(BF16)
    grads = weight_grads_call(second_all, cot_all, dgate, dup, hidden)
    grads, dgate, dup = lax.optimization_barrier((grads, dgate, dup))
    grads = lax.psum_scatter(grads.reshape(-1, hidden_cols), ("row", "dp"), scatter_dimension=0, tiled=True)
    dmid_all, gain2_grad = back_call(dgate, dup, gate_all, up_all, middle, cot_tok, gain2)
    dmid_all = dmid_all.reshape(length, features)

    dqkv, inner1, blk, outline = attend_back_call(
        dmid_all, out_all_w, q, k, v, cosine, sine, segc, segr, qkv_cols, attn, down_part, middle
    )
    dfirst, block_out, inner1, gains, qkv_grad, out_grad = last_call(
        dqkv, qkv_all, first, outline, blk, inner1.reshape(-1, 128), activations, inv1, gain2_grad
    )
    inner1 = jnp.sum(inner1, axis=0).reshape(length, 1) / (inv1 * features)
    own_x = activations.astype(F32)
    dmid_own = lax.dynamic_slice_in_dim(dmid_all, row * width, width, 1).astype(F32)
    input_grad = dmid_own + inv1 * first_gain[None] * dfirst - own_x * (inv1 * inv1 * inv1 * inner1)

    grads, dfirst = lax.optimization_barrier((grads, dfirst))
    grads = gather(grads.reshape(1, 3, -1, hidden_cols), "dp").astype(F32)
    return (
        block_out,
        input_grad,
        gains[0, 0],
        qkv_grad[:, :query_cols],
        qkv_grad[:, query_cols : query_cols + key_cols],
        qkv_grad[:, query_cols + key_span : query_cols + key_span + key_cols],
        out_grad,
        gains[1, 0],
        grads[:, 0].reshape(width, hidden_cols),
        grads[:, 1].reshape(width, hidden_cols),
        grads[:, 2].reshape(width, hidden_cols).T,
    )


def solution(mesh):
    tokens, block, swapped = P(("dp", "col"), "row"), P("row", "col"), P("col", "row")
    return jax.shard_map(
        local,
        mesh=mesh,
        in_specs=(
            tokens, P(("dp", "row")), P(("dp", "row")), P("row"), block, block, block, swapped,
            P("row"), block, block, swapped, tokens,
        ),
        out_specs=(tokens, tokens, P("row"), block, block, block, swapped, P("row"), block, block, swapped),
        check_vma=False,
    )
```

time: 1090 us -> 809 us (0.74)
  waiting for transfers between devices: 215 us -> 3.37 us
  Pallas kernels: 525 us -> 664 us
  blocking collectives: 138 us -> 0 us
  matrix products: 120 us -> 58.4 us
  local copies, waits for them, and re-layouts: 26 us -> 45.8 us
  starting transfers between devices: 18 us -> 0.08 us
  other arithmetic: 27.1 us -> 15.8 us
    reduce_scatter x6 -> x1, waiting for transfers between devices: 214 us -> 0.02 us  [local(): lax.psum_scatter(grads.reshape(-1, hidden_cols), ('row', 'dp'), scatter_d...]
    psum x3 -> x0, blocking collectives: 138 us -> none  [the longest x1 66.9 us: local(): gain1_grad = lax.psum(jnp.sum(dfirst * own_x * inv1, axis=0), ('dp', 'col'))]
    pallas_call x2 -> x3, Pallas kernels: 72.7 us -> 184 us  [the longest x1 90 us: last_call(): pl.pallas_call(functools.partial(last_kernel, size), out_shape=(jax.Shape...]
    pallas_call x1, Pallas kernels: 121 us -> 162 us  [back_call(): pl.pallas_call(functools.partial(back_kernel, rows_n, cols_n), out_shape=...]
    dot_general x6 -> x2, matrix products: 71.1 us -> 30.4 us  [dot(): lax.dot_general(left, right, (dims, ((), ())), preferred_element_type=F32)]
    pallas_call x1, Pallas kernels: 41.2 us -> 79.5 us  [attend_back_call(): pl.pallas_call(attend_back_kernel, out_shape=(jax.ShapeDtypeStruct((lengt...]
    pallas_call x1, Pallas kernels: 154 us -> 129 us  [middle_call(): pl.pallas_call(functools.partial(middle_kernel, rows_n, cols_n), out_shap...]
    pallas_call x1, Pallas kernels: 136 us -> 111 us  [first_call(): pl.pallas_call(functools.partial(first_kernel, size), out_shape=(jax.Shap...]
  transfers between devices with their start and end apart: 17 -> 2, of which waited for: 4 -> 1; matrix products, arithmetic and copies ran while one was open for 13% -> 5% of each run, Pallas kernels for 37% -> 41%
where the time goes in v3:
time: 809 us; the launch traced here: 802 us
  Pallas kernels  664 us (82%)
  matrix products  58.4 us (7%)
  local copies, waits for them, and re-layouts  45.8 us (6%)
  other arithmetic  15.8 us (2%)
  between operations  14.7 us (2%)
    pallas_call x1, Pallas kernels, back_call(): pl.pallas_call(functools.partial(back_kernel, rows_n, cols_n), out_shape=...  162 us
    pallas_call x1, Pallas kernels, middle_call(): pl.pallas_call(functools.partial(middle_kernel, rows_n, cols_n), out_shap...  129 us
    pallas_call x1, Pallas kernels, first_call(): pl.pallas_call(functools.partial(first_kernel, size), out_shape=(jax.Shap...  111 us
    pallas_call x1, Pallas kernels, last_call(): pl.pallas_call(functools.partial(last_kernel, size), out_shape=(jax.Shape...  90 us
    pallas_call x1, Pallas kernels, attend_back_call(): pl.pallas_call(attend_back_kernel, out_shape=(jax.ShapeDtypeStruct((lengt...  79.5 us
    pallas_call x1, Pallas kernels, attend_call(): pl.pallas_call(functools.partial(attend_kernel, size), out_shape=(jax.Sha...  53.6 us
    pallas_call x1, Pallas kernels, weight_grads_call(): pl.pallas_call(weight_grads_kernel, grid=(3, parts), out_shape=jax.ShapeD...  40.1 us
    dot_general x2, matrix products, dot(): lax.dot_general(left, right, (dims, ((), ())), preferred_element_type=F32)  30.4 us
  transfers between devices with their start and end apart: 2, of which 1 were waited for; matrix products, arithmetic and copies ran while one was open for 5% of the time, Pallas kernels for 41%

profile of v3, /device:TPU:0, one launch (start us, length us, event | category | flops | bytes accessed | tf_op | source)
XLA Modules:
  0.0 802.4 jit_solution(17369173981570371377)
XLA Ops:
  7.2 0.0 reduce-scatter.2.cloned.1.call-start
  7.2 0.7 convert_element_type.38
  7.9 0.7 convert_element_type.39
  8.6 2.1 pad_maximum_fusion.qkv_ref
  10.7 1.3 maximum_bitcast_fusion.small_ref
  12.0 110.8 %shard_map.212 = (bf16[4,1024,512]{2,1,0:T(8,128)(2,1)}, bf16[1024,2048]{1,0:T(8,128)(2,1)}, f32[1024,1]{1,0:T(8,128)}, bf16[256,2048]{1,0:T(8,128)(2,1)}, f32[4...) custom-call(bf16[1024,512]{1,0:T(8,128)(2,1)} %act_ref.3, ...), custom_call_target="tpu_custom_call" | custom-call | tf_op jit(solution)/shard_map/pallas_call | solution.py:473
  122.9 0.8 copy.48
  123.7 0.6 copy.44
  124.3 0.1 constant_dynamic-slice_fusion
  124.4 1.0 copy.37.segc_ref
  125.4 0.2 broadcast_multiply_fusion
  125.6 3.0 fusion.13
  128.6 0.0 copy-done.5
  128.6 53.6 %shard_map.213 = (bf16[8,1024,64]{2,1,0:T(8,128)(2,1)}, bf16[2,1024,64]{2,1,0:T(8,128)(2,1)}, bf16[2,1024,64]{2,1,0:T(8,128)(2,1)}, bf16[1024,512]{1,0:T(8,128)(...) custom-call(bf16[1024,2048]{1,0:T(8,128)(2,1)} %get-tuple-element.46.first_ref, ...), custom_call_target="tpu_custom_call" | custom-call | flops 44999999488 | bytes 1048576 | tf_op jit(solution)/shard_map/pallas_call | solution.py:579
  182.2 128.8 %shard_map.214 = (f32[256,2048]{1,0:T(8,128)}, bf16[4,256,2048]{2,1,0:T(8,128)(2,1)}, bf16[4,256,2048]{2,1,0:T(8,128)(2,1)}, bf16[4,512,2048]{2,1,0:T(8,128)(2,1)}, bf16[4,2048,512]{2,1,0:T(8,128)(2,1)}) custom-call(bf16[1024,512]{1,0:T(8,128)(2,1)} %get-tuple-element.50.attn_ref, bf16[4,512,512]{2,1,0:T(8,128)(2,1)} %get-tuple-element.51.weight_ref, ...), custom_call_target="tpu_custom_call" | custom-call | flops 130000003072 | bytes 1048576 | tf_op jit(solution)/shard_map/pallas_call | solution.py:828
  311.0 7.8 reshape_reshape.3
  318.8 14.6 %fusion.6 = f32[1024,2048,1]{1,0,2:T(8,128)} fusion(bf16[4,2048,512]{2,1,0:T(8,128)(2,1)} %get-tuple-element.57, bf16[1024,4,512]{2,1,0:T(4,128)(2,1)} %reshape_reshape.3), kind=kOutput, calls=%fused_computation.10 | convolution fusion | flops 8589934592 | bytes 20971520 | tf_op jit(solution)/shard_map/dot_general | solution.py:1144
  333.4 0.0 copy-done
  333.4 0.0 copy-done.8
  333.4 11.1 %fusion.19 = f32[1024,2048]{1,0:T(8,128)} fusion(bf16[1024,2048]{1,0:T(8,128)(2,1)S(1)} %bitcast.80, bf16[2048,2048]{1,0:T(8,128)(2,1)S(1)} %bitcast.54), kind=kOutput, calls=%fused_computation.31 | convolution fusion | flops 8589934592 | bytes 20971520 | tf_op jit(solution)/shard_map/dot_general | solution.py:1087
  344.5 19.3 %multiply_convert_fusion = (bf16[1024,2048]{1,0:T(8,128)(2,1)}, bf16[1024,2048]{1,0:T(8,128)(2,1)}, bf16[1024,2048]{1,0:T(8,128)(2,1)}) fusion(f32[1024,2048]{1,0:T(8,128)} %fusion.19, f32[1024,2048,1]{1,0,2:T(8,128)} %fusion.6, bf16[1024,2048]{1,0:T(8,128)(2,1)S(1)} %bitcast.81, bf16[2048,2048]{1,0:T(8,128)(2,1)} %bitcast.55), kind=kOutput, calls=%fused_computation.5 | convolution fusion | flops 8621391872 | bytes 41943040 | tf_op jit(solution)/shard_map/dot_general | solution.py:1087
  363.8 40.1 %shard_map.215 = bf16[8,3,256,2048]{3,2,1,0:T(8,128)(2,1)} custom-call(bf16[1024,2048]{1,0:T(8,128)(2,1)} %bitcast.79, bf16[1024,2048]{1,0:T(8,128)(2,1)} %bitcast.58, bf16[1024,2048]{1,0:T(8,128)(2,1)} %get-tuple-element.60.dgate_ref, bf16[1024,2048]{1,0:T(8,128)(2,1)} %get-tuple-element.61.dup_ref, bf16[1024,2048]{1,0:T(8,128)(2,1)} %get-tuple-element.83.hidden_ref), custom_call_target="tpu_custom_call" | custom-call | flops 30000001024 | bytes 1048576 | tf_op jit(solution)/shard_map/pallas_call | solution.py:1075
  403.9 0.0 reduce-scatter.2.cloned.1.call-update
  403.9 0.0 all-gather.2.cloned.1.call-start
  404.0 13.4 %fusion.8 = bf16[1024,4,512]{2,0,1:T(8,128)(2,1)S(1)} fusion(bf16[4,2048,512]{2,1,0:T(8,128)(2,1)} %get-tuple-element.57, bf16[1024,2048]{1,0:T(8,128)(2,1)} %get-tuple-element.83.hidden_ref), kind=kOutput, calls=%fused_computation.12 | convolution fusion | flops 8592031744 | bytes 16777216 | tf_op jit(solution)/shard_map/dot_general | solution.py:1140
  417.3 5.8 copy.39
  423.1 8.4 %convert_element_type.45.down_ref = bf16[4,256,2048]{2,1,0:T(8,128)(2,1)} reshape(bf16[1024,4,512]{2,1,0:T(4,128)(2,1)} %copy.39) | data formatting | bytes 8388608 | tf_op jit(solution)/shard_map/convert_element_type | solution.py:1141
  431.5 161.6 %shard_map.216 = (bf16[4,256,2048]{2,1,0:T(8,128)(2,1)}, f32[1,2048]{1,0:T(1,128)}) custom-call(bf16[4,256,2048]{2,1,0:T(8,128)(2,1)} %bitcast.59, bf16[4,256,2048]{2,1,0:T(8,128)(2,1)} %bitcast.60, bf16[2048,2048]{1,0:T(8,128)(2,1)} %bitcast.53, bf16[2048,2048]{1,0:T(8,128)(2,1)} %bitcast.56, f32[256,2048]{1,0:T(8,128)} %get-tuple-element.62.mid_ref, ...), custom_call_target="tpu_custom_call" | custom-call | tf_op jit(solution)/shard_map/pallas_call | solution.py:893
  593.1 79.5 %shard_map.217 = (bf16[1024,768]{1,0:T(8,128)(2,1)}, f32[1024,1]{1,0:T(8,128)}, bf16[4,256,512]{2,1,0:T(8,128)(2,1)}, bf16[4,256,512]{2,1,0:T(8,128)(2,1)}) custom-call(bf16[1024,2048]{1,0:T(8,128)(2,1)} %bitcast.64, bf16[4,512,512]{2,1,0:T(8,128)(2,1)} %get-tuple-element.51.weight_ref, bf16[8,1024,64]{2,1,0:T(8,128)(2,1)} %get-tuple-element.64.q_ref, ...), custom_call_target="tpu_custom_call" | custom-call | flops 80000000000 | bytes 1048576 | tf_op jit(solution)/shard_map/pallas_call | solution.py:740
  672.6 1.8 reduce
  674.5 90.0 %shard_map.218 = (f32[1024,512]{1,0:T(8,128)}, bf16[1024,512]{1,0:T(8,128)(2,1)}, f32[4,8,128]{2,1,0:T(8,128)}, f32[2,1,512]{2,1,0:T(1,128)}, f32[512,768]{1,0:T(8,128)}, /*index=5*/f32[512,512]{1,0:T(8,128)}) custom-call(bf16[1024,768]{1,0:T(8,128)(2,1)} %get-tuple-element.67.dqkv_ref, bf16[4,512,768]{2,1,0:T(8,128)(2,1)} %get-tuple-element.47.weight_ref, ...), custom_call_target="tpu_custom_call" | custom-call | flops 80000000000 | bytes 1048576 | tf_op jit(solution)/shard_map/pallas_call | solution.py:1020
  764.5 0.0 copy-start.1
  764.5 0.0 copy-start.6
  764.5 0.0 reduce-scatter.2.cloned.1.call-done
  764.5 0.0 all-gather.2.cloned.1.call-update
  764.6 0.9 reduce_sum.9
  765.4 1.0 copy.41
  766.5 2.3 slice.39
  768.7 1.7 fusion.15
  770.4 0.0 copy-done.7
  770.4 0.6 fusion.18
  771.0 2.0 fusion.17
  773.0 3.4 multiply_subtract_fusion
  776.4 3.3 all-gather.2.cloned.1.call-done
  779.7 8.0 %fusion.16 = (f32[2,1,256,2048]{3,2,1,0:T(8,128)}, f32[2,1,256,2048]{3,2,1,0:T(8,128)}, f32[2,1,256,2048]{3,2,1,0:T(8,128)}) fusion(bf16[2,3,256,2048]{3,2,1,0:T(8,128)(2,1)} %all-gather.2.cloned.1.call-done), kind=kLoop, calls=%fused_computation.28 | loop fusion | bytes 25165824 | tf_op jit(solution)/shard_map/slice | solution.py:1178
  787.7 5.5 copy.42
  793.2 1.0 copy.51
  794.2 1.0 copy.52
  (14 shorter events, 0.0 us)
Async XLA Ops:
  7.2 757.3 %reduce-scatter.2.cloned.1.call-start = ((), (), s32[]{:S(2)}) async-start(), calls=%async_computation.1 | async-start | bytes 28311552 | tf_op jit(solution)/shard_map/reduce_scatter | solution.py:1150
  124.4 4.2 copy-start.5
  318.8 14.6 %copy-start = (bf16[4,512,2048]{2,1,0:T(8,128)(2,1)S(1)}, bf16[4,512,2048]{2,1,0:T(8,128)(2,1)}, u32[]{:S(2)}) copy-start(bf16[4,512,2048]{2,1,0:T(8,128)(2,1)} %get-tuple-element.59) | copy-start | bytes 25165828
  318.8 14.6 %copy-start.8 = (bf16[4,256,2048]{2,1,0:T(8,128)(2,1)S(1)}, bf16[4,256,2048]{2,1,0:T(8,128)(2,1)}, u32[]{:S(2)}) copy-start(bf16[4,256,2048]{2,1,0:T(8,128)(2,1)} %get-tuple-element.55) | copy-start | bytes 12582916
  403.9 375.8 %all-gather.2.cloned.1.call-start = ((), (), s32[]{:S(2)}) async-start(), calls=%async_computation.2 | async-start | bytes 9437184 | tf_op jit(solution)/shard_map/all_gather | solution.py:1099
  764.5 6.0 copy-start.7
  764.5 8.5 %copy-start.1 = (bf16[1024,512]{1,0:T(8,128)(2,1)S(1)}, bf16[1024,512]{1,0:T(8,128)(2,1)}, u32[]{:S(2)}) copy-start(bf16[1024,512]{1,0:T(8,128)(2,1)} %act_ref.3) | copy-start | bytes 3145732
  764.5 8.5 %copy-start.2 = (f32[1024,512]{1,0:T(8,128)S(1)}, f32[1024,512]{1,0:T(8,128)}, u32[]{:S(2)}) copy-start(f32[1024,512]{1,0:T(8,128)} %get-tuple-element.74) | copy-start | bytes 6291460
  764.5 8.5 %copy-start.6 = (f32[512]{0:T(512)S(1)}, f32[512]{0:T(512)}, u32[]{:S(2)}) copy-start(f32[512]{0:T(512)} %param.16) | copy-start | bytes 6148
  787.7 5.5 copy-start.4
  787.7 6.5 copy-start.3
Sparse Core Ops, SparseCore 0:
  404.0 184.8 reduce-scatter.1
  764.7 14.9 all-gather.1

commit v4 on v3

--- a/solution.py
+++ b/solution.py
@@ -145,53 +145,71 @@
 
 
 class RowScatter:
-    def __init__(self, size, part_ref, recv_ref, sends, recvs):
+    def __init__(self, size, part_ref, recv_ref, sends, recvs, begin=0):
         self.size, self.part, self.recv = size, part_ref, recv_ref
         self.bits = size.bit_length() - 1
         self.row = lax.axis_index("row")
-        half = part_ref.shape[1] // 2
+        half = recv_ref.shape[1] // 2
         self.rows = [pl.ds(part * half, half) for part in range(2)]
+        self.own = [pl.ds(pl.multiple_of(begin + part * half, 16), half) for part in range(2)]
         self.plans = []
         for part in range(2):
             order = self.order(part)
-            steps = []
+            steps, held = [], {}
             for step in range(self.bits):
                 bit, rest = 1 << order[step], order[step + 1 :]
                 count = 1 << len(rest)
-                copies = []
+                copies, sums = [], {}
                 for item in range(count - 1, -1, -1):
                     mask = sum(1 << other for j, other in enumerate(rest) if item >> j & 1)
                     place = size - 2 * count + item
-                    copies.append((
-                        item, mask, place,
-                        remote(
-                            part_ref.at[self.row ^ mask ^ bit, self.rows[part]], recv_ref.at[place, self.rows[part]],
-                            sends, recvs, part * (size - 1) + place, {"row": self.row ^ bit},
-                        ),
-                    ))
+                    copy = remote(
+                        self.spot(part, mask ^ bit, held), recv_ref.at[place, self.rows[part]],
+                        sends, recvs, part * (size - 1) + place, {"row": self.row ^ bit},
+                    )
+                    copies.append((mask, place, held.get(mask), copy))
+                    sums[mask] = place
+                held = sums
                 steps.append(copies)
             self.plans.append(steps)
 
+    def spot(self, part, mask, held):
+        if mask in held:
+            return self.recv.at[held[mask], self.rows[part]]
+        return self.part.at[self.row ^ mask, self.own[part]]
+
     def order(self, part):
         return list(range(self.bits)) if part == 0 else list(range(self.bits))[::-1]
 
     def start(self):
         for part in range(2):
-            for _, _, _, copy in self.plans[part][0]:
-                copy.start()
+            for copies in self.plans[part][0]:
+                copies[3].start()
 
     def event(self, step, finish):
         last = step + 1 == self.bits
         for part in range(2):
-            rows = self.rows[part]
-            for item, mask, place, copy in self.plans[part][step]:
+            rows, own = self.rows[part], self.own[part]
+            for mask, place, before, copy in self.plans[part][step]:
                 copy.wait_recv()
-                total = self.part[self.row ^ mask, rows].astype(F32) + self.recv[place, rows].astype(F32)
+                size, begin, start = min(64, rows.size), own.start, rows.start
+
+                @pl.loop(0, rows.size // size)
+                def _(i):
+                    here = pl.ds(pl.multiple_of(start + i * size, 16), size)
+                    if before is None:
+                        had = self.part[self.row ^ mask, pl.ds(pl.multiple_of(begin + i * size, 16), size)]
+                    else:
+                        had = self.recv[before, here]
+                    total = had.astype(F32) + self.recv[place, here].astype(F32)
+                    if last:
+                        finish(here, total)
+                    else:
+                        self.recv[place, here] = total.astype(BF16)
+
                 if last:
-                    finish(rows, total)
                     continue
-                self.part[self.row ^ mask, rows] = total.astype(BF16)
-                for _, mask2, _, copy2 in self.plans[part][step + 1]:
+                for mask2, _, _, copy2 in self.plans[part][step + 1]:
                     if mask2 ^ 1 << self.order(part)[step + 1] == mask:
                         copy2.start()
 
@@ -265,12 +283,12 @@
     def __init__(self, size, part, recv, sends, recvs):
         self.size, self.part, self.recv, self.sends, self.recvs = size, part, recv, sends, recvs
         self.col = lax.axis_index("col")
-        self.times = 2 * size - 1
+        self.times = size
 
     def copy(self, side, target, source):
         step = 1 if side == 0 else self.size - 1
         return pltpu.make_async_remote_copy(
-            src_ref=source.at[target], dst_ref=self.recv.at[side, target], send_sem=self.sends.at[side],
+            src_ref=self.recv.at[target + 1 - side] if source is None else source.at[target], dst_ref=self.recv.at[target + 1 - side], send_sem=self.sends.at[side],
             recv_sem=self.recvs.at[side * self.size + target],
             device_id={"col": lax.rem(self.col + step, self.size)}, device_id_type=MESH,
         )
@@ -294,7 +312,14 @@
 
             @pl.when(valid & jnp.logical_not(first) & (target != col))
             def _():
-                self.recv[side, place] = (self.recv[side, place].astype(F32) + self.part[place].astype(F32)).astype(BF16)
+                chunk = min(64, self.part.shape[1])
+
+                @pl.loop(0, self.part.shape[1] // chunk)
+                def _(i):
+                    rows = pl.ds(pl.multiple_of(i * chunk, 16), chunk)
+                    self.recv[place + 1 - side, rows] = (
+                        self.recv[place + 1 - side, rows].astype(F32) + self.part[place, rows].astype(F32)
+                    ).astype(BF16)
 
             @pl.when(valid & (step > 0))
             def _():
@@ -306,12 +331,12 @@
 
             @pl.when(valid & (target != col) & jnp.logical_not(first))
             def _():
-                self.copy(side, place, self.recv.at[side]).start()
+                self.copy(side, place, None).start()
 
     def total(self, rows):
         got = self.part[self.col, rows].astype(F32)
-        got += jnp.where(self.col > 0, self.recv[0, self.col, rows].astype(F32), 0.0)
-        got += jnp.where(self.col < self.size - 1, self.recv[1, self.col, rows].astype(F32), 0.0)
+        got += jnp.where(self.col > 0, self.recv[self.col + 1, rows].astype(F32), 0.0)
+        got += jnp.where(self.col < self.size - 1, self.recv[self.col, rows].astype(F32), 0.0)
         return got
 
 
@@ -366,11 +391,13 @@
     lines[0].event(0)
     for move in smalls:
         move.start()
-    gather.start()
     moves = [
         remote(cot_ref.at[pl.ds((row ^ mask) * quarter, quarter)], got_ref.at[row], s2, r2, mask - 1, {"row": row ^ mask})
         for mask in range(1, size)
     ]
+    for move in moves:
+        move.start()
+    gather.start()
     got_ref[row] = cot_ref[pl.ds(pl.multiple_of(row * quarter, 16), quarter)]
 
     def half(ref, place):
@@ -404,15 +431,22 @@
 
         return act
 
-    act = seen(0)
+    act, act1 = seen(0), seen(1)
     act(col)
+    near = ColGather(size, zc_ref, szc, rzc, 0, 1)
     for step in range(1, size - 1):
         lines[0].event(step, act)
+    for move in moves:
+        move.wait()
+    for j in range(size):
+        zc_ref[col, :, j * width : (j + 1) * width] = got_ref[j]
+    tok_ref[...] = zc_ref[col]
+    near.event(0)
+    lines[1].event(0)
+    lines[0].event(size - 1, act)
+    act1(col)
     gather.event(0)
-    lines[0].event(size - 1, act)
-    lines[1].event(0)
-    for move in moves:
-        move.start()
+    lines[1].event(1, act1)
     for step in range(1, gather.bits):
         gather.event(step)
     for move in smalls:
@@ -436,18 +470,8 @@
     for mask in range(1, size):
         hand(0, mask).wait_recv()
         across(0, mask).start()
-    act = seen(1)
-    act(col)
-    lines[1].event(1, act)
-    for move in moves:
-        move.wait()
-    for j in range(size):
-        zc_ref[col, :, j * width : (j + 1) * width] = got_ref[j]
-    tok_ref[...] = zc_ref[col]
-    near = ColGather(size, zc_ref, szc, rzc, 0, 1)
-    near.event(0)
     for step in range(2, size):
-        lines[1].event(step, act)
+        lines[1].event(step, act1)
     for mask in range(1, size):
         hand(1, mask).wait_recv()
         across(1, mask).start()
@@ -638,9 +662,10 @@
 
 def attend_back_kernel(
     dmid_ref, weight_ref, q_ref, k_ref, v_ref, cos_ref, sin_ref, segc_ref, segr_ref,
-    attn_ref, down_ref, mid_ref,
-    dqkv_ref, inner_ref, blk_ref, line_ref, do_ref, dq_ref, dk_ref, dv_ref,
-    recv_ref, part_ref, other_ref, share_ref, s1, r1, score, rcore, srow, rrow,
+    attn_ref, down_ref, mid_ref, upshare_ref, downshare_ref,
+    dqkv_ref, inner_ref, blk_ref, line_ref, gup_ref, gdown_ref, do_ref, dq_ref, dk_ref, dv_ref,
+    recv_ref, part_ref, other_ref, share_ref, urecv_ref, drecv_ref, ustage_ref, dstage_ref,
+    s1, r1, score, rcore, srow, rrow, su, ru, sd, rd, copied, sf, rf,
 ):
     row, core = lax.axis_index("row"), lax.axis_index("dp")
     cols_n = down_ref.shape[0]
@@ -654,6 +679,12 @@
     greet(row_size=parts, col_size=cols_n, dp_size=2)
     line = ColScatter(cols_n, down_ref, recv_ref, s1, r1)
     line.event(0)
+    sums = [
+        (RowScatter(parts, upshare_ref, urecv_ref, su, ru), ustage_ref, gup_ref),
+        (RowScatter(parts, downshare_ref, drecv_ref, sd, rd), dstage_ref, gdown_ref),
+    ]
+    for scatter, _, _ in sums:
+        scatter.start()
     for j in range(parts):
         part_ref[j] = lax.dot_general(
             attn_ref[...], dmid_ref[:, j * width : (j + 1) * width], (((0,), (0,)), ((), ())), preferred_element_type=F32
@@ -702,7 +733,12 @@
             ds = (weights * (back - jnp.sum(weights * back, axis=1, keepdims=True))).astype(BF16)
             dq = jnp.dot(ds, keys, preferred_element_type=F32)
             inner_ref[rows] += jnp.sum(dq * query.astype(F32), axis=1, keepdims=True)
-            dq_ref[head, rows] = dq
+            for side in range(2):
+
+                @pl.when(lax.rem(head, 2) == side)
+                def _():
+                    dq_ref[lax.div(head, 2), rows, side * HEAD : (side + 1) * HEAD] = dq
+
             dk_ref[kv, :extent] += lax.dot_general(ds, query, (((0,), (0,)), ((), ())), preferred_element_type=F32)
 
     @pl.loop(0, length // block)
@@ -712,8 +748,11 @@
         cosine, sine = cos_ref[rows], sin_ref[rows]
         for ref, count, start, factor in ((dq_ref, heads, 0, HEAD ** (-0.5)), (dk_ref, kvs, query_cols, 1.0), (dv_ref, kvs, query_cols + key_cols, None)):
             for j in range((count + 1) // 2):
-                sides = [ref[2 * j + side, rows] if 2 * j + side < count else jnp.zeros((block, HEAD), F32) for side in range(2)]
-                part = jnp.concatenate(sides, axis=1)
+                if ref is dq_ref:
+                    part = dq_ref[j, rows]
+                else:
+                    sides = [ref[2 * j + side, rows] if 2 * j + side < count else jnp.zeros((block, HEAD), F32) for side in range(2)]
+                    part = jnp.concatenate(sides, axis=1)
                 if factor is not None:
                     part = (part * cosine - turn(part * sine, low)) * factor
                 dqkv_ref[rows, start + 128 * j : start + 128 * (j + 1)] = part.astype(BF16)
@@ -722,15 +761,42 @@
             more += jnp.sum(dk_ref[kv, rows] * k_ref[kv, rows].astype(F32) + dv_ref[kv, rows] * v_ref[kv, rows].astype(F32), axis=1, keepdims=True)
         inner_ref[rows] += more
 
-    for time in range(2, line.times):
+    def finish(stage):
+        def act(rows, total):
+            stage[rows] = total
+
+        return act
+
+    if cols_n > 2:
+        line.event(2)
+    bits = sums[0][0].bits
+    for step in range(bits - 1):
+        for scatter, stage, _ in sums:
+            scatter.event(step, finish(stage))
+    for time in range(3, line.times):
         line.event(time)
-    for j in range(parts):
-        columns = slice(j * width, (j + 1) * width)
-        blk_ref[j] = (mid_ref[:, columns] + line.total(slice(None))[:, columns]).astype(BF16)
+    results = []
+    for k, (scatter, stage, out) in enumerate(sums):
+        scatter.event(bits - 1, finish(stage))
+        moves = settle(stage, out, core, copied, sf, rf, k)
+        for move in moves:
+            move.start()
+        results += moves
+        scatter.close()
+
+    @pl.loop(0, mid_ref.shape[0] // 64)
+    def _(i):
+        rows = pl.ds(pl.multiple_of(i * 64, 16), 64)
+        total = mid_ref[rows] + line.total(rows)
+        for j in range(parts):
+            blk_ref[j, rows] = total[:, j * width : (j + 1) * width].astype(BF16)
+
     row_moves(parts, share_ref, line_ref, srow, rrow, 0, False)
-
-
-def attend_back_call(dmid, weight, q, k, v, cosine, sine, segc, segr, columns, attn, down, middle):
+    for move in results:
+        move.wait()
+
+
+def attend_back_call(dmid, weight, q, k, v, cosine, sine, segc, segr, columns, attn, down, middle, upshare, downshare):
     rows_n, cols_n = lax.axis_size("row"), lax.axis_size("col")
     _, heads_cols, width = weight.shape
     quarter = middle.shape[0]
@@ -744,23 +810,33 @@
             jax.ShapeDtypeStruct((length, 1), F32),
             jax.ShapeDtypeStruct((rows_n, quarter, width), BF16),
             jax.ShapeDtypeStruct((rows_n, heads_cols // 2, width), BF16),
+            jax.ShapeDtypeStruct((2 * upshare.shape[1], upshare.shape[2]), F32),
+            jax.ShapeDtypeStruct((2 * downshare.shape[1], downshare.shape[2]), F32),
         ),
-        in_specs=[VM] * 12,
-        out_specs=(VM,) * 4,
+        in_specs=[VM] * 14,
+        out_specs=(VM,) * 4 + (pl.BlockSpec(memory_space=pl.ANY),) * 2,
         scratch_shapes=[
             pltpu.VMEM((heads, length, HEAD), BF16),
-            pltpu.VMEM((heads, length, HEAD), F32),
+            pltpu.VMEM(((heads + 1) // 2, length, 2 * HEAD), F32),
             pltpu.VMEM((kvs, length, HEAD), F32),
             pltpu.VMEM((kvs, length, HEAD), F32),
-            pltpu.VMEM((2,) + down.shape, BF16),
+            pltpu.VMEM((down.shape[0] + 1,) + down.shape[1:], BF16),
             pltpu.VMEM(weight.shape, BF16),
             pltpu.VMEM((rows_n, heads_cols // 2, width), BF16),
             pltpu.VMEM((rows_n, heads_cols // 2, width), BF16),
+            pltpu.VMEM((rows_n - 1,) + upshare.shape[1:], BF16),
+            pltpu.VMEM((rows_n - 1,) + downshare.shape[1:], BF16),
+            pltpu.VMEM(upshare.shape[1:], F32),
+            pltpu.VMEM(downshare.shape[1:], F32),
             dma((2,)), dma((2 * cols_n,)), dma((1,)), dma((1,)), dma((rows_n - 1,)), dma((rows_n - 1,)),
+        ]
+        + [dma((2 * (rows_n - 1),))] * 4
+        + [dma((2,))] * 3
+        + [
         ],
         compiler_params=params(5),
         cost_estimate=cost(80),
-    )(dmid, weight, q, k, v, cosine, sine, segc, segr, attn, down, middle)
+    )(dmid, weight, q, k, v, cosine, sine, segc, segr, attn, down, middle, upshare, downshare)
 
 
 def middle_kernel(
@@ -848,24 +924,95 @@
     )(attn, weight, x, gain, tok, near, following, up, down)
 
 
-def back_kernel(rows_n, cols_n, dgate_ref, dup_ref, gate_ref, up_ref, mid_ref, tok_ref, gain_ref, dmid_ref, grad_ref, part_ref, recv_ref, s1, r1, s2, r2):
-    row, col = lax.axis_index("row"), lax.axis_index("col")
+def settle(stage, out, core, copied, sends, recvs, place):
+    rows = pl.ds(pl.multiple_of(core * stage.shape[0], 8), stage.shape[0])
+    return (
+        pltpu.make_async_copy(stage, out.at[rows], copied.at[place]),
+        remote(stage, out.at[rows], sends, recvs, place, {"dp": 1 - core}),
+    )
+
+
+def back_kernel(
+    rows_n, cols_n, dgate_ref, dup_ref, gate_ref, up_ref, mid_ref, tok_ref, gain_ref, second_ref,
+    dmid_ref, grad_ref, ggate_ref, share_ref,
+    w0_ref, w1_ref, part_ref, recv_ref, other_ref, grecv_ref, stage_ref,
+    loads, s1, r1, s2, r2, sg, rg, score, rcore, copied, sf, rf, free,
+):
+    row, col, core = lax.axis_index("row"), lax.axis_index("col"), lax.axis_index("dp")
     quarter, features = mid_ref.shape
-    greet(row_size=rows_n, col_size=cols_n)
+    width = features // rows_n
+    hidden = dgate_ref.shape[1]
+    share = width // 2
+    moves = [pltpu.make_async_copy(ref, kept, loads.at[k]) for k, (ref, kept) in enumerate(((gate_ref, w0_ref), (up_ref, w1_ref)))]
+    for move in moves:
+        move.start()
+    greet(row_size=rows_n, col_size=cols_n, dp_size=2)
+    for move in moves:
+        move.wait()
 
     def prepare(target):
-        tile = 512
-
-        @pl.loop(0, features // tile)
+        rows = pl.ds(pl.multiple_of(target * quarter, 16), quarter)
+
+        @pl.loop(0, rows_n)
         def _(i):
-            columns = pl.ds(i * tile, tile)
-            value = lax.dot_general(dgate_ref[target], gate_ref[columns], (((1,), (1,)), ((), ())), preferred_element_type=F32)
-            value += lax.dot_general(dup_ref[target], up_ref[columns], (((1,), (1,)), ((), ())), preferred_element_type=F32)
+            columns = pl.ds(pl.multiple_of(i * width, 128), width)
+            value = lax.dot_general(dgate_ref[rows], w0_ref[i], (((1,), (1,)), ((), ())), preferred_element_type=F32)
+            value += lax.dot_general(dup_ref[rows], w1_ref[i], (((1,), (1,)), ((), ())), preferred_element_type=F32)
             part_ref[target, :, columns] = value.astype(BF16)
 
+    tile = min(512, hidden)
+
+    def product(right, kept):
+        @pl.loop(0, rows_n)
+        def _(i):
+            for t in range(hidden // tile):
+                columns = slice(t * tile, (t + 1) * tile)
+                kept[i, :, columns] = lax.dot_general(
+                    second_ref[:, pl.ds(pl.multiple_of(i * width, 128), width)], right[:, columns], (((0,), (0,)), ((), ())),
+                    preferred_element_type=F32,
+                ).astype(BF16)
+
+    def add(kept):
+        @pl.loop(0, rows_n)
+        def _(i):
+            rows = pl.ds(pl.multiple_of(core * share, 16), share)
+            kept[i, rows] = (kept[i, rows].astype(F32) + other_ref[i].astype(F32)).astype(BF16)
+
     line = ColScatter(cols_n, part_ref, recv_ref, s1, r1)
-    for time in range(line.times):
-        line.event(time, prepare)
+    prepare(cols_n - 1)
+    prepare(0)
+    line.event(0)
+    for target in range(1, cols_n - 1):
+        prepare(target)
+    cross = [
+        remote(kept.at[:, pl.ds(pl.multiple_of((1 - core) * share, 16), share)], other_ref, score, rcore, k, {"dp": 1 - core})
+        for k, kept in enumerate((w0_ref, w1_ref))
+    ]
+    product(dgate_ref, w0_ref)
+    cross[0].start()
+    line.event(1)
+    product(dup_ref, w1_ref)
+    cross[0].wait()
+    add(w0_ref)
+    pl.semaphore_signal(free, inc=1, device_id={"dp": 1 - core}, device_id_type=MESH)
+    scatter = RowScatter(rows_n, w0_ref, grecv_ref, sg, rg, core * share)
+    scatter.start()
+    pl.semaphore_wait(free, 1)
+    cross[1].start()
+    if cols_n > 2:
+        line.event(2)
+    cross[1].wait()
+    add(w1_ref)
+    keep = pltpu.make_async_copy(w1_ref.at[:, pl.ds(pl.multiple_of(core * share, 16), share)], share_ref, copied.at[1])
+    keep.start()
+
+    def finish(rows, total):
+        stage_ref[rows] = total
+
+    for step in range(scatter.bits - 1):
+        scatter.event(step, finish)
+    for time in range(3, line.times):
+        line.event(time)
 
     grad_ref[...] = jnp.zeros_like(grad_ref)
 
@@ -883,29 +1030,51 @@
 
     gather = RowGather(rows_n, dmid_ref, s2, r2)
     gather.start()
+    scatter.event(scatter.bits - 1, finish)
+    results = settle(stage_ref, ggate_ref, core, copied, sf, rf, 0)
+    for move in results:
+        move.start()
     gather.run()
-
-
-def back_call(dgate, dup, gate, up, middle, tok, gain):
+    scatter.close()
+    keep.wait()
+    for move in results:
+        move.wait()
+
+
+def back_call(dgate, dup, gate, up, middle, tok, gain, second):
     rows_n, cols_n = lax.axis_size("row"), lax.axis_size("col")
     quarter, features = middle.shape
-    hidden = gate.shape[1]
+    hidden = dgate.shape[1]
+    width = features // rows_n
+    dma = pltpu.SemaphoreType.DMA
+    anywhere = pl.BlockSpec(memory_space=pl.ANY)
+    line = 2 * (rows_n - 1)
+    half = (rows_n, width // 2, hidden)
     return pl.pallas_call(
         functools.partial(back_kernel, rows_n, cols_n),
         out_shape=(
             jax.ShapeDtypeStruct((rows_n, quarter, features), BF16),
             jax.ShapeDtypeStruct((1, features), F32),
+            jax.ShapeDtypeStruct((width, hidden), F32),
+            jax.ShapeDtypeStruct(half, BF16),
         ),
-        in_specs=[VM] * 7,
-        out_specs=(VM,) * 2,
+        in_specs=[VM, VM, anywhere, anywhere, VM, VM, VM, VM],
+        out_specs=(VM, VM, anywhere, anywhere),
         scratch_shapes=[
+            pltpu.VMEM((rows_n, width, hidden), BF16),
+            pltpu.VMEM((rows_n, width, hidden), BF16),
             pltpu.VMEM((cols_n, quarter, features), BF16),
-            pltpu.VMEM((2, cols_n, quarter, features), BF16),
-        ]
-        + [pltpu.SemaphoreType.DMA((2,)), pltpu.SemaphoreType.DMA((2 * cols_n,))]
-        + [pltpu.SemaphoreType.DMA((2 * (rows_n - 1),))] * 2,
+            pltpu.VMEM((cols_n + 1, quarter, features), BF16),
+            pltpu.VMEM(half, BF16),
+            pltpu.VMEM((rows_n - 1,) + half[1:], BF16),
+            pltpu.VMEM(half[1:], F32),
+            dma((2,)), dma((2,)), dma((2 * cols_n,)),
+            dma((line,)), dma((line,)), dma((line,)), dma((line,)),
+            dma((2,)), dma((2,)), dma((2,)), dma((1,)), dma((1,)), pltpu.SemaphoreType.REGULAR,
+        ],
         compiler_params=params(3),
-    )(dgate.reshape(cols_n, quarter, hidden), dup.reshape(cols_n, quarter, hidden), gate, up, middle, tok, gain)
+        cost_estimate=cost(130),
+    )(dgate, dup, gate, up, middle, tok, gain, second)
 
 
 def last_kernel(
@@ -984,8 +1153,8 @@
 
     for step in range(scatter.bits - 1):
         scatter.event(step, finish)
-    qline.event(1)
-    qline.event(2)
+    for time in range(1, min(3, qline.times)):
+        qline.event(time)
     scatter.event(scatter.bits - 1, finish)
     scatter.close()
     for move in small:
@@ -1036,8 +1205,8 @@
             pltpu.VMEM((size, width // 2, columns), BF16),
             pltpu.VMEM((size, width // 2, columns), BF16),
             pltpu.VMEM((size, width // 2, columns), BF16),
-            pltpu.VMEM((2, size, width // 2, columns), BF16),
-            pltpu.VMEM((2, size, heads_cols // 2, width), BF16),
+            pltpu.VMEM((size + 1, width // 2, columns), BF16),
+            pltpu.VMEM((size + 1, heads_cols // 2, width), BF16),
             pltpu.VMEM((size, 1, width), F32),
             pltpu.VMEM((2, 1, width), F32),
             pltpu.VMEM((2 * size, 2, 1, width), F32),
@@ -1056,35 +1225,127 @@
     )(dqkv, weight.reshape(size, width, columns), first, outline, blk, inner, activations, inv1, grad2.reshape(size, 1, width))
 
 
-def weight_grads_kernel(second_ref, cot_ref, dgate_ref, dup_ref, hidden_ref, out_ref):
-    which, part = pl.program_id(0), pl.program_id(1)
-    span = out_ref.shape[2]
-    columns = pl.ds(pl.multiple_of(part * span, 128), span)
-    for index, left, right in ((0, second_ref, dgate_ref), (1, second_ref, dup_ref), (2, cot_ref, hidden_ref)):
-
-        @pl.when(which == index)
+def feed_kernel(
+    second_ref, cot_ref, gate_ref, up_ref, down_ref, dgate_ref, dup_ref, own_ref, part_ref,
+    hidden_ref, keep_ref, send_ref, other_ref, sends, recvs,
+):
+    core = lax.axis_index("dp")
+    step = pl.program_id(0)
+    rows_n, tile, width = down_ref.shape
+    tokens = second_ref.shape[0]
+    tiles = hidden_ref.shape[0]
+    block = min(512, tokens)
+    mine = tiles // 2
+
+    def place(t):
+        return pl.ds(pl.multiple_of(lax.rem(t, mine) * tile, tile), tile)
+
+    def give(t):
+        return remote(send_ref.at[:, place(t)], other_ref.at[:, place(t)], sends, recvs, lax.rem(t, mine), {"dp": 1 - core})
+
+    @pl.when(step == 0)
+    def _():
+        greet(dp_size=2)
+
+    @pl.when(step < tiles)
+    def _():
+        keep_ref[step] = down_ref[...]
+
+        @pl.loop(0, tokens // block)
+        def _(i):
+            rows = pl.ds(pl.multiple_of(i * block, block), block)
+            gate = jnp.dot(second_ref[rows], gate_ref[...], preferred_element_type=F32)
+            up = jnp.dot(second_ref[rows], up_ref[...], preferred_element_type=F32)
+            back = jnp.zeros((block, tile), F32)
+            for j in range(rows_n):
+                back += lax.dot_general(
+                    cot_ref[rows, j * width : (j + 1) * width], down_ref[j], (((1,), (1,)), ((), ())), preferred_element_type=F32
+                )
+            sigma = jax.nn.sigmoid(gate)
+            swish = gate * sigma
+            hidden_ref[step, rows] = (swish * up).astype(BF16)
+            dgate_ref[rows] = (back * up * (sigma * (1.0 + gate * (1.0 - sigma)))).astype(BF16)
+            dup_ref[rows] = (back * swish).astype(BF16)
+
+        for j in range(rows_n):
+            value = lax.dot_general(
+                hidden_ref[step], cot_ref[:, j * width : (j + 1) * width], (((0,), (0,)), ((), ())), preferred_element_type=F32
+            ).astype(BF16)
+
+            @pl.when(lax.div(step, mine) == core)
+            def _():
+                own_ref[j, place(step)] = value
+
+            @pl.when(lax.div(step, mine) != core)
+            def _():
+                send_ref[j, place(step)] = value
+
+        @pl.when(lax.div(step, mine) != core)
         def _():
-            out_ref[0, 0] = lax.dot_general(
-                left[:, columns], right[...], (((0,), (0,)), ((), ())), preferred_element_type=F32
-            ).astype(BF16)
-
-
-def weight_grads_call(second, cot, dgate, dup, hidden):
-    parts = 2 * lax.axis_size("row")
-    span, columns = second.shape[1] // parts, hidden.shape[1]
+            give(step).start()
+
+    @pl.when(step >= tiles)
+    def _():
+        quarter = part_ref.shape[1]
+        rows = pl.ds(pl.multiple_of((step - tiles) * quarter, quarter), quarter)
+        for j in range(rows_n):
+            total = jnp.zeros((quarter, width), F32)
+            for t in range(tiles):
+                total += jnp.dot(hidden_ref[t, rows], keep_ref[t, j], preferred_element_type=F32)
+            part_ref[0, :, j * width : (j + 1) * width] = total.astype(BF16)
+
+    @pl.when(step == pl.num_programs(0) - 1)
+    def _():
+        for t in range(mine):
+            give(t).wait()
+            for j in range(rows_n):
+                own_ref[j, place(t)] = (own_ref[j, place(t)].astype(F32) + other_ref[j, place(t)].astype(F32)).astype(BF16)
+
+
+def feed_call(second, cot, gate, up, down):
+    rows_n, hidden, width = down.shape
+    cols_n = lax.axis_size("col")
+    tokens, features = second.shape
+    tile = 256
+    tiles = hidden // tile
+    half = (rows_n, hidden // 2, width)
+
+    def place(i):
+        return jnp.minimum(i, tiles - 1)
+
     return pl.pallas_call(
-        weight_grads_kernel,
-        grid=(3, parts),
-        out_shape=jax.ShapeDtypeStruct((parts, 3, span, columns), BF16),
-        in_specs=[VM] * 5,
-        out_specs=pl.BlockSpec((1, 1, span, columns), lambda g, p: (p, g, 0, 0)),
-        compiler_params=pltpu.CompilerParams(vmem_limit_bytes=VMEM_LIMIT),
-        cost_estimate=cost(30),
-    )(second, cot, dgate, dup, hidden)
-
-
-def dot(left, right, dims):
-    return lax.dot_general(left, right, (dims, ((), ())), preferred_element_type=F32)
+        feed_kernel,
+        grid=(tiles + cols_n,),
+        out_shape=(
+            jax.ShapeDtypeStruct((tokens, hidden), BF16),
+            jax.ShapeDtypeStruct((tokens, hidden), BF16),
+            jax.ShapeDtypeStruct(half, BF16),
+            jax.ShapeDtypeStruct((cols_n, tokens // cols_n, features), BF16),
+        ),
+        in_specs=[
+            VM,
+            VM,
+            pl.BlockSpec((features, tile), lambda i: (0, place(i))),
+            pl.BlockSpec((features, tile), lambda i: (0, place(i))),
+            pl.BlockSpec((rows_n, tile, width), lambda i: (0, place(i), 0)),
+        ],
+        out_specs=(
+            pl.BlockSpec((tokens, tile), lambda i: (0, place(i))),
+            pl.BlockSpec((tokens, tile), lambda i: (0, place(i))),
+            VM,
+            pl.BlockSpec((1, tokens // cols_n, features), lambda i: (jnp.maximum(i - tiles, 0), 0, 0)),
+        ),
+        scratch_shapes=[
+            pltpu.VMEM((tiles, tokens, tile), BF16),
+            pltpu.VMEM((tiles, rows_n, tile, width), BF16),
+            pltpu.VMEM(half, BF16),
+            pltpu.VMEM(half, BF16),
+            pltpu.SemaphoreType.DMA((tiles // 2,)),
+            pltpu.SemaphoreType.DMA((tiles // 2,)),
+        ],
+        compiler_params=params(7),
+        cost_estimate=cost(50),
+    )(second, cot, gate, up, down)
 
 
 def rotary_tables(positions):
@@ -1093,10 +1354,6 @@
     phase = positions[:, None] * inverse[None, :]
     phase = jnp.concatenate([phase] * (2 * 128 // HEAD), axis=1)
     return (jnp.cos(phase), jnp.sin(phase))
-
-
-def gather(values, axis_name, axis=0):
-    return lax.all_gather(values, axis_name, axis=axis, tiled=True)
 
 
 def local(
@@ -1131,28 +1388,14 @@
     )
     gate_all, up_all = gate_all.reshape(features, hidden_cols), up_all.reshape(features, hidden_cols)
     second_all, cot_all = second_all.reshape(-1, features), cot_all.reshape(-1, features)
-    gate = dot(second_all, gate_all, ((1,), (0,)))
-    up = dot(second_all, up_all, ((1,), (0,)))
-    sigma = jax.nn.sigmoid(gate)
-    swish = gate * sigma
-    hidden = (swish * up).astype(BF16)
-    tokens = hidden.shape[0]
-    down_part = lax.dot_general(hidden, down_all, (((1,), (1,)), ((), ())), preferred_element_type=F32).reshape(tokens, features)
-    down_part = down_part.astype(BF16).reshape(-1, middle.shape[0], features)
-
-    cot_split = cot_all.reshape(tokens, rows, width)
-    dhidden = lax.dot_general(cot_split, down_all, (((1, 2), (0, 2)), ((), ())), preferred_element_type=F32)
-    swish_grad = sigma * (1.0 + gate * (1.0 - sigma))
-    dgate = (dhidden * up * swish_grad).astype(BF16)
-    dup = (dhidden * swish).astype(BF16)
-    grads = weight_grads_call(second_all, cot_all, dgate, dup, hidden)
-    grads, dgate, dup = lax.optimization_barrier((grads, dgate, dup))
-    grads = lax.psum_scatter(grads.reshape(-1, hidden_cols), ("row", "dp"), scatter_dimension=0, tiled=True)
-    dmid_all, gain2_grad = back_call(dgate, dup, gate_all, up_all, middle, cot_tok, gain2)
+    dgate, dup, down_share, down_part = feed_call(second_all, cot_all, gate_all, up_all, down_all)
+    dmid_all, gain2_grad, gate_grad, up_share = back_call(
+        dgate, dup, gate_all.reshape(rows, width, hidden_cols), up_all.reshape(rows, width, hidden_cols), middle, cot_tok, gain2, second_all
+    )
     dmid_all = dmid_all.reshape(length, features)
 
-    dqkv, inner1, blk, outline = attend_back_call(
-        dmid_all, out_all_w, q, k, v, cosine, sine, segc, segr, qkv_cols, attn, down_part, middle
+    dqkv, inner1, blk, outline, up_grad, down_grad = attend_back_call(
+        dmid_all, out_all_w, q, k, v, cosine, sine, segc, segr, qkv_cols, attn, down_part, middle, up_share, down_share
     )
     dfirst, block_out, inner1, gains, qkv_grad, out_grad = last_call(
         dqkv, qkv_all, first, outline, blk, inner1.reshape(-1, 128), activations, inv1, gain2_grad
@@ -1162,8 +1405,6 @@
     dmid_own = lax.dynamic_slice_in_dim(dmid_all, row * width, width, 1).astype(F32)
     input_grad = dmid_own + inv1 * first_gain[None] * dfirst - own_x * (inv1 * inv1 * inv1 * inner1)
 
-    grads, dfirst = lax.optimization_barrier((grads, dfirst))
-    grads = gather(grads.reshape(1, 3, -1, hidden_cols), "dp").astype(F32)
     return (
         block_out,
         input_grad,
@@ -1173,9 +1414,9 @@
         qkv_grad[:, query_cols + key_span : query_cols + key_span + key_cols],
         out_grad,
         gains[1, 0],
-        grads[:, 0].reshape(width, hidden_cols),
-        grads[:, 1].reshape(width, hidden_cols),
-        grads[:, 2].reshape(width, hidden_cols).T,
+        gate_grad,
+        up_grad,
+        down_grad,
     )
 
 

time: 809 us -> 707 us (0.87)
  matrix products: 58.4 us -> 0 us
  local copies, waits for them, and re-layouts: 45.8 us -> 18.4 us
  between operations: 14.7 us -> 1.24 us
    dot_general x4 -> x0, matrix products: 58.4 us -> none  [the longest x2 30.4 us: dot(): lax.dot_general(left, right, (dims, ((), ())), preferred_element_type=F32)]
    pallas_call x1, Pallas kernels: 162 us -> 132 us  [back_call(): pl.pallas_call(functools.partial(back_kernel, rows_n, cols_n), out_shape=...]
    pallas_call x1, Pallas kernels: 40.1 us -> 64.6 us  [feed_call(): pl.pallas_call(feed_kernel, grid=(tiles + cols_n,), out_shape=(jax.ShapeD...]
    pallas_call x1, Pallas kernels: 79.5 us -> 96.2 us  [attend_back_call(): pl.pallas_call(attend_back_kernel, out_shape=(jax.ShapeDtypeStruct((lengt...]
    pallas_call x1, Pallas kernels: 111 us -> 95.7 us  [first_call(): pl.pallas_call(functools.partial(first_kernel, size), out_shape=(jax.Shap...]
    convert_element_type x2 -> x0, local copies, waits for them, and re-layouts: 14.2 us -> none  [local(): down_part = down_part.astype(BF16).reshape(-1, middle.shape[0], features)]
    another operation x2 -> x0, local copies, waits for them, and re-layouts: 13.3 us -> none  [the longest x1 7.81 us: local(): cot_split = cot_all.reshape(tokens, rows, width)]
    unnamed x23 -> x28, local copies, waits for them, and re-layouts: 3.4 us -> 13.9 us
  transfers between devices with their start and end apart: 2 -> 0, of which waited for: 1 -> 0; matrix products, arithmetic and copies ran while one was open for 5% -> 0% of each run, Pallas kernels for 41% -> 0%
where the time goes in v4:
time: 707 us; the launch traced here: 701 us
  Pallas kernels  666 us (94%)
  local copies, waits for them, and re-layouts  18.4 us (3%)
  other arithmetic  14.8 us (2%)
    pallas_call x1, Pallas kernels, back_call(): pl.pallas_call(functools.partial(back_kernel, rows_n, cols_n), out_shape=...  132 us
    pallas_call x1, Pallas kernels, middle_call(): pl.pallas_call(functools.partial(middle_kernel, rows_n, cols_n), out_shap...  129 us
    pallas_call x1, Pallas kernels, attend_back_call(): pl.pallas_call(attend_back_kernel, out_shape=(jax.ShapeDtypeStruct((lengt...  96.2 us
    pallas_call x1, Pallas kernels, first_call(): pl.pallas_call(functools.partial(first_kernel, size), out_shape=(jax.Shap...  95.7 us
    pallas_call x1, Pallas kernels, last_call(): pl.pallas_call(functools.partial(last_kernel, size), out_shape=(jax.Shape...  90.7 us
    pallas_call x1, Pallas kernels, feed_call(): pl.pallas_call(feed_kernel, grid=(tiles + cols_n,), out_shape=(jax.ShapeD...  64.6 us
    pallas_call x1, Pallas kernels, attend_call(): pl.pallas_call(functools.partial(attend_kernel, size), out_shape=(jax.Sha...  57.5 us

profile of v4, /device:TPU:0, one launch (start us, length us, event | category | flops | bytes accessed | tf_op | source)
XLA Modules:
  0.0 700.7 jit_solution(9115413835703768607)
XLA Ops:
  0.7 0.7 convert_element_type.19
  1.4 0.7 convert_element_type.20
  2.0 1.3 maximum_bitcast_fusion.small_ref
  3.3 2.1 pad_maximum_fusion.qkv_ref
  5.5 95.7 %shard_map.212 = (bf16[4,1024,512]{2,1,0:T(8,128)(2,1)}, bf16[1024,2048]{1,0:T(8,128)(2,1)}, f32[1024,1]{1,0:T(8,128)}, bf16[256,2048]{1,0:T(8,128)(2,1)}, f32[4...) custom-call(bf16[1024,512]{1,0:T(8,128)(2,1)} %act_ref.3, ...), custom_call_target="tpu_custom_call" | custom-call | tf_op jit(solution)/shard_map/pallas_call | solution.py:497
  101.2 0.8 copy.30
  102.0 0.1 constant_dynamic-slice_fusion
  102.1 0.0 copy-start.8
  102.1 0.6 copy.28
  102.7 0.2 broadcast_multiply_fusion
  102.9 1.0 copy.24.segc_ref
  103.9 2.9 fusion.2
  106.9 0.0 copy-done.8
  106.9 57.5 %shard_map.213 = (bf16[8,1024,64]{2,1,0:T(8,128)(2,1)}, bf16[2,1024,64]{2,1,0:T(8,128)(2,1)}, bf16[2,1024,64]{2,1,0:T(8,128)(2,1)}, bf16[1024,512]{1,0:T(8,128)(...) custom-call(bf16[1024,2048]{1,0:T(8,128)(2,1)} %get-tuple-element.50.first_ref, ...), custom_call_target="tpu_custom_call" | custom-call | flops 44999999488 | bytes 1048576 | tf_op jit(solution)/shard_map/pallas_call | solution.py:603
  164.4 129.0 %shard_map.214 = (f32[256,2048]{1,0:T(8,128)}, bf16[4,256,2048]{2,1,0:T(8,128)(2,1)}, bf16[4,256,2048]{2,1,0:T(8,128)(2,1)}, bf16[4,512,2048]{2,1,0:T(8,128)(2,1)}, bf16[4,2048,512]{2,1,0:T(8,128)(2,1)}) custom-call(bf16[1024,512]{1,0:T(8,128)(2,1)} %get-tuple-element.54.attn_ref, bf16[4,512,512]{2,1,0:T(8,128)(2,1)} %get-tuple-element.55.weight_ref, ...), custom_call_target="tpu_custom_call" | custom-call | flops 130000003072 | bytes 1048576 | tf_op jit(solution)/shard_map/pallas_call | solution.py:904
  293.4 64.6 %shard_map.215 = (bf16[1024,2048]{1,0:T(8,128)(2,1)}, bf16[1024,2048]{1,0:T(8,128)(2,1)}, bf16[4,1024,512]{2,1,0:T(8,128)(2,1)}, bf16[4,256,2048]{2,1,0:T(8,128)(2,1)}) custom-call(bf16[1024,2048]{1,0:T(8,128)(2,1)} %bitcast.39, bf16[1024,2048]{1,0:T(8,128)(2,1)} %bitcast.41, bf16[2048,2048]{1,0:T(8,128)(2,1)} %bitcast.37, bf16[2048,2048]{1,0:T(8,128)(2,1)} %bitcast.38, ...), custom_call_target="tpu_custom_call" | custom-call | flops 49999998976 | bytes 1048576 | tf_op jit(solution)/shard_map/pallas_call | solution.py:1316
  358.0 132.4 %shard_map.216 = (bf16[4,256,2048]{2,1,0:T(8,128)(2,1)}, f32[1,2048]{1,0:T(1,128)}, f32[512,2048]{1,0:T(8,128)}, bf16[4,256,2048]{2,1,0:T(8,128)(2,1)}) custom-call(bf16[1024,2048]{1,0:T(8,128)(2,1)} %get-tuple-element.64.dgate_ref, bf16[1024,2048]{1,0:T(8,128)(2,1)} %get-tuple-element.65.dup_ref, bf16[4,512,2048]{2,1,0:T(8,128)(2,1)} %get-tuple-element.61.gate_ref, ...), custom_call_target="tpu_custom_call" | custom-call | flops 130000003072 | bytes 1048576 | tf_op jit(solution)/shard_map/pallas_call | solution.py:1053
  490.4 96.2 %shard_map.217 = (bf16[1024,768]{1,0:T(8,128)(2,1)}, f32[1024,1]{1,0:T(8,128)}, bf16[4,256,512]{2,1,0:T(8,128)(2,1)}, bf16[4,256,512]{2,1,0:T(8,128)(2,1)}, f32[512,2048]{1,0:T(8,128)}, /*index=5*/f32[2048,512]{1,0:T(8,128)}) custom-call(bf16[1024,2048]{1,0:T(8,128)(2,1)} %bitcast.23, bf16[4,512,512]{2,1,0:T(8,128)(2,1)} %get-tuple-element.55.weight_ref, ...), custom_call_target="tpu_custom_call" | custom-call | flops 80000000000 | bytes 1048576 | tf_op jit(solution)/shard_map/pallas_call | solution.py:806
  586.7 1.8 reduce
  588.5 0.0 copy-start.7
  588.5 0.0 copy-start.9
  588.5 90.7 %shard_map.218 = (f32[1024,512]{1,0:T(8,128)}, bf16[1024,512]{1,0:T(8,128)(2,1)}, f32[4,8,128]{2,1,0:T(8,128)}, f32[2,1,512]{2,1,0:T(1,128)}, f32[512,768]{1,0:T(8,128)}, /*index=5*/f32[512,512]{1,0:T(8,128)}) custom-call(bf16[1024,768]{1,0:T(8,128)(2,1)} %get-tuple-element.74.dqkv_ref, bf16[4,512,768]{2,1,0:T(8,128)(2,1)} %get-tuple-element.51.weight_ref, ...), custom_call_target="tpu_custom_call" | custom-call | flops 80000000000 | bytes 1048576 | tf_op jit(solution)/shard_map/pallas_call | solution.py:1189
  679.3 0.0 copy-start.3
  679.3 0.8 reduce_sum.9
  680.1 1.3 fusion.6
  681.4 0.2 copy.26
  681.6 0.0 copy-done.7
  681.6 0.3 fusion.4
  682.0 0.0 copy-done.9
  682.0 0.0 copy-done.3
  682.0 0.0 copy-start.4
  682.0 3.9 multiply_subtract_fusion
  685.8 0.0 copy-done.4
  685.8 0.0 copy-start.6
  685.8 0.8 fusion.5
  686.7 0.0 copy-start.5
  686.7 1.1 slice.30
  687.8 0.0 copy-start
  687.8 0.0 copy-done.6
  687.8 1.0 copy.36
  688.7 0.0 copy-done.5
  688.7 1.0 copy.37
  689.7 1.1 copy-done
  690.8 2.1 copy.38
  692.9 1.6 copy-done.2
  694.5 2.1 copy.39
  696.6 1.6 copy-done.1
  698.2 2.0 copy.40
  (4 shorter events, 0.0 us)
Async XLA Ops:
  102.1 4.8 copy-start.8
  588.5 93.1 %copy-start.7 = (f32[1024,1]{1,0:T(8,128)S(1)}, f32[1024,1]{1,0:T(8,128)}, u32[]{:S(2)}) copy-start(f32[1024,1]{1,0:T(8,128)} %get-tuple-element.78.inv_ref) | copy-start | bytes 12292
  588.5 93.4 %copy-start.9 = (f32[512]{0:T(512)S(1)}, f32[512]{0:T(512)}, u32[]{:S(2)}) copy-start(f32[512]{0:T(512)} %param.16) | copy-start | bytes 6148
  679.3 2.7 copy-start.3
  682.0 3.9 copy-start.4
  685.8 1.9 copy-start.6
  686.7 2.1 copy-start.5
  687.8 3.0 copy-start
  690.8 3.7 copy-start.2
  694.5 3.7 copy-start.1

commit v5 on v4

--- a/solution.py
+++ b/solution.py
@@ -280,16 +280,19 @@
 
 
 class ColScatter:
-    def __init__(self, size, part, recv, sends, recvs):
+    def __init__(self, size, part, recv, sends, recvs, begin=0, count=None, first=0):
         self.size, self.part, self.recv, self.sends, self.recvs = size, part, recv, sends, recvs
+        self.begin, self.count, self.first = begin, count or part.shape[1], first
         self.col = lax.axis_index("col")
         self.times = size
 
     def copy(self, side, target, source):
         step = 1 if side == 0 else self.size - 1
+        rows = pl.ds(self.begin, self.count)
         return pltpu.make_async_remote_copy(
-            src_ref=self.recv.at[target + 1 - side] if source is None else source.at[target], dst_ref=self.recv.at[target + 1 - side], send_sem=self.sends.at[side],
-            recv_sem=self.recvs.at[side * self.size + target],
+            src_ref=self.recv.at[target + 1 - side, rows] if source is None else source.at[target, rows],
+            dst_ref=self.recv.at[target + 1 - side, rows], send_sem=self.sends.at[2 * self.first + side],
+            recv_sem=self.recvs.at[(2 * self.first + side) * self.size + target],
             device_id={"col": lax.rem(self.col + step, self.size)}, device_id_type=MESH,
         )
 
@@ -312,11 +315,11 @@
 
             @pl.when(valid & jnp.logical_not(first) & (target != col))
             def _():
-                chunk = min(64, self.part.shape[1])
-
-                @pl.loop(0, self.part.shape[1] // chunk)
+                chunk = min(64, self.count)
+
+                @pl.loop(0, self.count // chunk)
                 def _(i):
-                    rows = pl.ds(pl.multiple_of(i * chunk, 16), chunk)
+                    rows = pl.ds(pl.multiple_of(self.begin + i * chunk, 16), chunk)
                     self.recv[place + 1 - side, rows] = (
                         self.recv[place + 1 - side, rows].astype(F32) + self.part[place, rows].astype(F32)
                     ).astype(BF16)
@@ -662,8 +665,8 @@
 
 def attend_back_kernel(
     dmid_ref, weight_ref, q_ref, k_ref, v_ref, cos_ref, sin_ref, segc_ref, segr_ref,
-    attn_ref, down_ref, mid_ref, upshare_ref, downshare_ref,
-    dqkv_ref, inner_ref, blk_ref, line_ref, gup_ref, gdown_ref, do_ref, dq_ref, dk_ref, dv_ref,
+    attn_ref, down_ref, mid_ref, upshare_ref, gateshare_ref,
+    dqkv_ref, inner_ref, blk_ref, line_ref, gup_ref, ggate_ref, do_ref, dq_ref, dk_ref, dv_ref,
     recv_ref, part_ref, other_ref, share_ref, urecv_ref, drecv_ref, ustage_ref, dstage_ref,
     s1, r1, score, rcore, srow, rrow, su, ru, sd, rd, copied, sf, rf,
 ):
@@ -681,7 +684,7 @@
     line.event(0)
     sums = [
         (RowScatter(parts, upshare_ref, urecv_ref, su, ru), ustage_ref, gup_ref),
-        (RowScatter(parts, downshare_ref, drecv_ref, sd, rd), dstage_ref, gdown_ref),
+        (RowScatter(parts, gateshare_ref, drecv_ref, sd, rd), dstage_ref, ggate_ref),
     ]
     for scatter, _, _ in sums:
         scatter.start()
@@ -796,7 +799,7 @@
         move.wait()
 
 
-def attend_back_call(dmid, weight, q, k, v, cosine, sine, segc, segr, columns, attn, down, middle, upshare, downshare):
+def attend_back_call(dmid, weight, q, k, v, cosine, sine, segc, segr, columns, attn, down, middle, upshare, gateshare):
     rows_n, cols_n = lax.axis_size("row"), lax.axis_size("col")
     _, heads_cols, width = weight.shape
     quarter = middle.shape[0]
@@ -811,7 +814,7 @@
             jax.ShapeDtypeStruct((rows_n, quarter, width), BF16),
             jax.ShapeDtypeStruct((rows_n, heads_cols // 2, width), BF16),
             jax.ShapeDtypeStruct((2 * upshare.shape[1], upshare.shape[2]), F32),
-            jax.ShapeDtypeStruct((2 * downshare.shape[1], downshare.shape[2]), F32),
+            jax.ShapeDtypeStruct((2 * gateshare.shape[1], gateshare.shape[2]), F32),
         ),
         in_specs=[VM] * 14,
         out_specs=(VM,) * 4 + (pl.BlockSpec(memory_space=pl.ANY),) * 2,
@@ -825,9 +828,9 @@
             pltpu.VMEM((rows_n, heads_cols // 2, width), BF16),
             pltpu.VMEM((rows_n, heads_cols // 2, width), BF16),
             pltpu.VMEM((rows_n - 1,) + upshare.shape[1:], BF16),
-            pltpu.VMEM((rows_n - 1,) + downshare.shape[1:], BF16),
+            pltpu.VMEM((rows_n - 1,) + gateshare.shape[1:], BF16),
             pltpu.VMEM(upshare.shape[1:], F32),
-            pltpu.VMEM(downshare.shape[1:], F32),
+            pltpu.VMEM(gateshare.shape[1:], F32),
             dma((2,)), dma((2 * cols_n,)), dma((1,)), dma((1,)), dma((rows_n - 1,)), dma((rows_n - 1,)),
         ]
         + [dma((2 * (rows_n - 1),))] * 4
@@ -836,7 +839,7 @@
         ],
         compiler_params=params(5),
         cost_estimate=cost(80),
-    )(dmid, weight, q, k, v, cosine, sine, segc, segr, attn, down, middle, upshare, downshare)
+    )(dmid, weight, q, k, v, cosine, sine, segc, segr, attn, down, middle, upshare, gateshare)
 
 
 def middle_kernel(
@@ -933,9 +936,9 @@
 
 
 def back_kernel(
-    rows_n, cols_n, dgate_ref, dup_ref, gate_ref, up_ref, mid_ref, tok_ref, gain_ref, second_ref,
-    dmid_ref, grad_ref, ggate_ref, share_ref,
-    w0_ref, w1_ref, part_ref, recv_ref, other_ref, grecv_ref, stage_ref,
+    rows_n, cols_n, dgate_ref, dup_ref, gate_ref, up_ref, mid_ref, tok_ref, gain_ref, second_ref, down_ref,
+    dmid_ref, grad_ref, gdown_ref, share0_ref, share1_ref,
+    w0_ref, w1_ref, part_ref, recv_ref, other_ref, drecv_ref, stage_ref,
     loads, s1, r1, s2, r2, sg, rg, score, rcore, copied, sf, rf, free,
 ):
     row, col, core = lax.axis_index("row"), lax.axis_index("col"), lax.axis_index("dp")
@@ -973,75 +976,90 @@
                 ).astype(BF16)
 
     def add(kept):
-        @pl.loop(0, rows_n)
+        chunk = min(64, share)
+        chunks = share // chunk
+
+        @pl.loop(0, rows_n * chunks)
         def _(i):
-            rows = pl.ds(pl.multiple_of(core * share, 16), share)
-            kept[i, rows] = (kept[i, rows].astype(F32) + other_ref[i].astype(F32)).astype(BF16)
-
-    line = ColScatter(cols_n, part_ref, recv_ref, s1, r1)
-    prepare(cols_n - 1)
-    prepare(0)
-    line.event(0)
-    for target in range(1, cols_n - 1):
-        prepare(target)
+            block, start = lax.div(i, chunks), lax.rem(i, chunks) * chunk
+            rows = pl.ds(pl.multiple_of(core * share + start, 16), chunk)
+            other = other_ref[block, pl.ds(pl.multiple_of(start, 16), chunk)]
+            kept[block, rows] = (kept[block, rows].astype(F32) + other.astype(F32)).astype(BF16)
+
+    half = quarter // 2
+    lines = [ColScatter(cols_n, part_ref, recv_ref, s1, r1, k * half, half, k) for k in range(2)]
+    gathers = [RowGather(rows_n, dmid_ref, s2, r2, k * half, half, k * 2 * (rows_n - 1)) for k in range(2)]
+    scatter = RowScatter(rows_n, down_ref, drecv_ref, sg, rg)
     cross = [
         remote(kept.at[:, pl.ds(pl.multiple_of((1 - core) * share, 16), share)], other_ref, score, rcore, k, {"dp": 1 - core})
         for k, kept in enumerate((w0_ref, w1_ref))
     ]
+    keeps = [
+        pltpu.make_async_copy(kept.at[:, pl.ds(pl.multiple_of(core * share, 16), share)], out, copied.at[1 + k])
+        for k, (kept, out) in enumerate(((w0_ref, share0_ref), (w1_ref, share1_ref)))
+    ]
+
+    def finish(rows, total):
+        stage_ref[rows] = total
+
+    def norm_back(k):
+        @pl.loop(0, half // 32)
+        def _(i):
+            rows = pl.ds(pl.multiple_of(k * half + i * 32, 32), 32)
+            got = lines[k].total(rows)
+            middle = mid_ref[rows]
+            inverse = lax.rsqrt(jnp.sum(middle * middle, axis=1, keepdims=True) / features + EPSILON)
+            weighted = got * gain_ref[...]
+            inner = jnp.sum(middle * weighted, axis=1, keepdims=True) / features
+            grad_ref[...] += jnp.sum(got * middle * inverse, axis=0, keepdims=True)
+            value = tok_ref[rows].astype(F32) + inverse * weighted - middle * (inverse * inverse * inverse * inner)
+            dmid_ref[row, rows] = value.astype(BF16)
+
+    grad_ref[...] = jnp.zeros_like(grad_ref)
+    scatter.start()
+    for time in range(cols_n):
+        lines[0].event(time, prepare)
+        if time == cols_n - 2:
+            for step in range(scatter.bits - 1):
+                scatter.event(step, finish)
+    lines[1].event(0)
+    norm_back(0)
+    gathers[0].start()
+    scatter.event(scatter.bits - 1, finish)
+    results = settle(stage_ref, gdown_ref, core, copied, sf, rf, 0)
+    for move in results:
+        move.start()
     product(dgate_ref, w0_ref)
     cross[0].start()
-    line.event(1)
+    lines[1].event(1)
+    gathers[0].event(0)
     product(dup_ref, w1_ref)
+    for time in range(2, cols_n - 1):
+        lines[1].event(time)
+    for step in range(1, gathers[0].bits):
+        gathers[0].event(step)
     cross[0].wait()
     add(w0_ref)
+    keeps[0].start()
     pl.semaphore_signal(free, inc=1, device_id={"dp": 1 - core}, device_id_type=MESH)
-    scatter = RowScatter(rows_n, w0_ref, grecv_ref, sg, rg, core * share)
-    scatter.start()
     pl.semaphore_wait(free, 1)
     cross[1].start()
-    if cols_n > 2:
-        line.event(2)
+    lines[1].event(cols_n - 1)
+    norm_back(1)
+    gathers[1].start()
     cross[1].wait()
     add(w1_ref)
-    keep = pltpu.make_async_copy(w1_ref.at[:, pl.ds(pl.multiple_of(core * share, 16), share)], share_ref, copied.at[1])
-    keep.start()
-
-    def finish(rows, total):
-        stage_ref[rows] = total
-
-    for step in range(scatter.bits - 1):
-        scatter.event(step, finish)
-    for time in range(3, line.times):
-        line.event(time)
-
-    grad_ref[...] = jnp.zeros_like(grad_ref)
-
-    @pl.loop(0, quarter // 64)
-    def _(i):
-        rows = pl.ds(i * 64, 64)
-        got = line.total(rows)
-        middle = mid_ref[rows]
-        inverse = lax.rsqrt(jnp.sum(middle * middle, axis=1, keepdims=True) / features + EPSILON)
-        weighted = got * gain_ref[...]
-        inner = jnp.sum(middle * weighted, axis=1, keepdims=True) / features
-        grad_ref[...] += jnp.sum(got * middle * inverse, axis=0, keepdims=True)
-        value = tok_ref[rows].astype(F32) + inverse * weighted - middle * (inverse * inverse * inverse * inner)
-        dmid_ref[row, rows] = value.astype(BF16)
-
-    gather = RowGather(rows_n, dmid_ref, s2, r2)
-    gather.start()
-    scatter.event(scatter.bits - 1, finish)
-    results = settle(stage_ref, ggate_ref, core, copied, sf, rf, 0)
-    for move in results:
-        move.start()
-    gather.run()
+    keeps[1].start()
+    gathers[1].run()
+    gathers[0].finish()
     scatter.close()
-    keep.wait()
+    for move in keeps:
+        move.wait()
     for move in results:
         move.wait()
 
 
-def back_call(dgate, dup, gate, up, middle, tok, gain, second):
+def back_call(dgate, dup, gate, up, middle, tok, gain, second, down_share):
     rows_n, cols_n = lax.axis_size("row"), lax.axis_size("col")
     quarter, features = middle.shape
     hidden = dgate.shape[1]
@@ -1055,26 +1073,27 @@
         out_shape=(
             jax.ShapeDtypeStruct((rows_n, quarter, features), BF16),
             jax.ShapeDtypeStruct((1, features), F32),
-            jax.ShapeDtypeStruct((width, hidden), F32),
+            jax.ShapeDtypeStruct((2 * down_share.shape[1], width), F32),
+            jax.ShapeDtypeStruct(half, BF16),
             jax.ShapeDtypeStruct(half, BF16),
         ),
-        in_specs=[VM, VM, anywhere, anywhere, VM, VM, VM, VM],
-        out_specs=(VM, VM, anywhere, anywhere),
+        in_specs=[VM, VM, anywhere, anywhere, VM, VM, VM, VM, VM],
+        out_specs=(VM, VM, anywhere, anywhere, anywhere),
         scratch_shapes=[
             pltpu.VMEM((rows_n, width, hidden), BF16),
             pltpu.VMEM((rows_n, width, hidden), BF16),
             pltpu.VMEM((cols_n, quarter, features), BF16),
             pltpu.VMEM((cols_n + 1, quarter, features), BF16),
             pltpu.VMEM(half, BF16),
-            pltpu.VMEM((rows_n - 1,) + half[1:], BF16),
-            pltpu.VMEM(half[1:], F32),
-            dma((2,)), dma((2,)), dma((2 * cols_n,)),
-            dma((line,)), dma((line,)), dma((line,)), dma((line,)),
-            dma((2,)), dma((2,)), dma((2,)), dma((1,)), dma((1,)), pltpu.SemaphoreType.REGULAR,
+            pltpu.VMEM((rows_n - 1,) + down_share.shape[1:], BF16),
+            pltpu.VMEM(down_share.shape[1:], F32),
+            dma((2,)), dma((4,)), dma((4 * cols_n,)),
+            dma((2 * line,)), dma((2 * line,)), dma((line,)), dma((line,)),
+            dma((2,)), dma((2,)), dma((3,)), dma((1,)), dma((1,)), pltpu.SemaphoreType.REGULAR,
         ],
         compiler_params=params(3),
         cost_estimate=cost(130),
-    )(dgate, dup, gate, up, middle, tok, gain, second)
+    )(dgate, dup, gate, up, middle, tok, gain, second, down_share)
 
 
 def last_kernel(
@@ -1389,13 +1408,14 @@
     gate_all, up_all = gate_all.reshape(features, hidden_cols), up_all.reshape(features, hidden_cols)
     second_all, cot_all = second_all.reshape(-1, features), cot_all.reshape(-1, features)
     dgate, dup, down_share, down_part = feed_call(second_all, cot_all, gate_all, up_all, down_all)
-    dmid_all, gain2_grad, gate_grad, up_share = back_call(
-        dgate, dup, gate_all.reshape(rows, width, hidden_cols), up_all.reshape(rows, width, hidden_cols), middle, cot_tok, gain2, second_all
+    dmid_all, gain2_grad, down_grad, gate_share, up_share = back_call(
+        dgate, dup, gate_all.reshape(rows, width, hidden_cols), up_all.reshape(rows, width, hidden_cols), middle, cot_tok, gain2, second_all,
+        down_share,
     )
     dmid_all = dmid_all.reshape(length, features)
 
-    dqkv, inner1, blk, outline, up_grad, down_grad = attend_back_call(
-        dmid_all, out_all_w, q, k, v, cosine, sine, segc, segr, qkv_cols, attn, down_part, middle, up_share, down_share
+    dqkv, inner1, blk, outline, up_grad, gate_grad = attend_back_call(
+        dmid_all, out_all_w, q, k, v, cosine, sine, segc, segr, qkv_cols, attn, down_part, middle, up_share, gate_share
     )
     dfirst, block_out, inner1, gains, qkv_grad, out_grad = last_call(
         dqkv, qkv_all, first, outline, blk, inner1.reshape(-1, 128), activations, inv1, gain2_grad

time: 707 us -> 688 us (0.973)
  Pallas kernels: 666 us -> 647 us
    pallas_call x1, Pallas kernels: 132 us -> 112 us  [back_call(): pl.pallas_call(functools.partial(back_kernel, rows_n, cols_n), out_shape=...]
where the time goes in v5:
time: 688 us; the launch traced here: 682 us
  Pallas kernels  647 us (94%)
  local copies, waits for them, and re-layouts  18.4 us (3%)
  other arithmetic  14.8 us (2%)
    pallas_call x1, Pallas kernels, middle_call(): pl.pallas_call(functools.partial(middle_kernel, rows_n, cols_n), out_shap...  129 us
    pallas_call x1, Pallas kernels, back_call(): pl.pallas_call(functools.partial(back_kernel, rows_n, cols_n), out_shape=...  112 us
    pallas_call x1, Pallas kernels, attend_back_call(): pl.pallas_call(attend_back_kernel, out_shape=(jax.ShapeDtypeStruct((lengt...  96.1 us
    pallas_call x1, Pallas kernels, first_call(): pl.pallas_call(functools.partial(first_kernel, size), out_shape=(jax.Shap...  95.7 us
    pallas_call x1, Pallas kernels, last_call(): pl.pallas_call(functools.partial(last_kernel, size), out_shape=(jax.Shape...  92.6 us
    pallas_call x1, Pallas kernels, feed_call(): pl.pallas_call(feed_kernel, grid=(tiles + cols_n,), out_shape=(jax.ShapeD...  64.5 us
    pallas_call x1, Pallas kernels, attend_call(): pl.pallas_call(functools.partial(attend_kernel, size), out_shape=(jax.Sha...  57.5 us
    unnamed x28, local copies, waits for them, and re-layouts  13.9 us

profile of v5, /device:TPU:0, one launch (start us, length us, event | category | flops | bytes accessed | tf_op | source)
XLA Modules:
  0.0 681.6 jit_solution(8960504769577892372)
XLA Ops:
  0.7 0.7 convert_element_type.19
  1.4 0.7 convert_element_type.20
  2.0 1.3 maximum_bitcast_fusion.small_ref
  3.3 2.1 pad_maximum_fusion.qkv_ref
  5.5 95.7 %shard_map.212 = (bf16[4,1024,512]{2,1,0:T(8,128)(2,1)}, bf16[1024,2048]{1,0:T(8,128)(2,1)}, f32[1024,1]{1,0:T(8,128)}, bf16[256,2048]{1,0:T(8,128)(2,1)}, f32[4...) custom-call(bf16[1024,512]{1,0:T(8,128)(2,1)} %act_ref.3, ...), custom_call_target="tpu_custom_call" | custom-call | tf_op jit(solution)/shard_map/pallas_call | solution.py:500
  101.2 0.8 copy.30
  102.0 0.1 constant_dynamic-slice_fusion
  102.1 0.0 copy-start.8
  102.1 0.6 copy.28
  102.7 0.2 broadcast_multiply_fusion
  102.9 1.0 copy.24.segc_ref
  104.0 2.9 fusion.2
  106.9 0.0 copy-done.8
  106.9 57.5 %shard_map.213 = (bf16[8,1024,64]{2,1,0:T(8,128)(2,1)}, bf16[2,1024,64]{2,1,0:T(8,128)(2,1)}, bf16[2,1024,64]{2,1,0:T(8,128)(2,1)}, bf16[1024,512]{1,0:T(8,128)(...) custom-call(bf16[1024,2048]{1,0:T(8,128)(2,1)} %get-tuple-element.51.first_ref, ...), custom_call_target="tpu_custom_call" | custom-call | flops 44999999488 | bytes 1048576 | tf_op jit(solution)/shard_map/pallas_call | solution.py:606
  164.4 129.1 %shard_map.214 = (f32[256,2048]{1,0:T(8,128)}, bf16[4,256,2048]{2,1,0:T(8,128)(2,1)}, bf16[4,256,2048]{2,1,0:T(8,128)(2,1)}, bf16[4,512,2048]{2,1,0:T(8,128)(2,1)}, bf16[4,2048,512]{2,1,0:T(8,128)(2,1)}) custom-call(bf16[1024,512]{1,0:T(8,128)(2,1)} %get-tuple-element.55.attn_ref, bf16[4,512,512]{2,1,0:T(8,128)(2,1)} %get-tuple-element.56.weight_ref, ...), custom_call_target="tpu_custom_call" | custom-call | flops 130000003072 | bytes 1048576 | tf_op jit(solution)/shard_map/pallas_call | solution.py:907
  293.5 64.5 %shard_map.215 = (bf16[1024,2048]{1,0:T(8,128)(2,1)}, bf16[1024,2048]{1,0:T(8,128)(2,1)}, bf16[4,1024,512]{2,1,0:T(8,128)(2,1)}, bf16[4,256,2048]{2,1,0:T(8,128)(2,1)}) custom-call(bf16[1024,2048]{1,0:T(8,128)(2,1)} %bitcast.39, bf16[1024,2048]{1,0:T(8,128)(2,1)} %bitcast.41, bf16[2048,2048]{1,0:T(8,128)(2,1)} %bitcast.37, bf16[2048,2048]{1,0:T(8,128)(2,1)} %bitcast.38, ...), custom_call_target="tpu_custom_call" | custom-call | flops 49999998976 | bytes 1048576 | tf_op jit(solution)/shard_map/pallas_call | solution.py:1335
  358.0 111.5 %shard_map.216 = (bf16[4,256,2048]{2,1,0:T(8,128)(2,1)}, f32[1,2048]{1,0:T(1,128)}, f32[2048,512]{1,0:T(8,128)}, bf16[4,256,2048]{2,1,0:T(8,128)(2,1)}, bf16[4,256,2048]{2,1,0:T(8,128)(2,1)}) custom-call(bf16[1024,2048]{1,0:T(8,128)(2,1)} %get-tuple-element.65.dgate_ref, bf16[1024,2048]{1,0:T(8,128)(2,1)} %get-tuple-element.66.dup_ref, ...), custom_call_target="tpu_custom_call" | custom-call | flops 130000003072 | bytes 1048576 | tf_op jit(solution)/shard_map/pallas_call | solution.py:1071
  469.6 96.1 %shard_map.217 = (bf16[1024,768]{1,0:T(8,128)(2,1)}, f32[1024,1]{1,0:T(8,128)}, bf16[4,256,512]{2,1,0:T(8,128)(2,1)}, bf16[4,256,512]{2,1,0:T(8,128)(2,1)}, f32[512,2048]{1,0:T(8,128)}, /*index=5*/f32[512,2048]{1,0:T(8,128)}) custom-call(bf16[1024,2048]{1,0:T(8,128)(2,1)} %bitcast.23, bf16[4,512,512]{2,1,0:T(8,128)(2,1)} %get-tuple-element.56.weight_ref, ...), custom_call_target="tpu_custom_call" | custom-call | flops 80000000000 | bytes 1048576 | tf_op jit(solution)/shard_map/pallas_call | solution.py:809
  565.7 1.8 reduce
  567.5 0.0 copy-start.7
  567.5 0.0 copy-start.9
  567.5 92.6 %shard_map.218 = (f32[1024,512]{1,0:T(8,128)}, bf16[1024,512]{1,0:T(8,128)(2,1)}, f32[4,8,128]{2,1,0:T(8,128)}, f32[2,1,512]{2,1,0:T(1,128)}, f32[512,768]{1,0:T(8,128)}, /*index=5*/f32[512,512]{1,0:T(8,128)}) custom-call(bf16[1024,768]{1,0:T(8,128)(2,1)} %get-tuple-element.76.dqkv_ref, bf16[4,512,768]{2,1,0:T(8,128)(2,1)} %get-tuple-element.52.weight_ref, ...), custom_call_target="tpu_custom_call" | custom-call | flops 80000000000 | bytes 1048576 | tf_op jit(solution)/shard_map/pallas_call | solution.py:1208
  660.2 0.0 copy-start.3
  660.2 0.8 reduce_sum.9
  661.0 1.3 fusion.6
  662.3 0.2 copy.26
  662.5 0.0 copy-done.7
  662.5 0.3 fusion.4
  662.9 0.0 copy-done.9
  662.9 0.0 copy-done.3
  662.9 0.0 copy-start.4
  662.9 3.9 multiply_subtract_fusion
  666.7 0.0 copy-done.4
  666.7 0.0 copy-start.6
  666.7 0.8 fusion.5
  667.6 0.0 copy-start.5
  667.6 1.1 slice.30
  668.7 0.0 copy-start.2
  668.7 0.0 copy-done.6
  668.7 1.0 copy.36
  669.6 0.0 copy-done.5
  669.6 1.0 copy.37
  670.6 1.1 copy-done.2
  671.7 2.1 copy.38
  673.8 1.6 copy-done.1
  675.4 2.1 copy.39
  677.5 1.6 copy-done
  679.1 2.0 copy.40
  (4 shorter events, 0.0 us)
Async XLA Ops:
  102.1 4.8 copy-start.8
  567.5 95.0 %copy-start.7 = (f32[1024,1]{1,0:T(8,128)S(1)}, f32[1024,1]{1,0:T(8,128)}, u32[]{:S(2)}) copy-start(f32[1024,1]{1,0:T(8,128)} %get-tuple-element.80.inv_ref) | copy-start | bytes 12292
  567.5 95.3 %copy-start.9 = (f32[512]{0:T(512)S(1)}, f32[512]{0:T(512)}, u32[]{:S(2)}) copy-start(f32[512]{0:T(512)} %param.16) | copy-start | bytes 6148
  660.2 2.7 copy-start.3
  662.9 3.9 copy-start.4
  666.7 1.9 copy-start.6
  667.6 2.1 copy-start.5
  668.7 3.0 copy-start.2
  671.7 3.7 copy-start.1
  675.4 3.7 copy-start

commit v6 on v5

--- a/solution.py
+++ b/solution.py
@@ -876,11 +876,16 @@
         inverse = lax.rsqrt(squares / features + EPSILON)
         second_ref[col, rows] = (mid_ref[rows] * inverse * gain_ref[...]).astype(BF16)
 
-    RowScatter(rows_n, part_ref, recv_ref, s1, r1).run(finish)
+    scatter = RowScatter(rows_n, part_ref, recv_ref, s1, r1)
+    scatter.start()
+    for step in range(scatter.bits - 1):
+        scatter.event(step, finish)
+    for bulk in bulks:
+        bulk.start()
+    scatter.event(scatter.bits - 1, finish)
     line = ColGather(cols_n, second_ref, s2, r2)
     line.event(0)
-    for bulk in bulks:
-        bulk.start()
+    scatter.close()
     for step in range(3, cols_n):
         rest.event(step)
     rest.finish()
@@ -1122,6 +1127,11 @@
         small.append(remote(grad2_ref.at[row ^ mask], rgain_ref.at[row], sg, rg, mask - 1, {"row": row ^ mask}))
     for move in small:
         move.start()
+    block_ref[pl.ds(pl.multiple_of(row * quarter, 16), quarter)] = blk_ref[row]
+    for mask in range(1, size):
+        remote(
+            blk_ref.at[row ^ mask], block_ref.at[pl.ds(pl.multiple_of(row * quarter, 16), quarter)], sblk, rblk, mask - 1, {"row": row ^ mask}
+        ).start()
     oline = ColScatter(size, outline_ref, orecv_ref, so, ro)
     oline.event(0)
 
@@ -1143,7 +1153,6 @@
     cross.wait()
     add_halves(qpart_ref, qother_ref, qshare_ref)
     row_moves(size, qshare_ref, qline_ref, srow, rrow, 0, True)
-    scatter.start()
     for time in range(2, oline.times):
         oline.event(time)
     share_o = outline_ref.shape[1]
@@ -1156,12 +1165,8 @@
     gout_ref[pl.ds(pl.multiple_of(core * share_o, 8), share_o)] = oline.total(slice(None))
     across(gout_ref, share_o, 0).start()
 
-    block_ref[pl.ds(pl.multiple_of(row * quarter, 16), quarter)] = blk_ref[row]
-    for mask in range(1, size):
-        remote(
-            blk_ref.at[row ^ mask], block_ref.at[pl.ds(pl.multiple_of(row * quarter, 16), quarter)], sblk, rblk, mask - 1, {"row": row ^ mask}
-        ).start()
     row_moves(size, qshare_ref, qline_ref, srow, rrow, 0, False)
+    scatter.start()
     qline = ColScatter(size, qline_ref, qrecv_ref, sq, rq)
     qline.event(0)
     pair_ref[0] = jnp.zeros_like(pair_ref[0])
@@ -1253,7 +1258,7 @@
     rows_n, tile, width = down_ref.shape
     tokens = second_ref.shape[0]
     tiles = hidden_ref.shape[0]
-    block = min(512, tokens)
+    block = tokens
     mine = tiles // 2
 
     def place(t):

time: 688 us -> 692 us (level)
    pallas_call x1, Pallas kernels: 64.5 us -> 73.7 us  [feed_call(): pl.pallas_call(feed_kernel, grid=(tiles + cols_n,), out_shape=(jax.ShapeD...]
where the time goes in v6:
time: 692 us; the launch traced here: 686 us
  Pallas kernels  651 us (94%)
  local copies, waits for them, and re-layouts  18.4 us (3%)
  other arithmetic  14.8 us (2%)
    pallas_call x1, Pallas kernels, middle_call(): pl.pallas_call(functools.partial(middle_kernel, rows_n, cols_n), out_shap...  128 us
    pallas_call x1, Pallas kernels, back_call(): pl.pallas_call(functools.partial(back_kernel, rows_n, cols_n), out_shape=...  112 us
    pallas_call x1, Pallas kernels, attend_back_call(): pl.pallas_call(attend_back_kernel, out_shape=(jax.ShapeDtypeStruct((lengt...  95.9 us
    pallas_call x1, Pallas kernels, first_call(): pl.pallas_call(functools.partial(first_kernel, size), out_shape=(jax.Shap...  95.7 us
    pallas_call x1, Pallas kernels, last_call(): pl.pallas_call(functools.partial(last_kernel, size), out_shape=(jax.Shape...  88.5 us
    pallas_call x1, Pallas kernels, feed_call(): pl.pallas_call(feed_kernel, grid=(tiles + cols_n,), out_shape=(jax.ShapeD...  73.7 us
    pallas_call x1, Pallas kernels, attend_call(): pl.pallas_call(functools.partial(attend_kernel, size), out_shape=(jax.Sha...  57.5 us
    unnamed x28, local copies, waits for them, and re-layouts  13.9 us

profile of v6, /device:TPU:0, one launch (start us, length us, event | category | flops | bytes accessed | tf_op | source)
XLA Modules:
  0.0 685.9 jit_solution(13110251863414450848)
XLA Ops:
  0.7 0.7 convert_element_type.19
  1.4 0.7 convert_element_type.20
  2.0 1.3 maximum_bitcast_fusion.small_ref
  3.3 2.1 pad_maximum_fusion.qkv_ref
  5.5 95.7 %shard_map.212 = (bf16[4,1024,512]{2,1,0:T(8,128)(2,1)}, bf16[1024,2048]{1,0:T(8,128)(2,1)}, f32[1024,1]{1,0:T(8,128)}, bf16[256,2048]{1,0:T(8,128)(2,1)}, f32[4...) custom-call(bf16[1024,512]{1,0:T(8,128)(2,1)} %act_ref.3, ...), custom_call_target="tpu_custom_call" | custom-call | tf_op jit(solution)/shard_map/pallas_call | solution.py:500
  101.2 0.8 copy.30
  102.0 0.1 constant_dynamic-slice_fusion
  102.1 0.0 copy-start.8
  102.1 0.6 copy.28
  102.7 0.2 broadcast_multiply_fusion
  102.9 1.0 copy.24.segc_ref
  104.0 2.9 fusion.2
  106.9 0.0 copy-done.8
  106.9 57.5 %shard_map.213 = (bf16[8,1024,64]{2,1,0:T(8,128)(2,1)}, bf16[2,1024,64]{2,1,0:T(8,128)(2,1)}, bf16[2,1024,64]{2,1,0:T(8,128)(2,1)}, bf16[1024,512]{1,0:T(8,128)(...) custom-call(bf16[1024,2048]{1,0:T(8,128)(2,1)} %get-tuple-element.51.first_ref, ...), custom_call_target="tpu_custom_call" | custom-call | flops 44999999488 | bytes 1048576 | tf_op jit(solution)/shard_map/pallas_call | solution.py:606
  164.4 128.0 %shard_map.214 = (f32[256,2048]{1,0:T(8,128)}, bf16[4,256,2048]{2,1,0:T(8,128)(2,1)}, bf16[4,256,2048]{2,1,0:T(8,128)(2,1)}, bf16[4,512,2048]{2,1,0:T(8,128)(2,1)}, bf16[4,2048,512]{2,1,0:T(8,128)(2,1)}) custom-call(bf16[1024,512]{1,0:T(8,128)(2,1)} %get-tuple-element.55.attn_ref, bf16[4,512,512]{2,1,0:T(8,128)(2,1)} %get-tuple-element.56.weight_ref, ...), custom_call_target="tpu_custom_call" | custom-call | flops 130000003072 | bytes 1048576 | tf_op jit(solution)/shard_map/pallas_call | solution.py:912
  292.5 73.7 %shard_map.215 = (bf16[1024,2048]{1,0:T(8,128)(2,1)}, bf16[1024,2048]{1,0:T(8,128)(2,1)}, bf16[4,1024,512]{2,1,0:T(8,128)(2,1)}, bf16[4,256,2048]{2,1,0:T(8,128)(2,1)}) custom-call(bf16[1024,2048]{1,0:T(8,128)(2,1)} %bitcast.39, bf16[1024,2048]{1,0:T(8,128)(2,1)} %bitcast.41, bf16[2048,2048]{1,0:T(8,128)(2,1)} %bitcast.37, bf16[2048,2048]{1,0:T(8,128)(2,1)} %bitcast.38, ...), custom_call_target="tpu_custom_call" | custom-call | flops 49999998976 | bytes 1048576 | tf_op jit(solution)/shard_map/pallas_call | solution.py:1340
  366.1 112.1 %shard_map.216 = (bf16[4,256,2048]{2,1,0:T(8,128)(2,1)}, f32[1,2048]{1,0:T(1,128)}, f32[2048,512]{1,0:T(8,128)}, bf16[4,256,2048]{2,1,0:T(8,128)(2,1)}, bf16[4,256,2048]{2,1,0:T(8,128)(2,1)}) custom-call(bf16[1024,2048]{1,0:T(8,128)(2,1)} %get-tuple-element.65.dgate_ref, bf16[1024,2048]{1,0:T(8,128)(2,1)} %get-tuple-element.66.dup_ref, ...), custom_call_target="tpu_custom_call" | custom-call | flops 130000003072 | bytes 1048576 | tf_op jit(solution)/shard_map/pallas_call | solution.py:1076
  478.3 95.9 %shard_map.217 = (bf16[1024,768]{1,0:T(8,128)(2,1)}, f32[1024,1]{1,0:T(8,128)}, bf16[4,256,512]{2,1,0:T(8,128)(2,1)}, bf16[4,256,512]{2,1,0:T(8,128)(2,1)}, f32[512,2048]{1,0:T(8,128)}, /*index=5*/f32[512,2048]{1,0:T(8,128)}) custom-call(bf16[1024,2048]{1,0:T(8,128)(2,1)} %bitcast.23, bf16[4,512,512]{2,1,0:T(8,128)(2,1)} %get-tuple-element.56.weight_ref, ...), custom_call_target="tpu_custom_call" | custom-call | flops 80000000000 | bytes 1048576 | tf_op jit(solution)/shard_map/pallas_call | solution.py:809
  574.2 1.8 reduce
  576.0 0.0 copy-start.7
  576.0 0.0 copy-start.9
  576.0 88.5 %shard_map.218 = (f32[1024,512]{1,0:T(8,128)}, bf16[1024,512]{1,0:T(8,128)(2,1)}, f32[4,8,128]{2,1,0:T(8,128)}, f32[2,1,512]{2,1,0:T(1,128)}, f32[512,768]{1,0:T(8,128)}, /*index=5*/f32[512,512]{1,0:T(8,128)}) custom-call(bf16[1024,768]{1,0:T(8,128)(2,1)} %get-tuple-element.76.dqkv_ref, bf16[4,512,768]{2,1,0:T(8,128)(2,1)} %get-tuple-element.52.weight_ref, ...), custom_call_target="tpu_custom_call" | custom-call | flops 80000000000 | bytes 1048576 | tf_op jit(solution)/shard_map/pallas_call | solution.py:1213
  664.6 0.0 copy-start.3
  664.6 0.8 reduce_sum.9
  665.4 1.3 fusion.6
  666.7 0.2 copy.26
  666.9 0.0 copy-done.7
  666.9 0.3 fusion.4
  667.2 0.0 copy-done.9
  667.2 0.0 copy-done.3
  667.3 0.0 copy-start.4
  667.3 3.9 multiply_subtract_fusion
  671.1 0.0 copy-done.4
  671.1 0.8 fusion.5
  672.0 0.0 copy-start.5
  672.0 1.1 slice.30
  673.1 0.0 copy-start.2
  673.1 0.0 copy-done.6
  673.1 1.0 copy.36
  674.0 0.0 copy-done.5
  674.0 1.0 copy.37
  675.0 1.1 copy-done.2
  676.1 0.0 copy-start.1
  676.1 2.1 copy.38
  678.2 1.6 copy-done.1
  679.8 2.1 copy.39
  681.9 1.6 copy-done
  683.5 2.0 copy.40
  (4 shorter events, 0.0 us)
Async XLA Ops:
  102.1 4.8 copy-start.8
  576.0 90.9 %copy-start.7 = (f32[1024,1]{1,0:T(8,128)S(1)}, f32[1024,1]{1,0:T(8,128)}, u32[]{:S(2)}) copy-start(f32[1024,1]{1,0:T(8,128)} %get-tuple-element.80.inv_ref) | copy-start | bytes 12292
  576.0 91.2 %copy-start.9 = (f32[512]{0:T(512)S(1)}, f32[512]{0:T(512)}, u32[]{:S(2)}) copy-start(f32[512]{0:T(512)} %param.16) | copy-start | bytes 6148
  664.6 2.7 copy-start.3
  667.3 3.9 copy-start.4
  671.1 1.9 copy-start.6
  672.0 2.1 copy-start.5
  673.1 3.0 copy-start.2
  676.1 3.7 copy-start.1
  679.8 3.7 copy-start

commit v7 on v6

--- a/solution.py
+++ b/solution.py
@@ -227,8 +227,9 @@
 
 
 class ColGather:
-    def __init__(self, size, ref, sends, recvs, begin=0, end=None):
+    def __init__(self, size, ref, sends, recvs, begin=0, end=None, rows=None, first=0):
         self.size, self.ref, self.sends, self.recvs = size, ref, sends, recvs
+        self.rows, self.first = rows or pl.ds(0, ref.shape[1]), first
         self.begin, self.end = begin, size - 1 if end is None else end
         self.col = lax.axis_index("col")
 
@@ -241,9 +242,9 @@
 
     def copy(self, side, step):
         size, col = self.size, self.col
-        piece = self.ref.at[self.sides(step)[side][1]]
+        piece = self.ref.at[self.sides(step)[side][1], self.rows]
         target = lax.rem(col + (1 if side == 0 else size - 1), size)
-        return remote(piece, piece, self.sends, self.recvs, side * (size - 1) + step, {"col": target})
+        return remote(piece, piece, self.sends, self.recvs, self.first + side * (size - 1) + step, {"col": target})
 
     def event(self, step, seen=None):
         for side, place, has, goes in self.sides(step):
@@ -844,7 +845,7 @@
 
 def middle_kernel(
     rows_n, cols_n, attn_ref, weight_ref, x_ref, gain_ref, tok_ref, near_ref, next_ref, up_ref, down_ref,
-    mid_ref, second_ref, cot_ref, ups_ref, downs_ref, part_ref, recv_ref, s1, r1, s2, r2, szc, rzc, *shared,
+    mid_ref, second_ref, cot_ref, ups_ref, downs_ref, part_ref, recv0_ref, recv1_ref, s0, r0, s1, r1, s2, r2, szc, rzc, *shared,
 ):
     row, col = lax.axis_index("row"), lax.axis_index("col")
     quarter, features = mid_ref.shape
@@ -865,42 +866,64 @@
         for j in range(rows_n):
             part_ref[i, :, j * width : (j + 1) * width] = jnp.dot(own, weight_ref[j], preferred_element_type=F32).astype(BF16)
 
-    def finish(rows, total):
-        own = pl.ds(row * quarter + rows.start, rows.size)
-        squares = jnp.zeros((rows.size, 1), F32)
-        for j in range(rows_n):
-            columns = slice(j * width, (j + 1) * width)
-            value = total[:, columns] + x_ref[j, own].astype(F32)
-            mid_ref[rows, columns] = value
-            squares += jnp.sum(value * value, axis=1, keepdims=True)
-        inverse = lax.rsqrt(squares / features + EPSILON)
-        second_ref[col, rows] = (mid_ref[rows] * inverse * gain_ref[...]).astype(BF16)
-
-    scatter = RowScatter(rows_n, part_ref, recv_ref, s1, r1)
-    scatter.start()
-    for step in range(scatter.bits - 1):
-        scatter.event(step, finish)
+    half = quarter // 2
+
+    def finish(k):
+        def act(rows, total):
+            here = pl.ds(pl.multiple_of(k * half + rows.start, 16), rows.size)
+            own = pl.ds(pl.multiple_of(row * quarter + k * half + rows.start, 16), rows.size)
+            squares = jnp.zeros((rows.size, 1), F32)
+            for j in range(rows_n):
+                columns = slice(j * width, (j + 1) * width)
+                value = total[:, columns] + x_ref[j, own].astype(F32)
+                mid_ref[here, columns] = value
+                squares += jnp.sum(value * value, axis=1, keepdims=True)
+            inverse = lax.rsqrt(squares / features + EPSILON)
+            second_ref[col, here] = (mid_ref[here] * inverse * gain_ref[...]).astype(BF16)
+
+        return act
+
+    scatters = [
+        RowScatter(rows_n, part_ref, recv0_ref, s0, r0, 0),
+        RowScatter(rows_n, part_ref, recv1_ref, s1, r1, half),
+    ]
+    lines = [
+        ColGather(cols_n, second_ref, s2, r2, 0, None, pl.ds(k * half, half), k * 2 * (cols_n - 1)) for k in range(2)
+    ]
+    bits = scatters[0].bits
+    scatters[0].start()
+    scatters[0].event(0, finish(0))
+    scatters[1].start()
+    for step in range(1, bits):
+        scatters[0].event(step, finish(0))
+    lines[0].event(0)
+    for step in range(bits - 1):
+        scatters[1].event(step, finish(1))
     for bulk in bulks:
         bulk.start()
-    scatter.event(scatter.bits - 1, finish)
-    line = ColGather(cols_n, second_ref, s2, r2)
-    line.event(0)
-    scatter.close()
+    scatters[1].event(bits - 1, finish(1))
+    lines[1].event(0)
     for step in range(3, cols_n):
         rest.event(step)
     rest.finish()
-    line.event(1)
-    bits = bulks[0].gather.bits
+    lines[0].event(1)
+    lines[0].event(2)
+    lines[1].event(1)
+    for step in range(3, cols_n):
+        lines[0].event(step)
+        lines[1].event(step - 1)
     for bulk in bulks:
         bulk.event(0)
-    for step in range(2, cols_n):
-        line.event(step)
+    lines[1].event(cols_n - 1)
     for step in range(1, bits):
         for bulk in bulks:
             bulk.event(step)
     for bulk in bulks:
         bulk.finish()
-    line.finish()
+    for scatter in scatters:
+        scatter.close()
+    for line in lines:
+        line.finish()
 
 
 def middle_call(attn, weight, x, gain, tok, near, following, up, down):
@@ -922,10 +945,12 @@
         out_specs=(VM, VM, VM, anywhere, anywhere),
         scratch_shapes=[
             pltpu.VMEM((rows_n, quarter, features), BF16),
-            pltpu.VMEM((rows_n - 1, quarter, features), BF16),
+            pltpu.VMEM((rows_n - 1, quarter // 2, features), BF16),
+            pltpu.VMEM((rows_n - 1, quarter // 2, features), BF16),
         ]
-        + [dma((2 * (rows_n - 1),))] * 2
-        + [dma((2 * (cols_n - 1),))] * 4
+        + [dma((2 * (rows_n - 1),))] * 4
+        + [dma((4 * (cols_n - 1),))] * 2
+        + [dma((2 * (cols_n - 1),))] * 2
         + SharedGather.scratch(rows_n, 2),
         compiler_params=params(2),
         cost_estimate=cost(130),
@@ -1258,7 +1283,7 @@
     rows_n, tile, width = down_ref.shape
     tokens = second_ref.shape[0]
     tiles = hidden_ref.shape[0]
-    block = tokens
+    block = min(512, tokens)
     mine = tiles // 2
 
     def place(t):

time: 692 us -> 677 us (0.978)
  Pallas kernels: 651 us -> 636 us
    pallas_call x1, Pallas kernels: 73.7 us -> 64.5 us  [feed_call(): pl.pallas_call(feed_kernel, grid=(tiles + cols_n,), out_shape=(jax.ShapeD...]
where the time goes in v7:
time: 677 us; the launch traced here: 671 us
  Pallas kernels  636 us (94%)
  local copies, waits for them, and re-layouts  18.4 us (3%)
  other arithmetic  14.8 us (2%)
    pallas_call x1, Pallas kernels, middle_call(): pl.pallas_call(functools.partial(middle_kernel, rows_n, cols_n), out_shap...  123 us
    pallas_call x1, Pallas kernels, back_call(): pl.pallas_call(functools.partial(back_kernel, rows_n, cols_n), out_shape=...  111 us
    pallas_call x1, Pallas kernels, attend_back_call(): pl.pallas_call(attend_back_kernel, out_shape=(jax.ShapeDtypeStruct((lengt...  97 us
    pallas_call x1, Pallas kernels, first_call(): pl.pallas_call(functools.partial(first_kernel, size), out_shape=(jax.Shap...  95.7 us
    pallas_call x1, Pallas kernels, last_call(): pl.pallas_call(functools.partial(last_kernel, size), out_shape=(jax.Shape...  87.4 us
    pallas_call x1, Pallas kernels, feed_call(): pl.pallas_call(feed_kernel, grid=(tiles + cols_n,), out_shape=(jax.ShapeD...  64.5 us
    pallas_call x1, Pallas kernels, attend_call(): pl.pallas_call(functools.partial(attend_kernel, size), out_shape=(jax.Sha...  57.5 us
    unnamed x28, local copies, waits for them, and re-layouts  13.9 us

profile of v7, /device:TPU:0, one launch (start us, length us, event | category | flops | bytes accessed | tf_op | source)
XLA Modules:
  0.0 670.7 jit_solution(12255576755291492077)
XLA Ops:
  0.7 0.7 convert_element_type.19
  1.4 0.7 convert_element_type.20
  2.0 1.3 maximum_bitcast_fusion.small_ref
  3.3 2.1 pad_maximum_fusion.qkv_ref
  5.5 95.7 %shard_map.212 = (bf16[4,1024,512]{2,1,0:T(8,128)(2,1)}, bf16[1024,2048]{1,0:T(8,128)(2,1)}, f32[1024,1]{1,0:T(8,128)}, bf16[256,2048]{1,0:T(8,128)(2,1)}, f32[4...) custom-call(bf16[1024,512]{1,0:T(8,128)(2,1)} %act_ref.3, ...), custom_call_target="tpu_custom_call" | custom-call | tf_op jit(solution)/shard_map/pallas_call | solution.py:501
  101.2 0.8 copy.30
  102.0 0.1 constant_dynamic-slice_fusion
  102.1 0.0 copy-start.8
  102.1 0.6 copy.28
  102.7 0.2 broadcast_multiply_fusion
  102.9 1.0 copy.24.segc_ref
  104.0 2.9 fusion.2
  106.9 0.0 copy-done.8
  106.9 57.5 %shard_map.213 = (bf16[8,1024,64]{2,1,0:T(8,128)(2,1)}, bf16[2,1024,64]{2,1,0:T(8,128)(2,1)}, bf16[2,1024,64]{2,1,0:T(8,128)(2,1)}, bf16[1024,512]{1,0:T(8,128)(...) custom-call(bf16[1024,2048]{1,0:T(8,128)(2,1)} %get-tuple-element.51.first_ref, ...), custom_call_target="tpu_custom_call" | custom-call | flops 44999999488 | bytes 1048576 | tf_op jit(solution)/shard_map/pallas_call | solution.py:607
  164.4 123.4 %shard_map.214 = (f32[256,2048]{1,0:T(8,128)}, bf16[4,256,2048]{2,1,0:T(8,128)(2,1)}, bf16[4,256,2048]{2,1,0:T(8,128)(2,1)}, bf16[4,512,2048]{2,1,0:T(8,128)(2,1)}, bf16[4,2048,512]{2,1,0:T(8,128)(2,1)}) custom-call(bf16[1024,512]{1,0:T(8,128)(2,1)} %get-tuple-element.55.attn_ref, bf16[4,512,512]{2,1,0:T(8,128)(2,1)} %get-tuple-element.56.weight_ref, ...), custom_call_target="tpu_custom_call" | custom-call | flops 130000003072 | bytes 1048576 | tf_op jit(solution)/shard_map/pallas_call | solution.py:935
  287.9 64.5 %shard_map.215 = (bf16[1024,2048]{1,0:T(8,128)(2,1)}, bf16[1024,2048]{1,0:T(8,128)(2,1)}, bf16[4,1024,512]{2,1,0:T(8,128)(2,1)}, bf16[4,256,2048]{2,1,0:T(8,128)(2,1)}) custom-call(bf16[1024,2048]{1,0:T(8,128)(2,1)} %bitcast.39, bf16[1024,2048]{1,0:T(8,128)(2,1)} %bitcast.41, bf16[2048,2048]{1,0:T(8,128)(2,1)} %bitcast.37, bf16[2048,2048]{1,0:T(8,128)(2,1)} %bitcast.38, ...), custom_call_target="tpu_custom_call" | custom-call | flops 49999998976 | bytes 1048576 | tf_op jit(solution)/shard_map/pallas_call | solution.py:1365
  352.4 110.7 %shard_map.216 = (bf16[4,256,2048]{2,1,0:T(8,128)(2,1)}, f32[1,2048]{1,0:T(1,128)}, f32[2048,512]{1,0:T(8,128)}, bf16[4,256,2048]{2,1,0:T(8,128)(2,1)}, bf16[4,256,2048]{2,1,0:T(8,128)(2,1)}) custom-call(bf16[1024,2048]{1,0:T(8,128)(2,1)} %get-tuple-element.65.dgate_ref, bf16[1024,2048]{1,0:T(8,128)(2,1)} %get-tuple-element.66.dup_ref, ...), custom_call_target="tpu_custom_call" | custom-call | flops 130000003072 | bytes 1048576 | tf_op jit(solution)/shard_map/pallas_call | solution.py:1101
  463.1 97.0 %shard_map.217 = (bf16[1024,768]{1,0:T(8,128)(2,1)}, f32[1024,1]{1,0:T(8,128)}, bf16[4,256,512]{2,1,0:T(8,128)(2,1)}, bf16[4,256,512]{2,1,0:T(8,128)(2,1)}, f32[512,2048]{1,0:T(8,128)}, /*index=5*/f32[512,2048]{1,0:T(8,128)}) custom-call(bf16[1024,2048]{1,0:T(8,128)(2,1)} %bitcast.23, bf16[4,512,512]{2,1,0:T(8,128)(2,1)} %get-tuple-element.56.weight_ref, ...), custom_call_target="tpu_custom_call" | custom-call | flops 80000000000 | bytes 1048576 | tf_op jit(solution)/shard_map/pallas_call | solution.py:810
  560.1 1.8 reduce
  561.9 0.0 copy-start.7
  561.9 0.0 copy-start.9
  561.9 87.4 %shard_map.218 = (f32[1024,512]{1,0:T(8,128)}, bf16[1024,512]{1,0:T(8,128)(2,1)}, f32[4,8,128]{2,1,0:T(8,128)}, f32[2,1,512]{2,1,0:T(1,128)}, f32[512,768]{1,0:T(8,128)}, /*index=5*/f32[512,512]{1,0:T(8,128)}) custom-call(bf16[1024,768]{1,0:T(8,128)(2,1)} %get-tuple-element.76.dqkv_ref, bf16[4,512,768]{2,1,0:T(8,128)(2,1)} %get-tuple-element.52.weight_ref, ...), custom_call_target="tpu_custom_call" | custom-call | flops 80000000000 | bytes 1048576 | tf_op jit(solution)/shard_map/pallas_call | solution.py:1238
  649.4 0.0 copy-start.3
  649.4 0.8 reduce_sum.9
  650.2 1.3 fusion.6
  651.5 0.2 copy.26
  651.7 0.0 copy-done.7
  651.7 0.3 fusion.4
  652.0 0.0 copy-done.9
  652.1 0.0 copy-done.3
  652.1 0.0 copy-start.4
  652.1 3.9 multiply_subtract_fusion
  655.9 0.0 copy-done.4
  655.9 0.0 copy-start.6
  655.9 0.8 fusion.5
  656.8 0.0 copy-start.5
  656.8 1.1 slice.30
  657.9 0.0 copy-start.2
  657.9 0.0 copy-done.6
  657.9 1.0 copy.36
  658.8 0.0 copy-done.5
  658.8 1.0 copy.37
  659.8 1.1 copy-done.2
  660.9 2.1 copy.38
  663.0 1.6 copy-done.1
  664.6 2.1 copy.39
  666.7 1.6 copy-done
  668.3 2.0 copy.40
  (4 shorter events, 0.0 us)
Async XLA Ops:
  102.1 4.8 copy-start.8
  561.9 89.7 %copy-start.7 = (f32[1024,1]{1,0:T(8,128)S(1)}, f32[1024,1]{1,0:T(8,128)}, u32[]{:S(2)}) copy-start(f32[1024,1]{1,0:T(8,128)} %get-tuple-element.80.inv_ref) | copy-start | bytes 12292
  561.9 90.1 %copy-start.9 = (f32[512]{0:T(512)S(1)}, f32[512]{0:T(512)}, u32[]{:S(2)}) copy-start(f32[512]{0:T(512)} %param.16) | copy-start | bytes 6148
  649.4 2.7 copy-start.3
  652.1 3.9 copy-start.4
  655.9 1.9 copy-start.6
  656.8 2.1 copy-start.5
  657.9 3.0 copy-start.2
  660.9 3.7 copy-start.1
  664.6 3.7 copy-start

commit v8 on v7

--- a/solution.py
+++ b/solution.py
@@ -718,7 +718,7 @@
             add_halves(part_ref, other_ref, share_ref)
             row_moves(parts, share_ref, line_ref, srow, rrow, 0, True)
 
-        @pl.when(head == heads // 2)
+        @pl.when(head == max(heads // 2 - 1, 0))
         def _():
             line.event(1)
 
@@ -1283,7 +1283,7 @@
     rows_n, tile, width = down_ref.shape
     tokens = second_ref.shape[0]
     tiles = hidden_ref.shape[0]
-    block = min(512, tokens)
+    block = min(256, tokens)
     mine = tiles // 2
 
     def place(t):

time: 677 us -> 680 us (level)
  no operation moved by 1% of the time
where the time goes in v8:
time: 680 us; the launch traced here: 673 us
  Pallas kernels  639 us (94%)
  local copies, waits for them, and re-layouts  18.4 us (3%)
  other arithmetic  14.8 us (2%)
    pallas_call x1, Pallas kernels, middle_call(): pl.pallas_call(functools.partial(middle_kernel, rows_n, cols_n), out_shap...  123 us
    pallas_call x1, Pallas kernels, back_call(): pl.pallas_call(functools.partial(back_kernel, rows_n, cols_n), out_shape=...  111 us
    pallas_call x1, Pallas kernels, attend_back_call(): pl.pallas_call(attend_back_kernel, out_shape=(jax.ShapeDtypeStruct((lengt...  97 us
    pallas_call x1, Pallas kernels, first_call(): pl.pallas_call(functools.partial(first_kernel, size), out_shape=(jax.Shap...  95.7 us
    pallas_call x1, Pallas kernels, last_call(): pl.pallas_call(functools.partial(last_kernel, size), out_shape=(jax.Shape...  87.4 us
    pallas_call x1, Pallas kernels, feed_call(): pl.pallas_call(feed_kernel, grid=(tiles + cols_n,), out_shape=(jax.ShapeD...  67 us
    pallas_call x1, Pallas kernels, attend_call(): pl.pallas_call(functools.partial(attend_kernel, size), out_shape=(jax.Sha...  57.5 us
    unnamed x28, local copies, waits for them, and re-layouts  13.9 us

profile of v8, /device:TPU:0, one launch (start us, length us, event | category | flops | bytes accessed | tf_op | source)
XLA Modules:
  0.0 673.5 jit_solution(7465517138155608402)
XLA Ops:
  0.7 0.7 convert_element_type.19
  1.4 0.7 convert_element_type.20
  2.0 1.3 maximum_bitcast_fusion.small_ref
  3.3 2.1 pad_maximum_fusion.qkv_ref
  5.5 95.7 %shard_map.212 = (bf16[4,1024,512]{2,1,0:T(8,128)(2,1)}, bf16[1024,2048]{1,0:T(8,128)(2,1)}, f32[1024,1]{1,0:T(8,128)}, bf16[256,2048]{1,0:T(8,128)(2,1)}, f32[4...) custom-call(bf16[1024,512]{1,0:T(8,128)(2,1)} %act_ref.3, ...), custom_call_target="tpu_custom_call" | custom-call | tf_op jit(solution)/shard_map/pallas_call | solution.py:501
  101.2 0.8 copy.30
  102.0 0.1 constant_dynamic-slice_fusion
  102.1 0.0 copy-start.8
  102.1 0.6 copy.28
  102.7 0.2 broadcast_multiply_fusion
  102.9 1.0 copy.24.segc_ref
  104.0 2.9 fusion.2
  106.9 0.0 copy-done.8
  106.9 57.5 %shard_map.213 = (bf16[8,1024,64]{2,1,0:T(8,128)(2,1)}, bf16[2,1024,64]{2,1,0:T(8,128)(2,1)}, bf16[2,1024,64]{2,1,0:T(8,128)(2,1)}, bf16[1024,512]{1,0:T(8,128)(...) custom-call(bf16[1024,2048]{1,0:T(8,128)(2,1)} %get-tuple-element.51.first_ref, ...), custom_call_target="tpu_custom_call" | custom-call | flops 44999999488 | bytes 1048576 | tf_op jit(solution)/shard_map/pallas_call | solution.py:607
  164.4 123.4 %shard_map.214 = (f32[256,2048]{1,0:T(8,128)}, bf16[4,256,2048]{2,1,0:T(8,128)(2,1)}, bf16[4,256,2048]{2,1,0:T(8,128)(2,1)}, bf16[4,512,2048]{2,1,0:T(8,128)(2,1)}, bf16[4,2048,512]{2,1,0:T(8,128)(2,1)}) custom-call(bf16[1024,512]{1,0:T(8,128)(2,1)} %get-tuple-element.55.attn_ref, bf16[4,512,512]{2,1,0:T(8,128)(2,1)} %get-tuple-element.56.weight_ref, ...), custom_call_target="tpu_custom_call" | custom-call | flops 130000003072 | bytes 1048576 | tf_op jit(solution)/shard_map/pallas_call | solution.py:935
  287.9 67.0 %shard_map.215 = (bf16[1024,2048]{1,0:T(8,128)(2,1)}, bf16[1024,2048]{1,0:T(8,128)(2,1)}, bf16[4,1024,512]{2,1,0:T(8,128)(2,1)}, bf16[4,256,2048]{2,1,0:T(8,128)(2,1)}) custom-call(bf16[1024,2048]{1,0:T(8,128)(2,1)} %bitcast.39, bf16[1024,2048]{1,0:T(8,128)(2,1)} %bitcast.41, bf16[2048,2048]{1,0:T(8,128)(2,1)} %bitcast.37, bf16[2048,2048]{1,0:T(8,128)(2,1)} %bitcast.38, ...), custom_call_target="tpu_custom_call" | custom-call | flops 49999998976 | bytes 1048576 | tf_op jit(solution)/shard_map/pallas_call | solution.py:1365
  354.9 110.9 %shard_map.216 = (bf16[4,256,2048]{2,1,0:T(8,128)(2,1)}, f32[1,2048]{1,0:T(1,128)}, f32[2048,512]{1,0:T(8,128)}, bf16[4,256,2048]{2,1,0:T(8,128)(2,1)}, bf16[4,256,2048]{2,1,0:T(8,128)(2,1)}) custom-call(bf16[1024,2048]{1,0:T(8,128)(2,1)} %get-tuple-element.65.dgate_ref, bf16[1024,2048]{1,0:T(8,128)(2,1)} %get-tuple-element.66.dup_ref, ...), custom_call_target="tpu_custom_call" | custom-call | flops 130000003072 | bytes 1048576 | tf_op jit(solution)/shard_map/pallas_call | solution.py:1101
  465.8 97.0 %shard_map.217 = (bf16[1024,768]{1,0:T(8,128)(2,1)}, f32[1024,1]{1,0:T(8,128)}, bf16[4,256,512]{2,1,0:T(8,128)(2,1)}, bf16[4,256,512]{2,1,0:T(8,128)(2,1)}, f32[512,2048]{1,0:T(8,128)}, /*index=5*/f32[512,2048]{1,0:T(8,128)}) custom-call(bf16[1024,2048]{1,0:T(8,128)(2,1)} %bitcast.23, bf16[4,512,512]{2,1,0:T(8,128)(2,1)} %get-tuple-element.56.weight_ref, ...), custom_call_target="tpu_custom_call" | custom-call | flops 80000000000 | bytes 1048576 | tf_op jit(solution)/shard_map/pallas_call | solution.py:810
  562.8 1.8 reduce
  564.7 0.0 copy-start.7
  564.7 0.0 copy-start.9
  564.7 87.4 %shard_map.218 = (f32[1024,512]{1,0:T(8,128)}, bf16[1024,512]{1,0:T(8,128)(2,1)}, f32[4,8,128]{2,1,0:T(8,128)}, f32[2,1,512]{2,1,0:T(1,128)}, f32[512,768]{1,0:T(8,128)}, /*index=5*/f32[512,512]{1,0:T(8,128)}) custom-call(bf16[1024,768]{1,0:T(8,128)(2,1)} %get-tuple-element.76.dqkv_ref, bf16[4,512,768]{2,1,0:T(8,128)(2,1)} %get-tuple-element.52.weight_ref, ...), custom_call_target="tpu_custom_call" | custom-call | flops 80000000000 | bytes 1048576 | tf_op jit(solution)/shard_map/pallas_call | solution.py:1238
  652.1 0.0 copy-start.3
  652.1 0.8 reduce_sum.9
  652.9 1.3 fusion.6
  654.2 0.2 copy.26
  654.4 0.0 copy-done.7
  654.4 0.3 fusion.4
  654.8 0.0 copy-done.9
  654.8 0.0 copy-done.3
  654.8 0.0 copy-start.4
  654.8 3.9 multiply_subtract_fusion
  658.6 0.0 copy-done.4
  658.7 0.8 fusion.5
  659.5 0.0 copy-start.5
  659.5 1.1 slice.30
  660.6 0.0 copy-start.2
  660.6 0.0 copy-done.6
  660.6 1.0 copy.36
  661.5 0.0 copy-done.5
  661.6 1.0 copy.37
  662.5 1.1 copy-done.2
  663.6 0.0 copy-start.1
  663.6 2.1 copy.38
  665.7 1.6 copy-done.1
  667.3 2.1 copy.39
  669.4 1.6 copy-done
  671.0 2.0 copy.40
  (4 shorter events, 0.0 us)
Async XLA Ops:
  102.1 4.8 copy-start.8
  564.7 89.7 %copy-start.7 = (f32[1024,1]{1,0:T(8,128)S(1)}, f32[1024,1]{1,0:T(8,128)}, u32[]{:S(2)}) copy-start(f32[1024,1]{1,0:T(8,128)} %get-tuple-element.80.inv_ref) | copy-start | bytes 12292
  564.7 90.1 %copy-start.9 = (f32[512]{0:T(512)S(1)}, f32[512]{0:T(512)}, u32[]{:S(2)}) copy-start(f32[512]{0:T(512)} %param.16) | copy-start | bytes 6148
  652.1 2.7 copy-start.3
  654.8 3.9 copy-start.4
  658.6 1.9 copy-start.6
  659.5 2.1 copy-start.5
  660.6 3.0 copy-start.2
  663.6 3.7 copy-start.1
  667.3 3.7 copy-start

commit v9 on v7

--- a/solution.py
+++ b/solution.py
@@ -1355,7 +1355,7 @@
     rows_n, hidden, width = down.shape
     cols_n = lax.axis_size("col")
     tokens, features = second.shape
-    tile = 256
+    tile = 512
     tiles = hidden // tile
     half = (rows_n, hidden // 2, width)
 

time: 677 us -> 673 us (level)
  no operation moved by 1% of the time
where the time goes in v9:
time: 673 us; the launch traced here: 667 us
  Pallas kernels  633 us (94%)
  local copies, waits for them, and re-layouts  18.4 us (3%)
  other arithmetic  14.8 us (2%)
    pallas_call x1, Pallas kernels, middle_call(): pl.pallas_call(functools.partial(middle_kernel, rows_n, cols_n), out_shap...  123 us
    pallas_call x1, Pallas kernels, back_call(): pl.pallas_call(functools.partial(back_kernel, rows_n, cols_n), out_shape=...  111 us
    pallas_call x1, Pallas kernels, attend_back_call(): pl.pallas_call(attend_back_kernel, out_shape=(jax.ShapeDtypeStruct((lengt...  96.9 us
    pallas_call x1, Pallas kernels, first_call(): pl.pallas_call(functools.partial(first_kernel, size), out_shape=(jax.Shap...  95.7 us
    pallas_call x1, Pallas kernels, last_call(): pl.pallas_call(functools.partial(last_kernel, size), out_shape=(jax.Shape...  87.4 us
    pallas_call x1, Pallas kernels, feed_call(): pl.pallas_call(feed_kernel, grid=(tiles + cols_n,), out_shape=(jax.ShapeD...  60.9 us
    pallas_call x1, Pallas kernels, attend_call(): pl.pallas_call(functools.partial(attend_kernel, size), out_shape=(jax.Sha...  57.5 us
    unnamed x28, local copies, waits for them, and re-layouts  13.9 us

profile of v9, /device:TPU:0, one launch (start us, length us, event | category | flops | bytes accessed | tf_op | source)
XLA Modules:
  0.0 667.0 jit_solution(2938426223210348401)
XLA Ops:
  0.7 0.7 convert_element_type.19
  1.4 0.7 convert_element_type.20
  2.0 1.3 maximum_bitcast_fusion.small_ref
  3.3 2.1 pad_maximum_fusion.qkv_ref
  5.5 95.7 %shard_map.212 = (bf16[4,1024,512]{2,1,0:T(8,128)(2,1)}, bf16[1024,2048]{1,0:T(8,128)(2,1)}, f32[1024,1]{1,0:T(8,128)}, bf16[256,2048]{1,0:T(8,128)(2,1)}, f32[4...) custom-call(bf16[1024,512]{1,0:T(8,128)(2,1)} %act_ref.3, ...), custom_call_target="tpu_custom_call" | custom-call | tf_op jit(solution)/shard_map/pallas_call | solution.py:501
  101.2 0.8 copy.30
  102.0 0.1 constant_dynamic-slice_fusion
  102.1 0.0 copy-start.8
  102.1 0.6 copy.28
  102.7 0.2 broadcast_multiply_fusion
  102.9 1.0 copy.24.segc_ref
  104.0 2.9 fusion.2
  106.9 0.0 copy-done.8
  106.9 57.5 %shard_map.213 = (bf16[8,1024,64]{2,1,0:T(8,128)(2,1)}, bf16[2,1024,64]{2,1,0:T(8,128)(2,1)}, bf16[2,1024,64]{2,1,0:T(8,128)(2,1)}, bf16[1024,512]{1,0:T(8,128)(...) custom-call(bf16[1024,2048]{1,0:T(8,128)(2,1)} %get-tuple-element.51.first_ref, ...), custom_call_target="tpu_custom_call" | custom-call | flops 44999999488 | bytes 1048576 | tf_op jit(solution)/shard_map/pallas_call | solution.py:607
  164.4 123.4 %shard_map.214 = (f32[256,2048]{1,0:T(8,128)}, bf16[4,256,2048]{2,1,0:T(8,128)(2,1)}, bf16[4,256,2048]{2,1,0:T(8,128)(2,1)}, bf16[4,512,2048]{2,1,0:T(8,128)(2,1)}, bf16[4,2048,512]{2,1,0:T(8,128)(2,1)}) custom-call(bf16[1024,512]{1,0:T(8,128)(2,1)} %get-tuple-element.55.attn_ref, bf16[4,512,512]{2,1,0:T(8,128)(2,1)} %get-tuple-element.56.weight_ref, ...), custom_call_target="tpu_custom_call" | custom-call | flops 130000003072 | bytes 1048576 | tf_op jit(solution)/shard_map/pallas_call | solution.py:935
  287.9 60.9 %shard_map.215 = (bf16[1024,2048]{1,0:T(8,128)(2,1)}, bf16[1024,2048]{1,0:T(8,128)(2,1)}, bf16[4,1024,512]{2,1,0:T(8,128)(2,1)}, bf16[4,256,2048]{2,1,0:T(8,128)(2,1)}) custom-call(bf16[1024,2048]{1,0:T(8,128)(2,1)} %bitcast.39, bf16[1024,2048]{1,0:T(8,128)(2,1)} %bitcast.41, bf16[2048,2048]{1,0:T(8,128)(2,1)} %bitcast.37, bf16[2048,2048]{1,0:T(8,128)(2,1)} %bitcast.38, ...), custom_call_target="tpu_custom_call" | custom-call | flops 49999998976 | bytes 1048576 | tf_op jit(solution)/shard_map/pallas_call | solution.py:1365
  348.8 110.8 %shard_map.216 = (bf16[4,256,2048]{2,1,0:T(8,128)(2,1)}, f32[1,2048]{1,0:T(1,128)}, f32[2048,512]{1,0:T(8,128)}, bf16[4,256,2048]{2,1,0:T(8,128)(2,1)}, bf16[4,256,2048]{2,1,0:T(8,128)(2,1)}) custom-call(bf16[1024,2048]{1,0:T(8,128)(2,1)} %get-tuple-element.65.dgate_ref, bf16[1024,2048]{1,0:T(8,128)(2,1)} %get-tuple-element.66.dup_ref, ...), custom_call_target="tpu_custom_call" | custom-call | flops 130000003072 | bytes 1048576 | tf_op jit(solution)/shard_map/pallas_call | solution.py:1101
  459.6 96.9 %shard_map.217 = (bf16[1024,768]{1,0:T(8,128)(2,1)}, f32[1024,1]{1,0:T(8,128)}, bf16[4,256,512]{2,1,0:T(8,128)(2,1)}, bf16[4,256,512]{2,1,0:T(8,128)(2,1)}, f32[512,2048]{1,0:T(8,128)}, /*index=5*/f32[512,2048]{1,0:T(8,128)}) custom-call(bf16[1024,2048]{1,0:T(8,128)(2,1)} %bitcast.23, bf16[4,512,512]{2,1,0:T(8,128)(2,1)} %get-tuple-element.56.weight_ref, ...), custom_call_target="tpu_custom_call" | custom-call | flops 80000000000 | bytes 1048576 | tf_op jit(solution)/shard_map/pallas_call | solution.py:810
  556.6 1.8 reduce
  558.4 0.0 copy-start.7
  558.4 0.0 copy-start.9
  558.4 87.4 %shard_map.218 = (f32[1024,512]{1,0:T(8,128)}, bf16[1024,512]{1,0:T(8,128)(2,1)}, f32[4,8,128]{2,1,0:T(8,128)}, f32[2,1,512]{2,1,0:T(1,128)}, f32[512,768]{1,0:T(8,128)}, /*index=5*/f32[512,512]{1,0:T(8,128)}) custom-call(bf16[1024,768]{1,0:T(8,128)(2,1)} %get-tuple-element.76.dqkv_ref, bf16[4,512,768]{2,1,0:T(8,128)(2,1)} %get-tuple-element.52.weight_ref, ...), custom_call_target="tpu_custom_call" | custom-call | flops 80000000000 | bytes 1048576 | tf_op jit(solution)/shard_map/pallas_call | solution.py:1238
  645.8 0.0 copy-start.3
  645.9 0.8 reduce_sum.9
  646.7 1.3 fusion.6
  647.9 0.2 copy.26
  648.2 0.0 copy-done.7
  648.2 0.3 fusion.4
  648.5 0.0 copy-done.9
  648.5 0.0 copy-done.3
  648.5 0.0 copy-start.4
  648.6 3.9 multiply_subtract_fusion
  652.4 0.0 copy-done.4
  652.4 0.0 copy-start.6
  652.4 0.8 fusion.5
  653.2 0.0 copy-start.5
  653.2 1.1 slice.30
  654.3 0.0 copy-start.2
  654.3 0.0 copy-done.6
  654.3 1.0 copy.36
  655.3 0.0 copy-done.5
  655.3 1.0 copy.37
  656.3 1.1 copy-done.2
  657.4 2.1 copy.38
  659.5 1.6 copy-done.1
  661.1 2.1 copy.39
  663.2 1.6 copy-done
  664.8 2.0 copy.40
  (4 shorter events, 0.0 us)
Async XLA Ops:
  102.1 4.8 copy-start.8
  558.4 89.8 %copy-start.7 = (f32[1024,1]{1,0:T(8,128)S(1)}, f32[1024,1]{1,0:T(8,128)}, u32[]{:S(2)}) copy-start(f32[1024,1]{1,0:T(8,128)} %get-tuple-element.80.inv_ref) | copy-start | bytes 12292
  558.4 90.1 %copy-start.9 = (f32[512]{0:T(512)S(1)}, f32[512]{0:T(512)}, u32[]{:S(2)}) copy-start(f32[512]{0:T(512)} %param.16) | copy-start | bytes 6148
  645.8 2.7 copy-start.3
  648.5 3.9 copy-start.4
  652.4 1.9 copy-start.6
  653.2 2.1 copy-start.5
  654.3 3.0 copy-start.2
  657.4 3.7 copy-start.1
  661.1 3.7 copy-start
